TPU v7x, 32 devices: a whole 2x2x4 slice. The times are simulated.
32 devices in a mesh: gx: 4 (over y, x), gy: 8 (over z, core).
Axes of the slice: x: 2, y: 2, z: 4, core: 2. Of those that a mesh axis runs over, the one named last changes fastest.
Arguments:
- inputs: bfloat16 [32, 32, 8, 128], P('gx', 'gy'), may hold values from -6 to 6
- preact: bfloat16 [32, 32, 8, 128], P('gx', 'gy'), may hold values from -6 to 6
- cotangent: bfloat16 [32, 32, 8, 128], P('gx', 'gy'), may hold values from -6 to 6
- spectral_w: bfloat16 [32, 32, 8, 128, 128], P('gx', 'gy'), may hold values from -2 to 2
- skip_w: bfloat16 [128, 128], replicated, may hold values from -0.5 to 0.5
Outputs:
- grad_inputs: bfloat16 [32, 32, 8, 128], P('gx', 'gy')
- grad_spectral: bfloat16 [32, 32, 8, 128, 128], P('gx', 'gy')
- grad_skip: float32 [128, 128], replicated
All inputs are finite; a program needn't handle non-finite values.
Results may differ from a plain program's by a relative error of at most 0.0054.
Values may be sent and summed in bfloat16 or wider, within the bound.
No kernel may reach another device: no remote copies, remote signals or barrier semaphores. Data moves between devices by JAX's collectives and lax.ppermute only.
A program may use at most 64 MiB of HBM per device.

v0:
```python
import math

import jax
import jax.numpy as jnp
from jax import lax
from jax.sharding import PartitionSpec as P

highest = lax.Precision.HIGHEST


def cas_table(modes, length, offset, cells):
    index = jnp.arange(modes, dtype=jnp.int32)
    freq = jnp.where(index < modes // 2, index, length - modes + index)
    where_cells = offset + jnp.arange(cells, dtype=jnp.int32)
    phase = freq[:, None] * where_cells[None, :] % length
    angle = phase.astype(jnp.float32) * (2.0 * math.pi / length)
    return (jnp.cos(angle) + jnp.sin(angle)) / math.sqrt(length)


def on_device(inputs, preact, cotangent, spectral_w, skip_w):
    cells_x, cells_y, cells_z, channels = inputs.shape
    length_x = cells_x * lax.axis_size("gx")
    length_y = cells_y * lax.axis_size("gy")
    local_modes_x, local_modes_y, modes_z = (
        spectral_w.shape[0],
        spectral_w.shape[1],
        spectral_w.shape[2],
    )
    modes_x = local_modes_x * lax.axis_size("gx")
    modes_y = local_modes_y * lax.axis_size("gy")
    table_z = cas_table(modes_z, cells_z, 0, cells_z)
    table_x = cas_table(modes_x, length_x, lax.axis_index("gx") * cells_x, cells_x)
    table_y = cas_table(modes_y, length_y, lax.axis_index("gy") * cells_y, cells_y)
    preact_wide = preact.astype(jnp.float32)
    gelu_slope = 0.5 * (
        1.0 + jax.scipy.special.erf(preact_wide * (1.0 / math.sqrt(2.0)))
    ) + preact_wide * jnp.exp(-0.5 * preact_wide * preact_wide) * (1.0 / math.sqrt(2.0 * math.pi))
    grad_pre = (cotangent.astype(jnp.float32) * gelu_slope).astype(jnp.bfloat16)
    fields = jnp.stack([inputs, grad_pre]).astype(jnp.float32)
    z_modes = jnp.einsum("ck,fijkh->fijch", table_z, fields, precision=highest)
    table_rows = table_y
    part_y = lax.psum_scatter(
        jnp.einsum("bj,fijch->bfich", table_rows, z_modes, precision=highest),
        "gy",
        scatter_dimension=0,
        tiled=True,
    )
    table_rows = table_x
    owned_modes = lax.psum_scatter(
        jnp.einsum("ai,bfich->abfch", table_rows, part_y, precision=highest),
        "gx",
        scatter_dimension=0,
        tiled=True,
    )
    input_modes = owned_modes[:, :, 0]
    grad_modes = owned_modes[:, :, 1]
    grad_spectral = jnp.einsum(
        "abcp,abcq->abcpq", input_modes, grad_modes, precision=highest
    ).astype(jnp.bfloat16)
    back_modes = jnp.einsum(
        "abcq,abcpq->abcp", grad_modes, spectral_w.astype(jnp.float32), precision=highest
    ).astype(jnp.bfloat16)
    table_rows = table_x
    over_first = jnp.einsum(
        "ai,abch->ibch",
        table_rows,
        lax.all_gather(back_modes, "gx", axis=0, tiled=True).astype(jnp.float32),
        precision=highest,
    )
    table_rows = table_y
    cell_modes = jnp.einsum(
        "bj,ibch->ijch",
        table_rows,
        lax.all_gather(over_first, "gy", axis=1, tiled=True),
        precision=highest,
    )
    spectral_cells = jnp.einsum("ck,ijch->ijkh", table_z, cell_modes, precision=highest)
    flat_grad = grad_pre.reshape(-1, channels)
    skip_part = lax.dot_general(
        flat_grad, skip_w, (((1,), (1,)), ((), ())), preferred_element_type=jnp.float32
    )
    grad_inputs = (skip_part.reshape(cells_x, cells_y, cells_z, channels) + spectral_cells).astype(
        jnp.bfloat16
    )
    local_sum = lax.dot_general(
        inputs.reshape(-1, channels),
        flat_grad,
        (((0,), (0,)), ((), ())),
        preferred_element_type=jnp.float32,
    )
    grad_skip = lax.psum(local_sum, ("gx", "gy")) / math.sqrt(length_x * length_y * cells_z)
    return (grad_inputs, grad_spectral, grad_skip)


def solution(mesh):
    in_specs = (
        P("gx", "gy", None, None),
        P("gx", "gy", None, None),
        P("gx", "gy", None, None),
        P("gx", "gy", None, None, None),
        P(),
    )
    out_specs = (P("gx", "gy", None, None), P("gx", "gy", None, None, None), P())
    return jax.shard_map(
        on_device, mesh=mesh, in_specs=in_specs, out_specs=out_specs, check_vma=False
    )
```

profile of v0, /device:TPU:0, one launch (start us, length us, event | category | flops | bytes accessed | tf_op | source)
XLA Modules:
  0.0 201.0 jit_solution(10419160019453791646)
XLA Ops:
  8.0 0.0 reduce-scatter.3.cloned.1.call-start
  8.1 0.9 fusion.22
  9.0 1.2 convolution_bitcast_fusion
  10.3 2.0 fusion.7
  12.2 2.5 %copy.25 = f32[32,2,8,8,128]{4,3,2,1,0:T(8,128)} copy(f32[32,2,8,8,128]{4,0,3,2,1:T(8,128)S(1)} %fusion.7) | data formatting | bytes 4194304 | tf_op jit(solution)/shard_map/bj,fijch->bfich/dot_general | solution.py:43
  14.8 0.0 reduce-scatter.5.cloned.1.call-start
  14.9 38.6 %reduce-scatter.3.cloned.1.call-done = f32[4,2,8,8,128]{4,3,2,1,0:T(8,128)} async-done(((f32[32,2,8,8,128]{4,3,2,1,0:T(8,128)}), f32[4,2,8,8,128]{4,3,2,1,0:T(8,128)}) %reduce-scatter.3.cloned.1.call-update) | async-done | bytes 262160 | tf_op jit(solution)/shard_map/reduce_scatter | solution.py:42
  53.4 3.1 %fusion.5 = f32[32,4,2,8,128]{4,0,3,2,1:T(8,128)} fusion(f32[4,2,8,8,128]{4,3,2,1,0:T(8,128)} %reduce-scatter.3.cloned.1.call-done, s32[8]{0:T(128)S(1)} %iota_add_fusion.1), kind=kOutput, calls=%fused_computation.10 | convolution fusion | flops 25169920 | bytes 1310752 | tf_op jit(solution)/shard_map/ai,bfich->abfch/dot_general | solution.py:50
  56.5 0.0 all-reduce.2.cloned.1.call-start
  56.6 0.8 convolution_bitcast_fusion.3
  57.4 0.0 all-gather.2.cloned.1.call-start
  57.5 25.7 %reduce-scatter.5.cloned.1.call-done = f32[8,4,2,8,128]{4,0,3,2,1:T(8,128)} async-done(((f32[32,4,2,8,128]{4,0,3,2,1:T(8,128)}), f32[8,4,2,8,128]{4,0,3,2,1:T(8,128)}) %reduce-scatter.5.cloned.1.call-update) | async-done | bytes 262160 | tf_op jit(solution)/shard_map/reduce_scatter | solution.py:49
  83.2 1.0 slice_bitcast_fusion
  84.2 15.4 %fusion.19 = f32[8,4,8,1,128]{4,3,2,1,0:T(1,128)S(1)} fusion(bf16[8,4,8,128,128]{4,3,2,1,0:T(8,128)(2,1)} %param.8, f32[8,4,8,128,1]{3,0,2,1,4:T(8,128)S(1)} %get-tuple-element.16), kind=kOutput, calls=%fused_computation.29 | convolution fusion | flops 50331648 | bytes 8650752 | tf_op jit(solution)/shard_map/abcq,abcpq->abcp/dot_general | solution.py:60
  99.6 8.9 %all_gather.6 = bf16[32,4,8,128]{3,2,1,0:T(8,128)(2,1)S(1)} all-gather(bf16[8,4,8,128]{3,2,1,0:T(8,128)(2,1)S(1)} %convert_element_type.38), channel_id=1, replica_groups=mesh['gx'=4,'gy'=8] {'gx'}, dimensions={0}, use_global_device_ids=true | all-gather | bytes 327680 | tf_op jit(solution)/shard_map/all_gather | solution.py:67
  108.5 0.3 fusion.3
  108.9 0.7 copy.28
  109.6 0.2 fusion.23
  109.7 72.1 %all-reduce.2.cloned.1.call-done = f32[128,128]{0,1:T(8,128)} async-done(((f32[128,128]{0,1:T(8,128)}), f32[128,128]{0,1:T(8,128)}) %all-reduce.2.cloned.1.call-update) | async-done | bytes 65552 | tf_op jit(solution)/shard_map/psum | solution.py:91
  181.9 0.8 broadcast_multiply_fusion
  182.7 0.7 copy.33
  183.5 7.0 %multiply_convert_fusion = bf16[8,4,8,128,128]{4,3,2,1,0:T(8,128)(2,1)} fusion(f32[8,4,8,128]{3,2,1,0:T(8,128)S(1)} %copy.32, f32[8,4,8,128]{3,2,1,0:T(8,128)S(1)} %copy.31), kind=kLoop, calls=%fused_computation | loop fusion | flops 8388608 | bytes 8650752 | tf_op jit(solution)/shard_map/convert_element_type | solution.py:59
  190.5 2.5 %convolution_bitcast_fusion.2 = f32[8,4,8,128]{3,1,2,0:T(4,128)S(1)} fusion(f32[8,32,8,128]{3,2,0,1:T(8,128)} %all-gather.2.cloned.1.call-done, s32[4]{0:T(128)S(1)} %iota_add_fusion), kind=kOutput, calls=%fused_computation.4 | convolution fusion | flops 12584960 | bytes 1179664 | tf_op jit(solution)/shard_map/bj,ibch->ijch/dot_general | solution.py:71
  192.9 0.9 fusion.1
  (14 shorter events, 0.2 us)
Async XLA Ops:
  8.0 101.6 %copy-start = (bf16[128,128]{1,0:T(8,128)(2,1)S(1)}, bf16[128,128]{1,0:T(8,128)(2,1)}, u32[]{:S(2)}) copy-start(bf16[128,128]{1,0:T(8,128)(2,1)} %param.9) | copy-start | bytes 98308
  8.0 48.5 %copy-start.1 = (bf16[8,4,8,128]{3,2,1,0:T(8,128)(2,1)S(1)}, bf16[8,4,8,128]{3,2,1,0:T(8,128)(2,1)}, u32[]{:S(2)}) copy-start(bf16[8,4,8,128]{3,2,1,0:T(8,128)(2,1)} %param.5) | copy-start | bytes 196612
  8.0 45.4 %reduce-scatter.3.cloned.1.call-start = ((), (), s32[]{:S(2)}) async-start(), calls=%async_computation.2 | async-start | bytes 2359296 | tf_op jit(solution)/shard_map/reduce_scatter | solution.py:42
  14.8 68.4 %reduce-scatter.5.cloned.1.call-start = ((), (), s32[]{:S(2)}) async-start(), calls=%async_computation.3 | async-start | bytes 1310720 | tf_op jit(solution)/shard_map/reduce_scatter | solution.py:49
  56.5 125.4 %all-reduce.2.cloned.1.call-start = ((), (), s32[]{:S(2)}) async-start(), calls=%async_computation.5 | async-start | bytes 131072 | tf_op jit(solution)/shard_map/psum | solution.py:91
  57.4 133.0 %all-gather.2.cloned.1.call-start = ((), (), s32[]{:S(2)}) async-start(), calls=%async_computation.4 | async-start | bytes 1179648 | tf_op jit(solution)/shard_map/all_gather | solution.py:74
Sparse Core Ops, SparseCore 0:
  14.9 38.4 reduce-scatter.2
  56.9 26.2 reduce-scatter.4
  109.7 22.1 all-gather.1
Sparse Core Ops, SparseCore 1:
  64.1 117.7 all-reduce.1
where the time goes:
time: 203 us; the launch traced here: 201 us
  waiting for transfers between devices  136 us (67%)
  matrix products  26.4 us (13%)
  between operations  15.3 us (8%)
  blocking collectives  8.9 us (4%)
  other arithmetic  8.79 us (4%)
  local copies, waits for them, and re-layouts  5.01 us (2%)
    psum x1, waiting for transfers between devices, on_device(): lax.psum(local_sum, ('gx', 'gy')) / math.sqrt(length_x * length_y * cells_z)  72.1 us
    reduce_scatter x1, waiting for transfers between devices, on_device(): lax.psum_scatter(jnp.einsum('bj,fijch->bfich', table_rows, z_modes, preci...  38.6 us
    reduce_scatter x1, waiting for transfers between devices, on_device(): lax.psum_scatter(jnp.einsum('ai,bfich->abfch', table_rows, part_y, precis...  25.7 us
    dot_general x1, matrix products, on_device(): jnp.einsum('abcq,abcpq->abcp', grad_modes, spectral_w.astype(jnp.float32)...  15.4 us
    all_gather x1, blocking collectives, on_device(): lax.all_gather(back_modes, 'gx', axis=0, tiled=True).astype(jnp.float32)  8.9 us
    convert_element_type x1, other arithmetic, on_device(): grad_spectral = jnp.einsum('abcp,abcq->abcpq', input_modes, grad_modes, p...  6.96 us
  transfers between devices with their start and end apart: 4, of which 3 were waited for; matrix products, arithmetic and copies ran while one was open for 13% of the time, Pallas kernels for 0%

commit v1 on v0

--- a/solution.py
+++ b/solution.py
@@ -1,11 +1,19 @@
+import functools
 import math
 
 import jax
 import jax.numpy as jnp
+import numpy as np
 from jax import lax
+from jax.experimental import pallas as pl
+from jax.experimental.pallas import tpu as pltpu
 from jax.sharding import PartitionSpec as P
 
 highest = lax.Precision.HIGHEST
+f32 = jnp.float32
+bf16 = jnp.bfloat16
+LANES = 128
+MIB = 1 << 20
 
 
 def cas_table(modes, length, offset, cells):
@@ -17,7 +25,382 @@
     return (jnp.cos(angle) + jnp.sin(angle)) / math.sqrt(length)
 
 
+def gelu_slope_of(preact_wide):
+    return 0.5 * (
+        1.0 + lax.erf(preact_wide * (1.0 / math.sqrt(2.0)))
+    ) + preact_wide * jnp.exp(-0.5 * preact_wide * preact_wide) * (1.0 / math.sqrt(2.0 * math.pi))
+
+
+def plain_cas(modes, length):
+    index = np.arange(modes)
+    freq = np.where(index < modes // 2, index, length - modes + index)
+    angle = 2.0 * np.pi * ((freq[:, None] * np.arange(length)[None, :]) % length) / length
+    return np.cos(angle) + np.sin(angle)
+
+
+def rounded_table(table):
+    values, counts = np.unique(np.round(np.abs(table), 12), return_counts=True)
+    best = None
+    for scale in np.linspace(1.0, 2.0, 512, endpoint=False):
+        kept = (values * scale).astype(np.float32).astype(bf16).astype(np.float64) / scale
+        error = np.sum(counts * (kept - values) ** 2)
+        if best is None or error < best[0]:
+            best = (error, scale)
+    return (table * best[1]).astype(np.float32).astype(bf16), 1.0 / best[1]
+
+
+def split_index(size, *parts):
+    return np.unravel_index(np.arange(size), parts)
+
+
+class Sizes:
+    def __init__(self, inputs, spectral_w, gx, gy):
+        self.gx, self.gy = gx, gy
+        self.devices = gx * gy
+        self.x, self.y, self.z, self.channels = inputs.shape
+        self.cells = self.x * self.y * self.z
+        self.width = 2 * self.z * self.channels // self.devices
+        self.back_width = self.z * self.channels // self.devices
+
+    def fits(self, inputs, spectral_w):
+        if inputs.shape[:3] != spectral_w.shape[:3] or self.channels != LANES:
+            return False
+        if self.back_width * 4 != LANES or self.y % 4:
+            return False
+        rows = self.x * self.y // 2
+        return rows == 16 and self.devices * 4 == LANES and self.x * self.y // 4 == 8 and self.z == 8
+
+
+def lanes_of(shape):
+    return lax.broadcasted_iota(jnp.int32, shape, len(shape) - 1)
+
+
+def open_kernel(in_ref, pre_ref, cot_ref, perm_ref, pack_ref, grad_ref):
+    grad = (cot_ref[...].astype(f32) * gelu_slope_of(pre_ref[...].astype(f32))).astype(bf16)
+    grad_ref[...] = grad
+    half = in_ref.shape[0] // 2
+    width = LANES // 2
+    for field, value in enumerate((in_ref[...], grad)):
+        rows = jnp.dot(perm_ref[...], value, preferred_element_type=f32)
+        even, odd = rows[:half], rows[half:]
+        low = lanes_of(even.shape) < width
+        pack_ref[field, 0] = jnp.where(low, even, pltpu.roll(odd, width, 1)).astype(bf16)
+        pack_ref[field, 1] = jnp.where(low, pltpu.roll(even, width, 1), odd).astype(bf16)
+
+
+def skip_kernel(in_ref, grad_ref, skip_ref, perm_ref, part_ref, sum_ref):
+    grad = grad_ref[...]
+    part_ref[...] = lax.dot_general(
+        grad, skip_ref[...], (((1,), (1,)), ((), ())), preferred_element_type=f32
+    )
+    total = lax.dot_general(
+        in_ref[...], grad, (((0,), (0,)), ((), ())), preferred_element_type=f32
+    )
+    high = total.astype(bf16)
+    low = (total - high.astype(f32)).astype(bf16)
+    sum_ref[...] = jnp.dot(
+        perm_ref[...], jnp.concatenate([high, low], 0), preferred_element_type=f32
+    )
+
+
+def plane_kernel(scale, x_ref, table_ref, out_ref):
+    rows, width = x_ref.shape[0], LANES // 2
+    made = jnp.dot(table_ref[...], x_ref[...], preferred_element_type=f32)
+    low = lanes_of((rows, LANES)) < width
+    straight = jnp.where(low, made[:rows], made[rows : 2 * rows])
+    crossed = jnp.where(low, made[2 * rows : 3 * rows], made[3 * rows :])
+    out_ref[...] = ((straight + pltpu.roll(crossed, width, 1)) * scale).astype(bf16)
+
+
+def modes_kernel(
+    scale, per_step, x_ref, z_ref, w_ref, perm_ref, sum_ref, in_ref, grad_ref, pack_ref, twin, back
+):
+    step = pl.program_id(0)
+    groups = per_step // 8
+
+    @pl.when(step == 0)
+    def _():
+        width = LANES // 2
+        made = []
+        for field in range(2):
+            first = x_ref[field, 0].astype(f32)
+            second = x_ref[field, 1].astype(f32)
+            low = lanes_of(first.shape) < width
+            even = jnp.where(low, first, pltpu.roll(second, width, 1))
+            odd = jnp.where(low, pltpu.roll(first, width, 1), second)
+            rows = jnp.concatenate([even, odd], 0).astype(bf16)
+            made.append(jnp.dot(z_ref[...], rows, preferred_element_type=f32) * scale)
+        in_ref[...] = made[0].T
+        grad_ref[...] = made[1]
+        high = made[1].astype(bf16).astype(f32)
+        low_part = made[1] - high
+        count = made[1].shape[0] // 8
+        twin[...] = jnp.concatenate(
+            [high.reshape(count, 8, LANES), low_part.reshape(count, 8, LANES)], 1
+        ).astype(bf16)
+
+    row = lax.broadcasted_iota(jnp.int32, (8, LANES), 0)
+    for group in range(groups):
+        weights = w_ref[group * 8 : group * 8 + 8].reshape(8 * LANES, LANES)
+        every = lax.dot_general(
+            twin[step * groups + group],
+            weights,
+            (((1,), (1,)), ((), ())),
+            preferred_element_type=f32,
+        )
+        every = every[:8] + every[8:]
+        total = jnp.zeros((8, LANES), f32)
+        for mode in range(8):
+            total += jnp.where(row == mode, every[:, mode * LANES : (mode + 1) * LANES], 0.0)
+        back[pl.ds(pl.multiple_of((step * groups + group) * 8, 8), 8), :] = total
+
+    @pl.when(step == pl.num_programs(0) - 1)
+    def _():
+        rows = jnp.dot(perm_ref[...], back[...].astype(bf16), preferred_element_type=f32)
+        quarter = rows.shape[0] // 4
+        group_of = lanes_of((quarter, LANES)) // (LANES // 4)
+        pieces = []
+        for part in range(4):
+            piece = jnp.zeros((quarter, LANES), f32)
+            for place in range(4):
+                source = rows[place * quarter : (place + 1) * quarter]
+                moved = pltpu.roll(source, (place - part) % 4 * (LANES // 4), 1)
+                piece = jnp.where(group_of == place, moved, piece)
+            pieces.append(piece)
+        every = jnp.concatenate(pieces, 0)
+        count = every.shape[0] // 8
+        pack_ref[...] = jnp.concatenate(
+            [every.reshape(count, 8, LANES), sum_ref[...].reshape(count, 8, LANES)], 1
+        ).astype(bf16)
+
+
+def outer_kernel(per_step, in_ref, grad_ref, out_ref):
+    step = pl.program_id(0)
+    columns = pltpu.roll(in_ref[...], in_ref.shape[1] - step * per_step, 1)
+    for mode in range(per_step):
+        column = jnp.broadcast_to(columns[:, mode : mode + 1], (LANES, LANES))
+        out_ref[mode] = (column * grad_ref[mode : mode + 1, :]).astype(bf16)
+
+
+def back_plane_kernel(scale, skip_scale, x_ref, table_ref, out_ref):
+    every = x_ref[...].astype(f32)
+    count = every.shape[0]
+    rows = count * 8
+    x = every[:, :8].reshape(rows, LANES)
+    turned = [x if s == 0 else pltpu.roll(x, s * (LANES // 4), 1) for s in range(4)]
+    made = jnp.dot(
+        table_ref[...], jnp.concatenate(turned, 0).astype(bf16), preferred_element_type=f32
+    )
+    group_of = lanes_of((rows, LANES)) // (LANES // 4)
+    out = made[:rows]
+    for place in range(1, 4):
+        out = jnp.where(group_of == place, made[place * rows : (place + 1) * rows], out)
+    out = out * scale
+    parts = jnp.sum(every[:, 8:], 0)
+    total = (parts + pltpu.roll(parts, 4, 0)) * skip_scale
+    high = total.astype(bf16).astype(f32)
+    row = lax.broadcasted_iota(jnp.int32, total.shape, 0)
+    total = jnp.where(row < 4, high, total - high)
+    out_ref[...] = jnp.concatenate(
+        [out.reshape(count, 8, LANES), jnp.broadcast_to(total[None], (count, 8, LANES))], 1
+    ).astype(bf16)
+
+
+def close_kernel(scale, x_ref, z_ref, part_ref, fold_ref, out_ref, skip_ref):
+    every = x_ref[...].astype(f32)
+    count = every.shape[0]
+    rows = every[:, :8].reshape(count * 8, LANES)
+    quarter = rows.shape[0] // 4
+    group_of = lanes_of((quarter, LANES)) // (LANES // 4)
+    pieces = []
+    for place in range(4):
+        piece = jnp.zeros((quarter, LANES), f32)
+        for part in range(4):
+            source = rows[part * quarter : (part + 1) * quarter]
+            moved = pltpu.roll(source, (part - place) % 4 * (LANES // 4), 1)
+            piece = jnp.where(group_of == part, moved, piece)
+        pieces.append(piece)
+    cells = jnp.dot(
+        z_ref[...], jnp.concatenate(pieces, 0).astype(bf16), preferred_element_type=f32
+    )
+    out_ref[...] = (part_ref[...] + cells * scale).astype(bf16)
+    sums = every[:, 8:].reshape(count * 8, LANES).astype(bf16)
+    skip_ref[...] = jnp.dot(fold_ref[...], sums, preferred_element_type=f32)
+
+
+def one_hot(rows, columns):
+    return (np.asarray(rows)[:, None] == np.asarray(columns)[None, :]).astype(np.float32)
+
+
+def make_tables(s):
+    cas_x = plain_cas(s.x * s.gx, s.x * s.gx)
+    cas_y = plain_cas(s.y * s.gy, s.y * s.gy)
+    cas_z = plain_cas(s.z, s.z)
+    norm = math.sqrt(s.x * s.gx * s.y * s.gy)
+    t = {}
+    yl, z, x, yh = split_index(s.cells, 2, s.z, s.x, s.y // 2)
+    t["cut"] = one_hot((x * s.y + yh * 2 + yl) * s.z + z, np.arange(s.cells))
+    device, which, row = split_index(2 * s.channels, s.devices, 2, 4)
+    t["sums"] = one_hot(which * s.channels + device * 4 + row, np.arange(2 * s.channels))
+    device, which, row = split_index(2 * s.channels, s.devices, 2, 4)
+    t["fold"] = one_hot(np.arange(s.channels), device * 4 + row)
+    count = s.devices * s.x * s.y // 2
+    px, py, x, yh = split_index(count, s.gx, s.gy, s.x, s.y // 2)
+    at_x = px * s.x + x
+    blocks = []
+    for b, y in ((0, 0), (1, 1), (1, 0), (0, 1)):
+        at_b = py * s.y + yh * 2 + b
+        at_y = py * s.y + yh * 2 + y
+        blocks.append(cas_x[at_x[:, None], at_x[None, :]] * cas_y[at_b[:, None], at_y[None, :]])
+    t["plane"], factor = rounded_table(np.concatenate(blocks, 0))
+    t["plane_scale"] = factor / norm
+    a, b, c = split_index(s.cells, s.x, s.y, s.z)
+    bl, z, al, bh = split_index(s.cells, 2, s.z, s.x, s.y // 2)
+    same = one_hot(a * s.y + b, al * s.y + bh * 2 + bl)
+    t["z"] = same * cas_z[c[:, None], z[None, :]]
+    t["z_scale"] = 1.0 / math.sqrt(s.z)
+    b, c, a = split_index(s.cells, s.y, s.z, s.x)
+    t["back_cut"] = one_hot((a * s.y + b) * s.z + c, np.arange(s.cells))
+    count = s.devices * s.x
+    px, py, x = split_index(count, s.gx, s.gy, s.x)
+    at_x = px * s.x + x
+    blocks = []
+    for place in range(4):
+        line = []
+        for turn in range(4):
+            at_y = py * s.y + place
+            at_b = py * s.y + (place - turn) % 4
+            line.append(cas_x[at_x[None, :], at_x[:, None]] * cas_y[at_b[None, :], at_y[:, None]])
+        blocks.append(np.concatenate(line, 1))
+    t["back_plane"], factor = rounded_table(np.concatenate(blocks, 0))
+    t["back_plane_scale"] = factor / norm
+    x, y, z = split_index(s.cells, s.x, s.y, s.z)
+    yl, c, xl = split_index(s.cells, s.y, s.z, s.x)
+    t["back_z"] = one_hot(x * s.y + y, xl * s.y + yl) * cas_z[c[None, :], z[:, None]]
+    return {
+        key: jnp.asarray(np.asarray(value, np.float32).astype(bf16))
+        if isinstance(value, np.ndarray)
+        else value
+        for key, value in t.items()
+    }
+
+
+def call(kernel, out_shape, limit, cost, **more):
+    return pl.pallas_call(
+        kernel,
+        out_shape=out_shape,
+        compiler_params=pltpu.CompilerParams(vmem_limit_bytes=limit * MIB),
+        cost_estimate=pl.CostEstimate(flops=cost[0], bytes_accessed=cost[1], transcendentals=0),
+        **more,
+    )
+
+
+def shaped(*shape, kind=bf16):
+    return jax.ShapeDtypeStruct(shape, kind)
+
+
+def exchange(pieces):
+    return lax.all_to_all(pieces, ("gx", "gy"), 0, 0)
+
+
+def on_device_whole_planes(s, inputs, preact, cotangent, spectral_w, skip_w):
+    t = make_tables(s)
+    cells, channels, devices = s.cells, s.channels, s.devices
+    flat = lambda array: array.reshape(cells, channels)
+    pieces, grad_pre = call(
+        open_kernel,
+        (shaped(2, 2, cells // 2, LANES), shaped(cells, channels)),
+        16,
+        (cells * cells * LANES * 4, 1 * MIB),
+    )(flat(inputs), flat(preact), flat(cotangent), t["cut"])
+    columns = exchange(pieces.reshape(devices, -1, LANES))
+    skip_part, sums = call(
+        skip_kernel,
+        (shaped(cells, channels, kind=f32), shaped(2 * channels, channels, kind=f32)),
+        16,
+        (cells * channels * channels * 8, 4 * MIB),
+    )(flat(inputs), grad_pre, skip_w, t["sums"])
+    rows = cells // s.z // 2 * devices
+    planes = call(
+        functools.partial(plane_kernel, t["plane_scale"]),
+        shaped(rows, LANES),
+        16,
+        (rows * rows * LANES * 8, 4 * MIB),
+    )(columns.reshape(rows, LANES), t["plane"])
+    owned = exchange(planes.reshape(devices, -1, LANES))
+
+    per_step = 16
+    whole = lambda *shape: pl.BlockSpec(shape, lambda i: (0,) * len(shape))
+    input_modes, grad_modes, back = call(
+        functools.partial(modes_kernel, t["z_scale"], per_step),
+        (
+            shaped(channels, cells, kind=f32),
+            shaped(cells, channels, kind=f32),
+            shaped(devices, 16, LANES),
+        ),
+        24,
+        (cells * channels * channels * 16, 9 * MIB),
+        grid=(cells // per_step,),
+        in_specs=[
+            whole(2, 2, cells // 2, LANES),
+            whole(cells, cells),
+            pl.BlockSpec((per_step, channels, channels), lambda i: (i, 0, 0)),
+            whole(cells, cells),
+            whole(2 * channels, channels),
+        ],
+        out_specs=(whole(channels, cells), whole(cells, channels), whole(devices, 16, LANES)),
+        scratch_shapes=[
+            pltpu.VMEM((cells // 8, 16, LANES), bf16),
+            pltpu.VMEM((cells, channels), f32),
+        ],
+    )(
+        owned.reshape(2, 2, cells // 2, LANES),
+        t["z"],
+        spectral_w.reshape(cells, channels, channels),
+        t["back_cut"],
+        sums,
+    )
+    back_columns = exchange(back)
+    grad_spectral = call(
+        functools.partial(outer_kernel, per_step),
+        shaped(cells, channels, channels),
+        16,
+        (cells * channels * channels * 2, 9 * MIB),
+        grid=(cells // per_step,),
+        in_specs=[whole(channels, cells), pl.BlockSpec((per_step, channels), lambda i: (i, 0))],
+        out_specs=pl.BlockSpec((per_step, channels, channels), lambda i: (i, 0, 0)),
+    )(input_modes, grad_modes)
+    total_cells = cells * devices
+    back_planes = call(
+        functools.partial(
+            back_plane_kernel, t["back_plane_scale"], 1.0 / math.sqrt(total_cells)
+        ),
+        shaped(devices, 16, LANES),
+        16,
+        (rows * rows * LANES * 8, 4 * MIB),
+    )(back_columns, t["back_plane"])
+    spectral = exchange(back_planes)
+    grad_inputs, grad_skip = call(
+        functools.partial(close_kernel, t["z_scale"]),
+        (shaped(cells, channels), shaped(channels, channels, kind=f32)),
+        16,
+        (cells * cells * LANES * 4, 1 * MIB),
+    )(spectral, t["back_z"], skip_part, t["fold"])
+    return (
+        grad_inputs.reshape(inputs.shape),
+        grad_spectral.reshape(spectral_w.shape),
+        grad_skip,
+    )
+
+
 def on_device(inputs, preact, cotangent, spectral_w, skip_w):
+    sizes = Sizes(inputs, spectral_w, lax.axis_size("gx"), lax.axis_size("gy"))
+    if sizes.fits(inputs, spectral_w):
+        return on_device_whole_planes(sizes, inputs, preact, cotangent, spectral_w, skip_w)
+    return on_device_any(inputs, preact, cotangent, spectral_w, skip_w)
+
+
+def on_device_any(inputs, preact, cotangent, spectral_w, skip_w):
     cells_x, cells_y, cells_z, channels = inputs.shape
     length_x = cells_x * lax.axis_size("gx")
     length_y = cells_y * lax.axis_size("gy")
@@ -33,7 +416,7 @@
     table_y = cas_table(modes_y, length_y, lax.axis_index("gy") * cells_y, cells_y)
     preact_wide = preact.astype(jnp.float32)
     gelu_slope = 0.5 * (
-        1.0 + jax.scipy.special.erf(preact_wide * (1.0 / math.sqrt(2.0)))
+        1.0 + lax.erf(preact_wide * (1.0 / math.sqrt(2.0)))
     ) + preact_wide * jnp.exp(-0.5 * preact_wide * preact_wide) * (1.0 / math.sqrt(2.0 * math.pi))
     grad_pre = (cotangent.astype(jnp.float32) * gelu_slope).astype(jnp.bfloat16)
     fields = jnp.stack([inputs, grad_pre]).astype(jnp.float32)

time: 203 us -> 69.4 us (0.34)
  waiting for transfers between devices: 136 us -> 5.29 us
  matrix products: 26.4 us -> 0 us
  Pallas kernels: 0 us -> 19.6 us
  blocking collectives: 8.9 us -> 25.2 us
  between operations: 15.3 us -> 0.71 us
  other arithmetic: 8.79 us -> 0 us
  local copies, waits for them, and re-layouts: 5.01 us -> 12.9 us
  starting transfers between devices: 0.17 us -> 5.13 us
    psum x1 -> x0, waiting for transfers between devices: 72.1 us -> none  [on_device(): lax.psum(local_sum, ('gx', 'gy')) / math.sqrt(length_x * length_y * cells_z)]
    reduce_scatter x2 -> x0, waiting for transfers between devices: 64.3 us -> none  [the longest x1 38.6 us: on_device(): lax.psum_scatter(jnp.einsum('bj,fijch->bfich', table_rows, z_modes, preci...]
    dot_general x9 -> x0, matrix products: 26.4 us -> none  [the longest x1 15.4 us: on_device(): jnp.einsum('abcq,abcpq->abcp', grad_modes, spectral_w.astype(jnp.float32)...]
    all_to_all x0 -> x2, blocking collectives: none -> 25.2 us  [exchange(): return lax.all_to_all(pieces, ('gx', 'gy'), 0, 0)]
    pallas_call x0 -> x7, Pallas kernels: none -> 19.6 us  [the longest x1 10.4 us: on_device_whole_planes(): call(functools.partial(outer_kernel, per_step), shaped(cells, channels, c...]
    unnamed x5 -> x28, local copies, waits for them, and re-layouts: 0.74 us -> 12.9 us
    all_gather x1 -> x0, blocking collectives: 8.9 us -> none  [on_device(): lax.all_gather(back_modes, 'gx', axis=0, tiled=True).astype(jnp.float32)]
    convert_element_type x3 -> x0, other arithmetic: 7.94 us -> none  [the longest x1 6.96 us: on_device(): grad_spectral = jnp.einsum('abcp,abcq->abcpq', input_modes, grad_modes, p...]
  transfers between devices with their start and end apart: 4 -> 2, of which waited for: 3 -> 1; matrix products, arithmetic and copies ran while one was open for 13% -> 0% of each run, Pallas kernels for 0% -> 16%
where the time goes in v1:
time: 69.4 us; the launch traced here: 68.8 us
  blocking collectives  25.2 us (36%)
  Pallas kernels  19.6 us (28%)
  local copies, waits for them, and re-layouts  12.9 us (19%)
  waiting for transfers between devices  5.29 us (8%)
  starting transfers between devices  5.13 us (7%)
  between operations  0.71 us (1%)
    all_to_all x2, blocking collectives, exchange(): return lax.all_to_all(pieces, ('gx', 'gy'), 0, 0)  25.2 us
    unnamed x28, local copies, waits for them, and re-layouts  12.9 us
    pallas_call x1, Pallas kernels, on_device_whole_planes(): call(functools.partial(outer_kernel, per_step), shaped(cells, channels, c...  10.4 us
    all_to_all x2, waiting for transfers between devices, exchange(): return lax.all_to_all(pieces, ('gx', 'gy'), 0, 0)  5.29 us
    all_to_all x2, starting transfers between devices, exchange(): return lax.all_to_all(pieces, ('gx', 'gy'), 0, 0)  5.13 us
    pallas_call x1, Pallas kernels, on_device_whole_planes(): call(functools.partial(modes_kernel, t['z_scale'], per_step), (shaped(cha...  4.74 us
    pallas_call x1, Pallas kernels, on_device_whole_planes(): call(functools.partial(plane_kernel, t['plane_scale']), shaped(rows, LANE...  1.43 us
    pallas_call x1, Pallas kernels, on_device_whole_planes(): call(functools.partial(back_plane_kernel, t['back_plane_scale'], 1.0 / ma...  1.41 us
  transfers between devices with their start and end apart: 2, of which 1 were waited for; matrix products, arithmetic and copies ran while one was open for 0% of the time, Pallas kernels for 16%

profile of v1, /device:TPU:0, one launch (start us, length us, event | category | flops | bytes accessed | tf_op | source)
XLA Modules:
  0.0 68.8 jit_solution(6137027651693895297)
XLA Ops:
  0.6 0.0 copy-start.1
  0.7 1.0 %copy-done.3 = bf16[8,4,8,128]{3,2,1,0:T(8,128)(2,1)S(1)} copy-done((bf16[8,4,8,128]{3,2,1,0:T(8,128)(2,1)S(1)}, bf16[8,4,8,128]{3,2,1,0:T(8,128)(2,1)}, u32[]{:S(2)}) %copy-start.3) | copy-done | bytes 65560
  1.6 0.9 %copy-done.9 = bf16[256,256]{1,0:T(8,128)(2,1)S(1)} copy-done((bf16[256,256]{1,0:T(8,128)(2,1)S(1)}, bf16[256,256]{1,0:T(8,128)(2,1)}, u32[]{:S(2)}) %copy-start.9) | copy-done | bytes 131096
  2.5 0.8 %copy-done.10 = bf16[8,4,8,128]{3,2,1,0:T(8,128)(2,1)S(1)} copy-done((bf16[8,4,8,128]{3,2,1,0:T(8,128)(2,1)S(1)}, bf16[8,4,8,128]{3,2,1,0:T(8,128)(2,1)}, u32[]{:S(2)}) %copy-start.10) | copy-done | bytes 65560
  3.4 0.8 %copy-done.11 = bf16[8,4,8,128]{3,2,1,0:T(8,128)(2,1)S(1)} copy-done((bf16[8,4,8,128]{3,2,1,0:T(8,128)(2,1)S(1)}, bf16[8,4,8,128]{3,2,1,0:T(8,128)(2,1)}, u32[]{:S(2)}) %copy-start.11) | copy-done | bytes 65560
  4.2 0.3 shard_map.148
  4.5 15.3 %all_to_all.20 = bf16[32,16,128]{2,1,0:T(8,128)(2,1)S(1)} all-to-all(bf16[32,16,128]{2,1,0:T(8,128)(2,1)S(1)} %bitcast.15), channel_id=1, replica_groups=mesh['gx'=4,'gy'=8] {'gx','gy'}, dimensions={0} | all-to-all | bytes 262144 | tf_op jit(solution)/shard_map/all_to_all | solution.py:303
  19.8 1.6 %copy-done.2 = bf16[2048,512]{1,0:T(8,128)(2,1)S(1)} copy-done((bf16[2048,512]{1,0:T(8,128)(2,1)S(1)}, bf16[2048,512]{1,0:T(8,128)(2,1)}, u32[]{:S(2)}) %copy-start.2) | copy-done | bytes 2097176
  21.4 1.4 %shard_map.149 = bf16[512,128]{1,0:T(8,128)(2,1)} custom-call(bf16[512,128]{1,0:T(8,128)(2,1)S(1)} %bitcast.12, bf16[2048,512]{1,0:T(8,128)(2,1)S(1)} %copy-done.2), custom_call_target="tpu_custom_call" | custom-call | flops 268435456 | bytes 4194304 | tf_op jit(solution)/shard_map/pallas_call | solution.py:324
  22.8 2.6 %all-to-all-start.1 = ((bf16[32,16,128]{2,1,0:T(8,128)(2,1)}), bf16[32,16,128]{2,1,0:T(8,128)(2,1)S(1)}, u32[]{:S(2)}, u32[]{:S(2)}) async-start(bf16[32,16,128]{2,1,0:T(8,128)(2,1)} %bitcast.5), calls=%async_computation.1 | async-start | bytes 262144 | tf_op jit(solution)/shard_map/all_to_all | solution.py:303
  25.4 0.8 %copy-done.4 = bf16[8,4,8,128]{3,2,1,0:T(8,128)(2,1)S(1)} copy-done((bf16[8,4,8,128]{3,2,1,0:T(8,128)(2,1)S(1)}, bf16[8,4,8,128]{3,2,1,0:T(8,128)(2,1)}, u32[]{:S(2)}) %copy-start.4) | copy-done | bytes 65560
  26.3 0.9 %copy-done.8 = bf16[256,256]{1,0:T(8,128)(2,1)S(1)} copy-done((bf16[256,256]{1,0:T(8,128)(2,1)S(1)}, bf16[256,256]{1,0:T(8,128)(2,1)}, u32[]{:S(2)}) %copy-start.8) | copy-done | bytes 131096
  27.2 0.8 %copy-done.13 = bf16[128,128]{1,0:T(8,128)(2,1)S(1)} copy-done((bf16[128,128]{1,0:T(8,128)(2,1)S(1)}, bf16[128,128]{1,0:T(8,128)(2,1)}, u32[]{:S(2)}) %copy-start.13) | copy-done | bytes 32792
  27.9 0.4 shard_map.150
  28.3 5.3 %all-to-all-done.1 = bf16[32,16,128]{2,1,0:T(8,128)(2,1)S(1)} async-done(((bf16[32,16,128]{2,1,0:T(8,128)(2,1)}), bf16[32,16,128]{2,1,0:T(8,128)(2,1)S(1)}, u32[]{:S(2)}, u32[]{:S(2)}) %all-to-all-start.1) | async-done | bytes 131104 | tf_op jit(solution)/shard_map/all_to_all | solution.py:303
  33.6 3.4 %copy-done = bf16[8,4,8,128,128]{4,3,2,1,0:T(8,128)(2,1)S(1)} copy-done((bf16[8,4,8,128,128]{4,3,2,1,0:T(8,128)(2,1)S(1)}, bf16[8,4,8,128,128]{4,3,2,1,0:T(8,128)(2,1)}, u32[]{:S(2)}) %copy-start) | copy-done | bytes 8388632
  37.0 0.9 %copy-done.5 = bf16[256,256]{1,0:T(8,128)(2,1)S(1)} copy-done((bf16[256,256]{1,0:T(8,128)(2,1)S(1)}, bf16[256,256]{1,0:T(8,128)(2,1)}, u32[]{:S(2)}) %copy-start.5) | copy-done | bytes 131096
  37.9 0.9 %copy-done.6 = bf16[256,256]{1,0:T(8,128)(2,1)S(1)} copy-done((bf16[256,256]{1,0:T(8,128)(2,1)S(1)}, bf16[256,256]{1,0:T(8,128)(2,1)}, u32[]{:S(2)}) %copy-start.6) | copy-done | bytes 131096
  38.8 4.7 %shard_map.151 = (f32[128,256]{1,0:T(8,128)S(1)}, f32[256,128]{1,0:T(8,128)S(1)}, bf16[32,16,128]{2,1,0:T(8,128)(2,1)S(1)}) custom-call(bf16[2,2,128,128]{3,2,1,0:T(8,128)(2,1)S(1)} %bitcast.11, bf16[256,256]{1,0:T(8,128)(2,1)S(1)} %copy-done.6, bf16[256,128,128]{2,1,0:T(8,128)(2,1)S(1)} %bitcast.10, bf16[256,256]{1,0:T(8,128)(2,1)S(1)} %copy-done.5, ...), custom_call_target="tpu_custom_call" | custom-call | flops 67108864 | bytes 9437184 | tf_op jit(solution)/shard_map/pallas_call | solution.py:334
  43.5 9.9 %all_to_all.21.x_ref = bf16[32,16,128]{2,1,0:T(8,128)(2,1)S(1)} all-to-all(bf16[32,16,128]{2,1,0:T(8,128)(2,1)S(1)} %get-tuple-element.15), channel_id=1, replica_groups=mesh['gx'=4,'gy'=8] {'gx','gy'}, dimensions={0} | all-to-all | bytes 262144 | tf_op jit(solution)/shard_map/all_to_all | solution.py:303
  53.4 1.4 %shard_map.152 = bf16[32,16,128]{2,1,0:T(8,128)(2,1)} custom-call(bf16[32,16,128]{2,1,0:T(8,128)(2,1)S(1)} %all_to_all.21.x_ref, bf16[1024,1024]{1,0:T(8,128)(2,1)S(1)} %copy-done.1), custom_call_target="tpu_custom_call" | custom-call | flops 268435456 | bytes 4194304 | tf_op jit(solution)/shard_map/pallas_call | solution.py:374
  54.8 2.6 %all-to-all-start.3 = ((bf16[32,16,128]{2,1,0:T(8,128)(2,1)}), bf16[32,16,128]{2,1,0:T(8,128)(2,1)S(1)}, u32[]{:S(2)}, u32[]{:S(2)}) async-start(bf16[32,16,128]{2,1,0:T(8,128)(2,1)} %shard_map.152), calls=%async_computation.3 | async-start | bytes 262144 | tf_op jit(solution)/shard_map/all_to_all | solution.py:303
  57.4 10.4 %shard_map.154 = bf16[256,128,128]{2,1,0:T(8,128)(2,1)} custom-call(f32[128,256]{1,0:T(8,128)S(1)} %get-tuple-element.18.in_ref, f32[256,128]{1,0:T(8,128)S(1)} %get-tuple-element.19.grad_ref), custom_call_target="tpu_custom_call" | custom-call | flops 8388608 | bytes 9437184 | tf_op jit(solution)/shard_map/pallas_call | solution.py:364
  67.8 1.0 %shard_map.153 = (bf16[256,128]{1,0:T(8,128)(2,1)}, f32[128,128]{1,0:T(8,128)}) custom-call(bf16[32,16,128]{2,1,0:T(8,128)(2,1)S(1)} %all-to-all-done.3.x_ref, bf16[256,256]{1,0:T(8,128)(2,1)S(1)} %copy-done.7, f32[256,128]{1,0:T(8,128)S(1)} %get-tuple-element.16.part_ref, bf16[128,256]{1,0:T(8,128)(2,1)S(1)} %copy-done.12), custom_call_target="tpu_custom_call" | custom-call | flops 33554432 | bytes 1048576 | tf_op jit(solution)/shard_map/pallas_call | solution.py:383
  (17 shorter events, 0.0 us)
Async XLA Ops:
  0.6 52.8 %copy-start.1 = (bf16[1024,1024]{1,0:T(8,128)(2,1)S(1)}, bf16[1024,1024]{1,0:T(8,128)(2,1)}, u32[]{:S(2)}) copy-start(bf16[1024,1024]{1,0:T(8,128)(2,1)} %constant.22.clone.table_ref) | copy-start | bytes 6291460
  0.6 1.0 %copy-start.3 = (bf16[8,4,8,128]{3,2,1,0:T(8,128)(2,1)S(1)}, bf16[8,4,8,128]{3,2,1,0:T(8,128)(2,1)}, u32[]{:S(2)}) copy-start(bf16[8,4,8,128]{3,2,1,0:T(8,128)(2,1)} %param.13) | copy-start | bytes 196612
  1.6 0.9 %copy-start.9 = (bf16[256,256]{1,0:T(8,128)(2,1)S(1)}, bf16[256,256]{1,0:T(8,128)(2,1)}, u32[]{:S(2)}) copy-start(bf16[256,256]{1,0:T(8,128)(2,1)} %constant.16.clone.perm_ref) | copy-start | bytes 393220
  2.5 0.8 %copy-start.10 = (bf16[8,4,8,128]{3,2,1,0:T(8,128)(2,1)S(1)}, bf16[8,4,8,128]{3,2,1,0:T(8,128)(2,1)}, u32[]{:S(2)}) copy-start(bf16[8,4,8,128]{3,2,1,0:T(8,128)(2,1)} %param.14) | copy-start | bytes 196612
  3.4 0.8 %copy-start.11 = (bf16[8,4,8,128]{3,2,1,0:T(8,128)(2,1)S(1)}, bf16[8,4,8,128]{3,2,1,0:T(8,128)(2,1)}, u32[]{:S(2)}) copy-start(bf16[8,4,8,128]{3,2,1,0:T(8,128)(2,1)} %param.15) | copy-start | bytes 196612
  19.8 1.6 %copy-start.2 = (bf16[2048,512]{1,0:T(8,128)(2,1)S(1)}, bf16[2048,512]{1,0:T(8,128)(2,1)}, u32[]{:S(2)}) copy-start(bf16[2048,512]{1,0:T(8,128)(2,1)} %constant.19.clone.table_ref) | copy-start | bytes 6291460
  22.8 10.8 %all-to-all-start.1 = ((bf16[32,16,128]{2,1,0:T(8,128)(2,1)}), bf16[32,16,128]{2,1,0:T(8,128)(2,1)S(1)}, u32[]{:S(2)}, u32[]{:S(2)}) async-start(bf16[32,16,128]{2,1,0:T(8,128)(2,1)} %bitcast.5), calls=%async_computation.1 | async-start | bytes 262144 | tf_op jit(solution)/shard_map/all_to_all | solution.py:303
  25.4 0.8 %copy-start.4 = (bf16[8,4,8,128]{3,2,1,0:T(8,128)(2,1)S(1)}, bf16[8,4,8,128]{3,2,1,0:T(8,128)(2,1)}, u32[]{:S(2)}) copy-start(bf16[8,4,8,128]{3,2,1,0:T(8,128)(2,1)} %param.13) | copy-start | bytes 196612
  26.3 0.9 %copy-start.8 = (bf16[256,256]{1,0:T(8,128)(2,1)S(1)}, bf16[256,256]{1,0:T(8,128)(2,1)}, u32[]{:S(2)}) copy-start(bf16[256,256]{1,0:T(8,128)(2,1)} %constant.17.clone.perm_ref) | copy-start | bytes 393220
  27.2 0.8 %copy-start.13 = (bf16[128,128]{1,0:T(8,128)(2,1)S(1)}, bf16[128,128]{1,0:T(8,128)(2,1)}, u32[]{:S(2)}) copy-start(bf16[128,128]{1,0:T(8,128)(2,1)} %skip_ref.1) | copy-start | bytes 98308
  33.6 3.4 %copy-start = (bf16[8,4,8,128,128]{4,3,2,1,0:T(8,128)(2,1)S(1)}, bf16[8,4,8,128,128]{4,3,2,1,0:T(8,128)(2,1)}, u32[]{:S(2)}) copy-start(bf16[8,4,8,128,128]{4,3,2,1,0:T(8,128)(2,1)} %param.16) | copy-start | bytes 25165828
  37.0 0.9 %copy-start.5 = (bf16[256,256]{1,0:T(8,128)(2,1)S(1)}, bf16[256,256]{1,0:T(8,128)(2,1)}, u32[]{:S(2)}) copy-start(bf16[256,256]{1,0:T(8,128)(2,1)} %constant.21.clone.perm_ref) | copy-start | bytes 393220
  37.9 0.9 %copy-start.6 = (bf16[256,256]{1,0:T(8,128)(2,1)S(1)}, bf16[256,256]{1,0:T(8,128)(2,1)}, u32[]{:S(2)}) copy-start(bf16[256,256]{1,0:T(8,128)(2,1)} %constant.20.clone.z_ref) | copy-start | bytes 393220
  38.8 29.0 %copy-start.7 = (bf16[256,256]{1,0:T(8,128)(2,1)S(1)}, bf16[256,256]{1,0:T(8,128)(2,1)}, u32[]{:S(2)}) copy-start(bf16[256,256]{1,0:T(8,128)(2,1)} %constant.23.clone.z_ref) | copy-start | bytes 393220
  38.8 29.0 %copy-start.12 = (bf16[128,256]{1,0:T(8,128)(2,1)S(1)}, bf16[128,256]{1,0:T(8,128)(2,1)}, u32[]{:S(2)}) copy-start(bf16[128,256]{1,0:T(8,128)(2,1)} %constant.18.clone.fold_ref) | copy-start | bytes 196612
  54.8 13.0 %all-to-all-start.3 = ((bf16[32,16,128]{2,1,0:T(8,128)(2,1)}), bf16[32,16,128]{2,1,0:T(8,128)(2,1)S(1)}, u32[]{:S(2)}, u32[]{:S(2)}) async-start(bf16[32,16,128]{2,1,0:T(8,128)(2,1)} %shard_map.152), calls=%async_computation.3 | async-start | bytes 262144 | tf_op jit(solution)/shard_map/all_to_all | solution.py:303

commit v2 on v1

--- a/solution.py
+++ b/solution.py
@@ -75,32 +75,40 @@
     return lax.broadcasted_iota(jnp.int32, shape, len(shape) - 1)
 
 
-def open_kernel(in_ref, pre_ref, cot_ref, perm_ref, pack_ref, grad_ref):
+def load(*pairs):
+    copies = [pltpu.make_async_copy(source, target, sem) for source, target, sem in pairs]
+    for copy in copies:
+        copy.start()
+    return copies
+
+
+def open_kernel(s, in_hbm, pre_hbm, cot_hbm, pack_ref, grad_ref, in_ref, pre_ref, cot_ref, sems):
+    copies = load(
+        (in_hbm, in_ref, sems.at[0]), (pre_hbm, pre_ref, sems.at[1]), (cot_hbm, cot_ref, sems.at[2])
+    )
+    cells = s.cells
+    place = lax.broadcasted_iota(jnp.int32, (cells, 1), 0)
+    half_y = s.y // 2
+    half = cells // 2
+    yl, rest = place // half, place % half
+    z, rest = rest // (s.x * half_y), rest % (s.x * half_y)
+    x, yh = rest // half_y, rest % half_y
+    source = (x * s.y + yh * 2 + yl) * s.z + z
+    order = (lax.broadcasted_iota(jnp.int32, (cells, cells), 1) == source).astype(f32).astype(bf16)
+    for copy in copies:
+        copy.wait()
     grad = (cot_ref[...].astype(f32) * gelu_slope_of(pre_ref[...].astype(f32))).astype(bf16)
     grad_ref[...] = grad
-    half = in_ref.shape[0] // 2
+    rows = jnp.dot(
+        order, jnp.concatenate([in_ref[...], grad], 1), preferred_element_type=f32
+    )
     width = LANES // 2
-    for field, value in enumerate((in_ref[...], grad)):
-        rows = jnp.dot(perm_ref[...], value, preferred_element_type=f32)
-        even, odd = rows[:half], rows[half:]
-        low = lanes_of(even.shape) < width
+    low = lanes_of((half, LANES)) < width
+    for field in range(2):
+        even = rows[:half, field * LANES : (field + 1) * LANES]
+        odd = rows[half:, field * LANES : (field + 1) * LANES]
         pack_ref[field, 0] = jnp.where(low, even, pltpu.roll(odd, width, 1)).astype(bf16)
         pack_ref[field, 1] = jnp.where(low, pltpu.roll(even, width, 1), odd).astype(bf16)
-
-
-def skip_kernel(in_ref, grad_ref, skip_ref, perm_ref, part_ref, sum_ref):
-    grad = grad_ref[...]
-    part_ref[...] = lax.dot_general(
-        grad, skip_ref[...], (((1,), (1,)), ((), ())), preferred_element_type=f32
-    )
-    total = lax.dot_general(
-        in_ref[...], grad, (((0,), (0,)), ((), ())), preferred_element_type=f32
-    )
-    high = total.astype(bf16)
-    low = (total - high.astype(f32)).astype(bf16)
-    sum_ref[...] = jnp.dot(
-        perm_ref[...], jnp.concatenate([high, low], 0), preferred_element_type=f32
-    )
 
 
 def plane_kernel(scale, x_ref, table_ref, out_ref):
@@ -112,77 +120,107 @@
     out_ref[...] = ((straight + pltpu.roll(crossed, width, 1)) * scale).astype(bf16)
 
 
+def field_modes(scale, first, second, z_ref):
+    width = LANES // 2
+    first, second = first.astype(f32), second.astype(f32)
+    low = lanes_of(first.shape) < width
+    even = jnp.where(low, first, pltpu.roll(second, width, 1))
+    odd = jnp.where(low, pltpu.roll(first, width, 1), second)
+    rows = jnp.concatenate([even, odd], 0).astype(bf16)
+    return jnp.dot(z_ref[...], rows, preferred_element_type=f32) * scale
+
+
+def split_twice(value):
+    high = value.astype(bf16)
+    return high, (value - high.astype(f32)).astype(bf16)
+
+
 def modes_kernel(
-    scale, per_step, x_ref, z_ref, w_ref, perm_ref, sum_ref, in_ref, grad_ref, pack_ref, twin, back
+    scale, x_ref, z_ref, w_ref, cut_ref, field_ref, pre_ref, perm_ref, grad_ref, pack_ref, back
 ):
-    step = pl.program_id(0)
-    groups = per_step // 8
-
-    @pl.when(step == 0)
-    def _():
-        width = LANES // 2
-        made = []
-        for field in range(2):
-            first = x_ref[field, 0].astype(f32)
-            second = x_ref[field, 1].astype(f32)
-            low = lanes_of(first.shape) < width
-            even = jnp.where(low, first, pltpu.roll(second, width, 1))
-            odd = jnp.where(low, pltpu.roll(first, width, 1), second)
-            rows = jnp.concatenate([even, odd], 0).astype(bf16)
-            made.append(jnp.dot(z_ref[...], rows, preferred_element_type=f32) * scale)
-        in_ref[...] = made[0].T
-        grad_ref[...] = made[1]
-        high = made[1].astype(bf16).astype(f32)
-        low_part = made[1] - high
-        count = made[1].shape[0] // 8
-        twin[...] = jnp.concatenate(
-            [high.reshape(count, 8, LANES), low_part.reshape(count, 8, LANES)], 1
-        ).astype(bf16)
-
+    grad_ref[...] = field_modes(scale, x_ref[1, 0], x_ref[1, 1], z_ref)
+    sums = lax.dot_general(
+        field_ref[...], pre_ref[...], (((0,), (0,)), ((), ())), preferred_element_type=f32
+    )
+    sums = jnp.dot(
+        perm_ref[...], jnp.concatenate(split_twice(sums), 0), preferred_element_type=f32
+    )
+    groups = grad_ref.shape[0] // 8
+    unrolled = 16
     row = lax.broadcasted_iota(jnp.int32, (8, LANES), 0)
-    for group in range(groups):
-        weights = w_ref[group * 8 : group * 8 + 8].reshape(8 * LANES, LANES)
-        every = lax.dot_general(
-            twin[step * groups + group],
-            weights,
-            (((1,), (1,)), ((), ())),
-            preferred_element_type=f32,
-        )
-        every = every[:8] + every[8:]
-        total = jnp.zeros((8, LANES), f32)
-        for mode in range(8):
-            total += jnp.where(row == mode, every[:, mode * LANES : (mode + 1) * LANES], 0.0)
-        back[pl.ds(pl.multiple_of((step * groups + group) * 8, 8), 8), :] = total
-
-    @pl.when(step == pl.num_programs(0) - 1)
-    def _():
-        rows = jnp.dot(perm_ref[...], back[...].astype(bf16), preferred_element_type=f32)
-        quarter = rows.shape[0] // 4
-        group_of = lanes_of((quarter, LANES)) // (LANES // 4)
-        pieces = []
-        for part in range(4):
-            piece = jnp.zeros((quarter, LANES), f32)
-            for place in range(4):
-                source = rows[place * quarter : (place + 1) * quarter]
-                moved = pltpu.roll(source, (place - part) % 4 * (LANES // 4), 1)
-                piece = jnp.where(group_of == place, moved, piece)
-            pieces.append(piece)
-        every = jnp.concatenate(pieces, 0)
-        count = every.shape[0] // 8
-        pack_ref[...] = jnp.concatenate(
-            [every.reshape(count, 8, LANES), sum_ref[...].reshape(count, 8, LANES)], 1
-        ).astype(bf16)
-
-
-def outer_kernel(per_step, in_ref, grad_ref, out_ref):
-    step = pl.program_id(0)
-    columns = pltpu.roll(in_ref[...], in_ref.shape[1] - step * per_step, 1)
-    for mode in range(per_step):
-        column = jnp.broadcast_to(columns[:, mode : mode + 1], (LANES, LANES))
-        out_ref[mode] = (column * grad_ref[mode : mode + 1, :]).astype(bf16)
-
-
-def back_plane_kernel(scale, skip_scale, x_ref, table_ref, out_ref):
+
+    @pl.loop(0, groups // unrolled)
+    def _(turn):
+        for group in range(unrolled):
+            start = pl.multiple_of((turn * unrolled + group) * 8, 8)
+            modes = grad_ref[pl.ds(start, 8), :]
+            high = modes.astype(bf16).astype(f32)
+            every = lax.dot_general(
+                jnp.concatenate([high, modes - high], 0).astype(bf16),
+                w_ref[pl.ds(start, 8)].reshape(8 * LANES, LANES),
+                (((1,), (1,)), ((), ())),
+                preferred_element_type=f32,
+            )
+            every = every[:8] + every[8:]
+            total = jnp.zeros((8, LANES), f32)
+            for mode in range(8):
+                total += jnp.where(row == mode, every[:, mode * LANES : (mode + 1) * LANES], 0.0)
+            back[pl.ds(start, 8), :] = total
+
+    rows = jnp.dot(cut_ref[...], back[...].astype(bf16), preferred_element_type=f32)
+    quarter = rows.shape[0] // 4
+    group_of = lanes_of((quarter, LANES)) // (LANES // 4)
+    pieces = []
+    for part in range(4):
+        piece = jnp.zeros((quarter, LANES), f32)
+        for place in range(4):
+            source = rows[place * quarter : (place + 1) * quarter]
+            moved = pltpu.roll(source, (place - part) % 4 * (LANES // 4), 1)
+            piece = jnp.where(group_of == place, moved, piece)
+        pieces.append(piece)
+    every = jnp.concatenate(pieces, 0)
+    count = every.shape[0] // 8
+    pack_ref[...] = jnp.concatenate(
+        [every.reshape(count, 8, LANES), sums.reshape(count, 8, LANES)], 1
+    ).astype(bf16)
+
+
+def outer_kernel(scale, x_ref, z_ref, grad_ref, out_hbm, flag_ref, in_ref, made, sems):
+    in_ref[...] = field_modes(scale, x_ref[0, 0], x_ref[0, 1], z_ref)
+    flag_ref[...] = jnp.zeros(flag_ref.shape, f32)
+    modes = in_ref.shape[0]
+    size, unrolled = 16, 4
+    row = lax.broadcasted_iota(jnp.int32, (3 * size, LANES), 0) % size
+
+    def copy(group):
+        part = pl.ds(group * size, size)
+        return pltpu.make_async_copy(made.at[part], out_hbm.at[part], sems.at[group])
+
+    @pl.loop(0, modes // size // unrolled)
+    def _(turn):
+        for at in range(unrolled):
+            group = turn * unrolled + at
+            start = pl.multiple_of(group * size, size)
+            in_high, in_low = split_twice(in_ref[pl.ds(start, size), :])
+            high, low = split_twice(grad_ref[pl.ds(start, size), :])
+            left = jnp.concatenate([in_high, in_low, in_high], 0)
+            right = jnp.concatenate([high, high, low], 0)
+            zero = jnp.zeros((), bf16)
+            right = jnp.concatenate([jnp.where(row == mode, right, zero) for mode in range(size)], 1)
+            every = lax.dot_general(
+                left, right, (((0,), (0,)), ((), ())), preferred_element_type=f32
+            )
+            for mode in range(size):
+                made[group * size + mode] = every[:, mode * LANES : (mode + 1) * LANES].astype(bf16)
+            copy(group).start()
+
+    @pl.loop(0, modes // size)
+    def _(group):
+        copy(group).wait()
+
+
+def back_plane_kernel(scale, skip_scale, x_ref, table_ref, after, out_ref):
+    del after
     every = x_ref[...].astype(f32)
     count = every.shape[0]
     rows = count * 8
@@ -206,7 +244,7 @@
     ).astype(bf16)
 
 
-def close_kernel(scale, x_ref, z_ref, part_ref, fold_ref, out_ref, skip_ref):
+def close_kernel(scale, x_ref, z_ref, pre_ref, weight_ref, fold_ref, out_ref, skip_ref):
     every = x_ref[...].astype(f32)
     count = every.shape[0]
     rows = every[:, :8].reshape(count * 8, LANES)
@@ -223,7 +261,10 @@
     cells = jnp.dot(
         z_ref[...], jnp.concatenate(pieces, 0).astype(bf16), preferred_element_type=f32
     )
-    out_ref[...] = (part_ref[...] + cells * scale).astype(bf16)
+    part = lax.dot_general(
+        pre_ref[...], weight_ref[...], (((1,), (1,)), ((), ())), preferred_element_type=f32
+    )
+    out_ref[...] = (part + cells * scale).astype(bf16)
     sums = every[:, 8:].reshape(count * 8, LANES).astype(bf16)
     skip_ref[...] = jnp.dot(fold_ref[...], sums, preferred_element_type=f32)
 
@@ -238,8 +279,6 @@
     cas_z = plain_cas(s.z, s.z)
     norm = math.sqrt(s.x * s.gx * s.y * s.gy)
     t = {}
-    yl, z, x, yh = split_index(s.cells, 2, s.z, s.x, s.y // 2)
-    t["cut"] = one_hot((x * s.y + yh * 2 + yl) * s.z + z, np.arange(s.cells))
     device, which, row = split_index(2 * s.channels, s.devices, 2, 4)
     t["sums"] = one_hot(which * s.channels + device * 4 + row, np.arange(2 * s.channels))
     device, which, row = split_index(2 * s.channels, s.devices, 2, 4)
@@ -285,17 +324,21 @@
     }
 
 
-def call(kernel, out_shape, limit, cost, **more):
+def call(kernel, out_shape, limit, flops, moved, **more):
     return pl.pallas_call(
         kernel,
         out_shape=out_shape,
         compiler_params=pltpu.CompilerParams(vmem_limit_bytes=limit * MIB),
-        cost_estimate=pl.CostEstimate(flops=cost[0], bytes_accessed=cost[1], transcendentals=0),
+        cost_estimate=pl.CostEstimate(flops=flops, bytes_accessed=moved, transcendentals=0),
         **more,
     )
 
 
-def shaped(*shape, kind=bf16):
+def in_vmem(*shape, kind=bf16):
+    return pltpu.VMEM(shape, kind)
+
+
+def in_hbm(*shape, kind=bf16):
     return jax.ShapeDtypeStruct(shape, kind)
 
 
@@ -306,86 +349,89 @@
 def on_device_whole_planes(s, inputs, preact, cotangent, spectral_w, skip_w):
     t = make_tables(s)
     cells, channels, devices = s.cells, s.channels, s.devices
+    rows = cells // s.z // 2 * devices
+    back_rows = devices * s.x
     flat = lambda array: array.reshape(cells, channels)
+    vmem = pl.BlockSpec(memory_space=pltpu.VMEM)
+    hbm = pl.BlockSpec(memory_space=pltpu.HBM)
+    anywhere = pl.BlockSpec(memory_space=pl.ANY)
+    field = pltpu.VMEM((cells, channels), bf16)
     pieces, grad_pre = call(
-        open_kernel,
-        (shaped(2, 2, cells // 2, LANES), shaped(cells, channels)),
+        functools.partial(open_kernel, s),
+        (in_vmem(2, 2, cells // 2, LANES), in_vmem(cells, channels)),
         16,
-        (cells * cells * LANES * 4, 1 * MIB),
-    )(flat(inputs), flat(preact), flat(cotangent), t["cut"])
+        1 << 40,
+        MIB,
+        in_specs=[hbm] * 3,
+        out_specs=(vmem, vmem),
+        scratch_shapes=[field, field, field, pltpu.SemaphoreType.DMA((3,))],
+    )(*(pltpu.with_memory_space_constraint(flat(a), pltpu.HBM) for a in (inputs, preact, cotangent)))
     columns = exchange(pieces.reshape(devices, -1, LANES))
-    skip_part, sums = call(
-        skip_kernel,
-        (shaped(cells, channels, kind=f32), shaped(2 * channels, channels, kind=f32)),
-        16,
-        (cells * channels * channels * 8, 4 * MIB),
-    )(flat(inputs), grad_pre, skip_w, t["sums"])
-    rows = cells // s.z // 2 * devices
     planes = call(
         functools.partial(plane_kernel, t["plane_scale"]),
-        shaped(rows, LANES),
+        in_vmem(rows, LANES),
         16,
-        (rows * rows * LANES * 8, 4 * MIB),
+        1 << 36,
+        4 * MIB,
+        in_specs=[vmem, vmem],
+        out_specs=vmem,
     )(columns.reshape(rows, LANES), t["plane"])
     owned = exchange(planes.reshape(devices, -1, LANES))
-
-    per_step = 16
-    whole = lambda *shape: pl.BlockSpec(shape, lambda i: (0,) * len(shape))
-    input_modes, grad_modes, back = call(
-        functools.partial(modes_kernel, t["z_scale"], per_step),
-        (
-            shaped(channels, cells, kind=f32),
-            shaped(cells, channels, kind=f32),
-            shaped(devices, 16, LANES),
-        ),
+    owned = owned.reshape(2, 2, cells // 2, LANES)
+    grad_modes, back = call(
+        functools.partial(modes_kernel, t["z_scale"]),
+        (in_vmem(cells, channels, kind=f32), in_vmem(devices, 16, LANES)),
         24,
-        (cells * channels * channels * 16, 9 * MIB),
-        grid=(cells // per_step,),
-        in_specs=[
-            whole(2, 2, cells // 2, LANES),
-            whole(cells, cells),
-            pl.BlockSpec((per_step, channels, channels), lambda i: (i, 0, 0)),
-            whole(cells, cells),
-            whole(2 * channels, channels),
-        ],
-        out_specs=(whole(channels, cells), whole(cells, channels), whole(devices, 16, LANES)),
-        scratch_shapes=[
-            pltpu.VMEM((cells // 8, 16, LANES), bf16),
-            pltpu.VMEM((cells, channels), f32),
-        ],
+        cells * channels * channels * 16,
+        9 * MIB,
+        in_specs=[vmem] * 7,
+        out_specs=(vmem, vmem),
+        scratch_shapes=[pltpu.VMEM((cells, channels), f32)],
     )(
-        owned.reshape(2, 2, cells // 2, LANES),
+        owned,
         t["z"],
         spectral_w.reshape(cells, channels, channels),
         t["back_cut"],
-        sums,
+        flat(inputs),
+        grad_pre,
+        t["sums"],
     )
     back_columns = exchange(back)
-    grad_spectral = call(
-        functools.partial(outer_kernel, per_step),
-        shaped(cells, channels, channels),
-        16,
-        (cells * channels * channels * 2, 9 * MIB),
-        grid=(cells // per_step,),
-        in_specs=[whole(channels, cells), pl.BlockSpec((per_step, channels), lambda i: (i, 0))],
-        out_specs=pl.BlockSpec((per_step, channels, channels), lambda i: (i, 0, 0)),
-    )(input_modes, grad_modes)
-    total_cells = cells * devices
+    grad_spectral, flag = call(
+        functools.partial(outer_kernel, t["z_scale"]),
+        (in_hbm(cells, channels, channels), in_vmem(8, LANES, kind=f32)),
+        24,
+        cells * channels * channels * 2,
+        9 * MIB,
+        in_specs=[vmem] * 3,
+        out_specs=(hbm, vmem),
+        scratch_shapes=[
+            pltpu.VMEM((cells, channels), f32),
+            pltpu.VMEM((cells, channels, channels), bf16),
+            pltpu.SemaphoreType.DMA((cells // 16,)),
+        ],
+    )(owned, t["z"], grad_modes)
     back_planes = call(
         functools.partial(
-            back_plane_kernel, t["back_plane_scale"], 1.0 / math.sqrt(total_cells)
+            back_plane_kernel, t["back_plane_scale"], 1.0 / math.sqrt(cells * devices)
         ),
-        shaped(devices, 16, LANES),
+        in_vmem(devices, 16, LANES),
         16,
-        (rows * rows * LANES * 8, 4 * MIB),
-    )(back_columns, t["back_plane"])
+        back_rows * back_rows * LANES * 32,
+        4 * MIB,
+        in_specs=[vmem, vmem, anywhere],
+        out_specs=vmem,
+    )(back_columns, t["back_plane"], flag)
     spectral = exchange(back_planes)
     grad_inputs, grad_skip = call(
         functools.partial(close_kernel, t["z_scale"]),
-        (shaped(cells, channels), shaped(channels, channels, kind=f32)),
+        (in_hbm(cells, channels), in_hbm(channels, channels, kind=f32)),
         16,
-        (cells * cells * LANES * 4, 1 * MIB),
-    )(spectral, t["back_z"], skip_part, t["fold"])
+        cells * cells * LANES * 4,
+        MIB,
+        in_specs=[vmem] * 5,
+        out_specs=(vmem, vmem),
+    )(spectral, t["back_z"], grad_pre, skip_w, t["fold"])
     return (
         grad_inputs.reshape(inputs.shape),
         grad_spectral.reshape(spectral_w.shape),

time: 69.4 us -> 54.8 us (0.79)
  local copies, waits for them, and re-layouts: 12.9 us -> 0.06 us
  blocking collectives: 25.2 us -> 35.3 us
  Pallas kernels: 19.6 us -> 11.9 us
  starting transfers between devices: 5.13 us -> 2.56 us
  waiting for transfers between devices: 5.29 us -> 3.95 us
    unnamed x28 -> x20, local copies, waits for them, and re-layouts: 12.9 us -> 0.06 us
    all_to_all x2 -> x3, blocking collectives: 25.2 us -> 35.3 us  [exchange(): return lax.all_to_all(pieces, ('gx', 'gy'), 0, 0)]
    pallas_call x6 -> x5, Pallas kernels: 18.2 us -> 11.2 us  [the longest x1 4.21 us: on_device_whole_planes(): call(functools.partial(outer_kernel, t['z_scale']), (in_hbm(cells, channe...]
    all_to_all x2 -> x1, starting transfers between devices: 5.13 us -> 2.56 us  [exchange(): return lax.all_to_all(pieces, ('gx', 'gy'), 0, 0)]
    all_to_all x2 -> x1, waiting for transfers between devices: 5.29 us -> 3.95 us  [exchange(): return lax.all_to_all(pieces, ('gx', 'gy'), 0, 0)]
  transfers between devices with their start and end apart: 2 -> 1, of which waited for: 1 -> 1; matrix products, arithmetic and copies ran while one was open for 0% -> 0% of each run, Pallas kernels for 16% -> 8%
where the time goes in v2:
time: 54.8 us; the launch traced here: 54.6 us
  blocking collectives  35.3 us (64%)
  Pallas kernels  11.9 us (22%)
  waiting for transfers between devices  3.95 us (7%)
  starting transfers between devices  2.56 us (5%)
  between operations  0.76 us (1%)
    all_to_all x3, blocking collectives, exchange(): return lax.all_to_all(pieces, ('gx', 'gy'), 0, 0)  35.3 us
    pallas_call x1, Pallas kernels, on_device_whole_planes(): call(functools.partial(outer_kernel, t['z_scale']), (in_hbm(cells, channe...  4.21 us
    all_to_all x1, waiting for transfers between devices, exchange(): return lax.all_to_all(pieces, ('gx', 'gy'), 0, 0)  3.95 us
    pallas_call x1, Pallas kernels, on_device_whole_planes(): call(functools.partial(modes_kernel, t['z_scale']), (in_vmem(cells, chann...  3.84 us
    all_to_all x1, starting transfers between devices, exchange(): return lax.all_to_all(pieces, ('gx', 'gy'), 0, 0)  2.56 us
    pallas_call x1, Pallas kernels, on_device_whole_planes(): call(functools.partial(open_kernel, s), (in_vmem(2, 2, cells // 2, LANES)...  1.38 us
  transfers between devices with their start and end apart: 1, of which 1 were waited for; matrix products, arithmetic and copies ran while one was open for 0% of the time, Pallas kernels for 8%

profile of v2, /device:TPU:0, one launch (start us, length us, event | category | flops | bytes accessed | tf_op | source)
XLA Modules:
  0.0 54.6 jit_solution(1177124546585780216)
XLA Ops:
  0.6 0.0 copy-start.9
  0.6 1.4 %shard_map.139 = (bf16[2,2,128,128]{3,2,1,0:T(8,128)(2,1)S(1)}, bf16[256,128]{1,0:T(8,128)(2,1)S(1)}) custom-call(bf16[256,128]{1,0:T(8,128)(2,1)} %bitcast.16, bf16[256,128]{1,0:T(8,128)(2,1)} %bitcast.19, bf16[256,128]{1,0:T(8,128)(2,1)} %bitcast.20), custom_call_target="tpu_custom_call" | custom-call | flops 1099511627776 | bytes 1048576 | tf_op jit(solution)/shard_map/pallas_call | solution.py:359
  2.0 15.3 %all_to_all.20 = bf16[32,16,128]{2,1,0:T(8,128)(2,1)S(1)} all-to-all(bf16[32,16,128]{2,1,0:T(8,128)(2,1)S(1)} %bitcast.13), channel_id=1, replica_groups=mesh['gx'=4,'gy'=8] {'gx','gy'}, dimensions={0} | all-to-all | bytes 262144 | tf_op jit(solution)/shard_map/all_to_all | solution.py:346
  17.3 0.0 copy-done.9
  17.3 0.0 copy-start.4
  17.3 0.0 copy-start.6
  17.4 0.8 %shard_map.140 = bf16[512,128]{1,0:T(8,128)(2,1)S(1)} custom-call(bf16[512,128]{1,0:T(8,128)(2,1)S(1)} %bitcast.14, bf16[2048,512]{1,0:T(8,128)(2,1)S(1)} %copy-done.9), custom_call_target="tpu_custom_call" | custom-call | flops 68719476736 | bytes 4194304 | tf_op jit(solution)/shard_map/pallas_call | solution.py:370
  18.1 0.0 copy-start.1
  18.1 0.0 copy-start.5
  18.2 0.0 copy-start.7
  18.2 0.0 copy-start.8
  18.2 10.1 %all_to_all.21 = bf16[32,16,128]{2,1,0:T(8,128)(2,1)S(1)} all-to-all(bf16[32,16,128]{2,1,0:T(8,128)(2,1)S(1)} %bitcast.15), channel_id=1, replica_groups=mesh['gx'=4,'gy'=8] {'gx','gy'}, dimensions={0} | all-to-all | bytes 262144 | tf_op jit(solution)/shard_map/all_to_all | solution.py:346
  28.3 0.0 copy-done
  28.3 0.0 copy-done.2
  28.3 0.0 copy-done.3
  28.3 0.0 copy-done.4
  28.3 0.0 copy-done.6
  28.4 3.8 %shard_map.141 = (f32[256,128]{1,0:T(8,128)S(1)}, bf16[32,16,128]{2,1,0:T(8,128)(2,1)}) custom-call(bf16[2,2,128,128]{3,2,1,0:T(8,128)(2,1)S(1)} %bitcast.11, bf16[256,256]{1,0:T(8,128)(2,1)S(1)} %copy-done.2, bf16[256,128,128]{2,1,0:T(8,128)(2,1)S(1)} %bitcast.10, bf16[256,256]{1,0:T(8,128)(2,1)S(1)} %copy-done.3, bf16[256,128]{1,0:T(8,128)(2,1)S(1)} %bitcast.17, ...), custom_call_target="tpu_custom_call" | custom-call | flops 67108864 | bytes 9437184 | tf_op jit(solution)/shard_map/pallas_call | solution.py:381
  32.2 2.6 %all-to-all-start.2 = ((bf16[32,16,128]{2,1,0:T(8,128)(2,1)}), bf16[32,16,128]{2,1,0:T(8,128)(2,1)S(1)}, u32[]{:S(2)}, u32[]{:S(2)}) async-start(bf16[32,16,128]{2,1,0:T(8,128)(2,1)} %get-tuple-element.13), calls=%async_computation.2 | async-start | bytes 262144 | tf_op jit(solution)/shard_map/all_to_all | solution.py:346
  34.8 4.2 %shard_map.142 = (bf16[256,128,128]{2,1,0:T(8,128)(2,1)}, f32[8,128]{1,0:T(8,128)S(1)}) custom-call(bf16[2,2,128,128]{3,2,1,0:T(8,128)(2,1)S(1)} %bitcast.12, bf16[256,256]{1,0:T(8,128)(2,1)S(1)} %copy-done.2, f32[256,128]{1,0:T(8,128)S(1)} %get-tuple-element.14.grad_ref), custom_call_target="tpu_custom_call" | custom-call | flops 8388608 | bytes 9437184 | tf_op jit(solution)/shard_map/pallas_call | solution.py:400
  39.0 4.0 %all-to-all-done.2.x_ref = bf16[32,16,128]{2,1,0:T(8,128)(2,1)S(1)} async-done(((bf16[32,16,128]{2,1,0:T(8,128)(2,1)}), bf16[32,16,128]{2,1,0:T(8,128)(2,1)S(1)}, u32[]{:S(2)}, u32[]{:S(2)}) %all-to-all-start.2) | async-done | bytes 131104 | tf_op jit(solution)/shard_map/all_to_all | solution.py:346
  42.9 0.8 %shard_map.143 = bf16[32,16,128]{2,1,0:T(8,128)(2,1)S(1)} custom-call(bf16[32,16,128]{2,1,0:T(8,128)(2,1)S(1)} %all-to-all-done.2.x_ref, bf16[1024,1024]{1,0:T(8,128)(2,1)S(1)} %copy-done.1, f32[8,128]{1,0:T(8,128)S(1)} %get-tuple-element.15.after), custom_call_target="tpu_custom_call" | custom-call | flops 268435456 | bytes 4194304 | tf_op jit(solution)/shard_map/pallas_call | solution.py:414
  43.7 9.9 %all_to_all.22.x_ref = bf16[32,16,128]{2,1,0:T(8,128)(2,1)S(1)} all-to-all(bf16[32,16,128]{2,1,0:T(8,128)(2,1)S(1)} %shard_map.143), channel_id=1, replica_groups=mesh['gx'=4,'gy'=8] {'gx','gy'}, dimensions={0} | all-to-all | bytes 262144 | tf_op jit(solution)/shard_map/all_to_all | solution.py:346
  53.6 0.9 %shard_map.144 = (bf16[256,128]{1,0:T(8,128)(2,1)}, f32[128,128]{1,0:T(8,128)}) custom-call(bf16[32,16,128]{2,1,0:T(8,128)(2,1)S(1)} %all_to_all.22.x_ref, bf16[256,256]{1,0:T(8,128)(2,1)S(1)} %copy-done.5, bf16[256,128]{1,0:T(8,128)(2,1)S(1)} %get-tuple-element.12.pre_ref, bf16[128,128]{1,0:T(8,128)(2,1)S(1)} %copy-done.8, bf16[128,256]{1,0:T(8,128)(2,1)S(1)} %copy-done.7), custom_call_target="tpu_custom_call" | custom-call | flops 33554432 | bytes 1048576 | tf_op jit(solution)/shard_map/pallas_call | solution.py:426
  (7 shorter events, 0.0 us)
Async XLA Ops:
  0.6 16.7 %copy-start.9 = (bf16[2048,512]{1,0:T(8,128)(2,1)S(1)}, bf16[2048,512]{1,0:T(8,128)(2,1)}, u32[]{:S(2)}) copy-start(bf16[2048,512]{1,0:T(8,128)(2,1)} %constant.16.clone.table_ref) | copy-start | bytes 6291460
  17.3 11.0 %copy-start = (bf16[8,4,8,128,128]{4,3,2,1,0:T(8,128)(2,1)S(1)}, bf16[8,4,8,128,128]{4,3,2,1,0:T(8,128)(2,1)}, u32[]{:S(2)}) copy-start(bf16[8,4,8,128,128]{4,3,2,1,0:T(8,128)(2,1)} %param.15) | copy-start | bytes 25165828
  17.3 11.0 %copy-start.2 = (bf16[256,256]{1,0:T(8,128)(2,1)S(1)}, bf16[256,256]{1,0:T(8,128)(2,1)}, u32[]{:S(2)}) copy-start(bf16[256,256]{1,0:T(8,128)(2,1)} %constant.17.clone.z_ref) | copy-start | bytes 393220
  17.3 11.0 %copy-start.3 = (bf16[256,256]{1,0:T(8,128)(2,1)S(1)}, bf16[256,256]{1,0:T(8,128)(2,1)}, u32[]{:S(2)}) copy-start(bf16[256,256]{1,0:T(8,128)(2,1)} %constant.18.clone.cut_ref) | copy-start | bytes 393220
  17.3 11.0 %copy-start.4 = (bf16[256,256]{1,0:T(8,128)(2,1)S(1)}, bf16[256,256]{1,0:T(8,128)(2,1)}, u32[]{:S(2)}) copy-start(bf16[256,256]{1,0:T(8,128)(2,1)} %constant.14.clone.perm_ref) | copy-start | bytes 393220
  17.3 11.0 %copy-start.6 = (bf16[8,4,8,128]{3,2,1,0:T(8,128)(2,1)S(1)}, bf16[8,4,8,128]{3,2,1,0:T(8,128)(2,1)}, u32[]{:S(2)}) copy-start(bf16[8,4,8,128]{3,2,1,0:T(8,128)(2,1)} %param.12) | copy-start | bytes 196612
  18.1 24.8 %copy-start.1 = (bf16[1024,1024]{1,0:T(8,128)(2,1)S(1)}, bf16[1024,1024]{1,0:T(8,128)(2,1)}, u32[]{:S(2)}) copy-start(bf16[1024,1024]{1,0:T(8,128)(2,1)} %constant.19.clone.table_ref) | copy-start | bytes 6291460
  18.1 35.5 %copy-start.5 = (bf16[256,256]{1,0:T(8,128)(2,1)S(1)}, bf16[256,256]{1,0:T(8,128)(2,1)}, u32[]{:S(2)}) copy-start(bf16[256,256]{1,0:T(8,128)(2,1)} %constant.20.clone.z_ref) | copy-start | bytes 393220
  18.2 35.4 %copy-start.7 = (bf16[128,256]{1,0:T(8,128)(2,1)S(1)}, bf16[128,256]{1,0:T(8,128)(2,1)}, u32[]{:S(2)}) copy-start(bf16[128,256]{1,0:T(8,128)(2,1)} %constant.15.clone.fold_ref) | copy-start | bytes 196612
  18.2 35.4 %copy-start.8 = (bf16[128,128]{1,0:T(8,128)(2,1)S(1)}, bf16[128,128]{1,0:T(8,128)(2,1)}, u32[]{:S(2)}) copy-start(bf16[128,128]{1,0:T(8,128)(2,1)} %weight_ref.1) | copy-start | bytes 98308
  32.2 10.7 %all-to-all-start.2 = ((bf16[32,16,128]{2,1,0:T(8,128)(2,1)}), bf16[32,16,128]{2,1,0:T(8,128)(2,1)S(1)}, u32[]{:S(2)}, u32[]{:S(2)}) async-start(bf16[32,16,128]{2,1,0:T(8,128)(2,1)} %get-tuple-element.13), calls=%async_computation.2 | async-start | bytes 262144 | tf_op jit(solution)/shard_map/all_to_all | solution.py:346

commit v3 on v2

--- a/solution.py
+++ b/solution.py
@@ -135,58 +135,68 @@
     return high, (value - high.astype(f32)).astype(bf16)
 
 
-def modes_kernel(
-    scale, x_ref, z_ref, w_ref, cut_ref, field_ref, pre_ref, perm_ref, grad_ref, pack_ref, back
-):
-    grad_ref[...] = field_modes(scale, x_ref[1, 0], x_ref[1, 1], z_ref)
-    sums = lax.dot_general(
-        field_ref[...], pre_ref[...], (((0,), (0,)), ((), ())), preferred_element_type=f32
-    )
-    sums = jnp.dot(
-        perm_ref[...], jnp.concatenate(split_twice(sums), 0), preferred_element_type=f32
-    )
-    groups = grad_ref.shape[0] // 8
-    unrolled = 16
-    row = lax.broadcasted_iota(jnp.int32, (8, LANES), 0)
-
-    @pl.loop(0, groups // unrolled)
-    def _(turn):
-        for group in range(unrolled):
-            start = pl.multiple_of((turn * unrolled + group) * 8, 8)
-            modes = grad_ref[pl.ds(start, 8), :]
-            high = modes.astype(bf16).astype(f32)
-            every = lax.dot_general(
-                jnp.concatenate([high, modes - high], 0).astype(bf16),
-                w_ref[pl.ds(start, 8)].reshape(8 * LANES, LANES),
-                (((1,), (1,)), ((), ())),
-                preferred_element_type=f32,
-            )
-            every = every[:8] + every[8:]
-            total = jnp.zeros((8, LANES), f32)
-            for mode in range(8):
-                total += jnp.where(row == mode, every[:, mode * LANES : (mode + 1) * LANES], 0.0)
-            back[pl.ds(start, 8), :] = total
-
-    rows = jnp.dot(cut_ref[...], back[...].astype(bf16), preferred_element_type=f32)
+def quarters(rows):
     quarter = rows.shape[0] // 4
     group_of = lanes_of((quarter, LANES)) // (LANES // 4)
     pieces = []
     for part in range(4):
-        piece = jnp.zeros((quarter, LANES), f32)
+        piece = rows[:quarter]
         for place in range(4):
             source = rows[place * quarter : (place + 1) * quarter]
-            moved = pltpu.roll(source, (place - part) % 4 * (LANES // 4), 1)
+            turn = (place - part) % 4
+            moved = source if turn == 0 else pltpu.roll(source, turn * (LANES // 4), 1)
             piece = jnp.where(group_of == place, moved, piece)
         pieces.append(piece)
-    every = jnp.concatenate(pieces, 0)
-    count = every.shape[0] // 8
-    pack_ref[...] = jnp.concatenate(
-        [every.reshape(count, 8, LANES), sums.reshape(count, 8, LANES)], 1
+    return jnp.concatenate(pieces, 0)
+
+
+def modes_kernel(scale, x_ref, z_ref, w_ref, field_ref, pre_ref, pack_ref, sum_ref, modes_ref, back):
+    sum_ref[...] = lax.dot_general(
+        field_ref[...], pre_ref[...], (((0,), (0,)), ((), ())), preferred_element_type=f32
     ).astype(bf16)
-
-
-def outer_kernel(scale, x_ref, z_ref, grad_ref, out_hbm, flag_ref, in_ref, made, sems):
+    modes_ref[...] = field_modes(scale, x_ref[1, 0], x_ref[1, 1], z_ref)
+    groups = modes_ref.shape[0] // 8
+    unrolled, on_vector = 16, 4
+    row = lax.broadcasted_iota(jnp.int32, (8, LANES), 0)
+    lane = lanes_of((LANES, LANES))
+
+    @pl.loop(0, groups // unrolled)
+    def _(turn):
+        kept = jnp.zeros((LANES, LANES), f32)
+        for at in range(unrolled):
+            group = turn * unrolled + at
+            start = pl.multiple_of(group * 8, 8)
+            if at < unrolled - on_vector:
+                modes = modes_ref[pl.ds(start, 8), :]
+                high = modes.astype(bf16).astype(f32)
+                every = lax.dot_general(
+                    jnp.concatenate([high, modes - high], 0).astype(bf16),
+                    w_ref[:, group].reshape(8 * LANES, LANES),
+                    (((1,), (1,)), ((), ())),
+                    preferred_element_type=f32,
+                )
+                every = every[:8] + every[8:]
+                total = jnp.zeros((8, LANES), f32)
+                for mode in range(8):
+                    part = every[:, mode * LANES : (mode + 1) * LANES]
+                    total = jnp.where(row == mode, part, total)
+                back[pl.ds(start, 8), :] = total
+            else:
+                for mode in range(8):
+                    weights = w_ref[mode, group].astype(f32)
+                    total = jnp.sum(weights * modes_ref[pl.ds(start + mode, 1), :], 1, keepdims=True)
+                    place = (at - unrolled + on_vector) * 8 + mode
+                    kept = jnp.where(lane == place, total, kept)
+        start = pl.multiple_of(((turn + 1) * unrolled - on_vector) * 8, 8)
+        back[pl.ds(start, on_vector * 8), :] = kept.T[: on_vector * 8]
+
+    rows = back[...].astype(bf16).astype(f32)
+    pack_ref[...] = quarters(rows).astype(bf16)
+
+
+def outer_kernel(scale, x_ref, z_ref, out_hbm, flag_ref, in_ref, grad_ref, made, sems):
     in_ref[...] = field_modes(scale, x_ref[0, 0], x_ref[0, 1], z_ref)
+    grad_ref[...] = field_modes(scale, x_ref[1, 0], x_ref[1, 1], z_ref)
     flag_ref[...] = jnp.zeros(flag_ref.shape, f32)
     modes = in_ref.shape[0]
     size, unrolled = 16, 4
@@ -219,12 +229,10 @@
         copy(group).wait()
 
 
-def back_plane_kernel(scale, skip_scale, x_ref, table_ref, after, out_ref):
+def back_plane_kernel(scale, x_ref, table_ref, after, out_ref):
     del after
-    every = x_ref[...].astype(f32)
-    count = every.shape[0]
-    rows = count * 8
-    x = every[:, :8].reshape(rows, LANES)
+    x = x_ref[...].astype(f32)
+    rows = x.shape[0]
     turned = [x if s == 0 else pltpu.roll(x, s * (LANES // 4), 1) for s in range(4)]
     made = jnp.dot(
         table_ref[...], jnp.concatenate(turned, 0).astype(bf16), preferred_element_type=f32
@@ -233,40 +241,17 @@
     out = made[:rows]
     for place in range(1, 4):
         out = jnp.where(group_of == place, made[place * rows : (place + 1) * rows], out)
-    out = out * scale
-    parts = jnp.sum(every[:, 8:], 0)
-    total = (parts + pltpu.roll(parts, 4, 0)) * skip_scale
-    high = total.astype(bf16).astype(f32)
-    row = lax.broadcasted_iota(jnp.int32, total.shape, 0)
-    total = jnp.where(row < 4, high, total - high)
-    out_ref[...] = jnp.concatenate(
-        [out.reshape(count, 8, LANES), jnp.broadcast_to(total[None], (count, 8, LANES))], 1
-    ).astype(bf16)
-
-
-def close_kernel(scale, x_ref, z_ref, pre_ref, weight_ref, fold_ref, out_ref, skip_ref):
-    every = x_ref[...].astype(f32)
-    count = every.shape[0]
-    rows = every[:, :8].reshape(count * 8, LANES)
-    quarter = rows.shape[0] // 4
-    group_of = lanes_of((quarter, LANES)) // (LANES // 4)
-    pieces = []
-    for place in range(4):
-        piece = jnp.zeros((quarter, LANES), f32)
-        for part in range(4):
-            source = rows[part * quarter : (part + 1) * quarter]
-            moved = pltpu.roll(source, (part - place) % 4 * (LANES // 4), 1)
-            piece = jnp.where(group_of == part, moved, piece)
-        pieces.append(piece)
-    cells = jnp.dot(
-        z_ref[...], jnp.concatenate(pieces, 0).astype(bf16), preferred_element_type=f32
-    )
+    out_ref[...] = (out * scale).astype(bf16)
+
+
+def close_kernel(scale, x_ref, z_ref, pre_ref, weight_ref, sum_ref, out_ref, skip_ref):
+    pieces = quarters(x_ref[...].astype(f32)).astype(bf16)
+    cells = jnp.dot(z_ref[...], pieces, preferred_element_type=f32)
     part = lax.dot_general(
         pre_ref[...], weight_ref[...], (((1,), (1,)), ((), ())), preferred_element_type=f32
     )
     out_ref[...] = (part + cells * scale).astype(bf16)
-    sums = every[:, 8:].reshape(count * 8, LANES).astype(bf16)
-    skip_ref[...] = jnp.dot(fold_ref[...], sums, preferred_element_type=f32)
+    skip_ref[...] = sum_ref[...].astype(f32)
 
 
 def one_hot(rows, columns):
@@ -279,10 +264,6 @@
     cas_z = plain_cas(s.z, s.z)
     norm = math.sqrt(s.x * s.gx * s.y * s.gy)
     t = {}
-    device, which, row = split_index(2 * s.channels, s.devices, 2, 4)
-    t["sums"] = one_hot(which * s.channels + device * 4 + row, np.arange(2 * s.channels))
-    device, which, row = split_index(2 * s.channels, s.devices, 2, 4)
-    t["fold"] = one_hot(np.arange(s.channels), device * 4 + row)
     count = s.devices * s.x * s.y // 2
     px, py, x, yh = split_index(count, s.gx, s.gy, s.x, s.y // 2)
     at_x = px * s.x + x
@@ -299,7 +280,7 @@
     t["z"] = same * cas_z[c[:, None], z[None, :]]
     t["z_scale"] = 1.0 / math.sqrt(s.z)
     b, c, a = split_index(s.cells, s.y, s.z, s.x)
-    t["back_cut"] = one_hot((a * s.y + b) * s.z + c, np.arange(s.cells))
+    t["z_turned"] = t["z"][(a * s.y + b) * s.z + c]
     count = s.devices * s.x
     px, py, x = split_index(count, s.gx, s.gy, s.x)
     at_x = px * s.x + x
@@ -378,51 +359,57 @@
     )(columns.reshape(rows, LANES), t["plane"])
     owned = exchange(planes.reshape(devices, -1, LANES))
     owned = owned.reshape(2, 2, cells // 2, LANES)
-    grad_modes, back = call(
+    back, sums = call(
         functools.partial(modes_kernel, t["z_scale"]),
-        (in_vmem(cells, channels, kind=f32), in_vmem(devices, 16, LANES)),
+        (in_vmem(cells, channels), in_vmem(channels, channels)),
         24,
         cells * channels * channels * 16,
         9 * MIB,
-        in_specs=[vmem] * 7,
+        in_specs=[vmem] * 5,
         out_specs=(vmem, vmem),
-        scratch_shapes=[pltpu.VMEM((cells, channels), f32)],
+        scratch_shapes=[pltpu.VMEM((cells, channels), f32), pltpu.VMEM((cells, channels), f32)],
     )(
         owned,
-        t["z"],
-        spectral_w.reshape(cells, channels, channels),
-        t["back_cut"],
+        t["z_turned"],
+        spectral_w.reshape(s.x, s.y * s.z, channels, channels),
         flat(inputs),
         grad_pre,
-        t["sums"],
-    )
-    back_columns = exchange(back)
+    )
+    pieces = lambda rows, sums: jnp.concatenate(
+        [rows.reshape(devices, 4, -1), sums.reshape(devices, 4, channels)], 2
+    )
+    split = lambda got: (
+        got[:, :, : 2 * LANES].reshape(cells, LANES),
+        got[:, :, 2 * LANES :],
+    )
+    back_columns, sums = split(exchange(pieces(back, sums)))
     grad_spectral, flag = call(
         functools.partial(outer_kernel, t["z_scale"]),
         (in_hbm(cells, channels, channels), in_vmem(8, LANES, kind=f32)),
         24,
         cells * channels * channels * 2,
         9 * MIB,
-        in_specs=[vmem] * 3,
+        in_specs=[vmem] * 2,
         out_specs=(hbm, vmem),
         scratch_shapes=[
+            pltpu.VMEM((cells, channels), f32),
             pltpu.VMEM((cells, channels), f32),
             pltpu.VMEM((cells, channels, channels), bf16),
             pltpu.SemaphoreType.DMA((cells // 16,)),
         ],
-    )(owned, t["z"], grad_modes)
+    )(owned, t["z"])
+    skip_rows = jnp.sum(sums.astype(f32), 0) * (1.0 / math.sqrt(cells * devices))
+    skip_rows = jnp.broadcast_to(skip_rows.astype(bf16), sums.shape)
     back_planes = call(
-        functools.partial(
-            back_plane_kernel, t["back_plane_scale"], 1.0 / math.sqrt(cells * devices)
-        ),
-        in_vmem(devices, 16, LANES),
+        functools.partial(back_plane_kernel, t["back_plane_scale"]),
+        in_vmem(back_rows, LANES),
         16,
         back_rows * back_rows * LANES * 32,
         4 * MIB,
         in_specs=[vmem, vmem, anywhere],
         out_specs=vmem,
     )(back_columns, t["back_plane"], flag)
-    spectral = exchange(back_planes)
+    spectral, sums = split(exchange(pieces(back_planes, skip_rows)))
     grad_inputs, grad_skip = call(
         functools.partial(close_kernel, t["z_scale"]),
         (in_hbm(cells, channels), in_hbm(channels, channels, kind=f32)),
@@ -431,7 +418,7 @@
         MIB,
         in_specs=[vmem] * 5,
         out_specs=(vmem, vmem),
-    )(spectral, t["back_z"], grad_pre, skip_w, t["fold"])
+    )(spectral, t["back_z"], grad_pre, skip_w, sums.reshape(channels, channels))
     return (
         grad_inputs.reshape(inputs.shape),
         grad_spectral.reshape(spectral_w.shape),

time: 54.8 us -> 53.9 us (0.984)
  Pallas kernels: 11.9 us -> 10.4 us
  other arithmetic: 0 us -> 0.78 us
    pallas_call x1, Pallas kernels: 3.84 us -> 2.27 us  [on_device_whole_planes(): call(functools.partial(modes_kernel, t['z_scale']), (in_vmem(cells, chann...]
    concatenate x0 -> x2, other arithmetic: none -> 0.73 us  [on_device_whole_planes(): jnp.concatenate([rows.reshape(devices, 4, -1), sums.reshape(devices, 4, c...]
where the time goes in v3:
time: 53.9 us; the launch traced here: 53.7 us
  blocking collectives  35.4 us (66%)
  Pallas kernels  10.4 us (19%)
  waiting for transfers between devices  3.48 us (6%)
  starting transfers between devices  2.55 us (5%)
  between operations  0.81 us (2%)
  other arithmetic  0.78 us (1%)
    all_to_all x3, blocking collectives, exchange(): return lax.all_to_all(pieces, ('gx', 'gy'), 0, 0)  35.4 us
    pallas_call x1, Pallas kernels, on_device_whole_planes(): call(functools.partial(outer_kernel, t['z_scale']), (in_hbm(cells, channe...  4.28 us
    all_to_all x1, waiting for transfers between devices, exchange(): return lax.all_to_all(pieces, ('gx', 'gy'), 0, 0)  3.48 us
    all_to_all x1, starting transfers between devices, exchange(): return lax.all_to_all(pieces, ('gx', 'gy'), 0, 0)  2.55 us
    pallas_call x1, Pallas kernels, on_device_whole_planes(): call(functools.partial(modes_kernel, t['z_scale']), (in_vmem(cells, chann...  2.27 us
    pallas_call x1, Pallas kernels, on_device_whole_planes(): call(functools.partial(open_kernel, s), (in_vmem(2, 2, cells // 2, LANES)...  1.38 us
  transfers between devices with their start and end apart: 1, of which 1 were waited for; matrix products, arithmetic and copies ran while one was open for 0% of the time, Pallas kernels for 8%

profile of v3, /device:TPU:0, one launch (start us, length us, event | category | flops | bytes accessed | tf_op | source)
XLA Modules:
  0.0 53.7 jit_solution(12589474782406563430)
XLA Ops:
  0.6 0.0 copy-start.7
  0.6 1.4 %shard_map.121 = (bf16[2,2,128,128]{3,2,1,0:T(8,128)(2,1)S(1)}, bf16[256,128]{1,0:T(8,128)(2,1)S(1)}) custom-call(bf16[256,128]{1,0:T(8,128)(2,1)} %bitcast.19, bf16[256,128]{1,0:T(8,128)(2,1)} %bitcast.23, bf16[256,128]{1,0:T(8,128)(2,1)} %bitcast.24), custom_call_target="tpu_custom_call" | custom-call | flops 1099511627776 | bytes 1048576 | tf_op jit(solution)/shard_map/pallas_call | solution.py:340
  2.0 15.3 %all_to_all.20 = bf16[32,16,128]{2,1,0:T(8,128)(2,1)S(1)} all-to-all(bf16[32,16,128]{2,1,0:T(8,128)(2,1)S(1)} %bitcast.16), channel_id=1, replica_groups=mesh['gx'=4,'gy'=8] {'gx','gy'}, dimensions={0} | all-to-all | bytes 262144 | tf_op jit(solution)/shard_map/all_to_all | solution.py:327
  17.3 0.0 copy-done.7
  17.3 0.8 %shard_map.122 = bf16[512,128]{1,0:T(8,128)(2,1)S(1)} custom-call(bf16[512,128]{1,0:T(8,128)(2,1)S(1)} %bitcast.17, bf16[2048,512]{1,0:T(8,128)(2,1)S(1)} %copy-done.7), custom_call_target="tpu_custom_call" | custom-call | flops 68719476736 | bytes 4194304 | tf_op jit(solution)/shard_map/pallas_call | solution.py:351
  18.1 0.0 copy-start.4
  18.1 0.0 copy-start.1
  18.1 0.0 copy-start.3
  18.1 0.0 copy-start.6
  18.2 10.1 %all_to_all.21 = bf16[32,16,128]{2,1,0:T(8,128)(2,1)S(1)} all-to-all(bf16[32,16,128]{2,1,0:T(8,128)(2,1)S(1)} %bitcast.18), channel_id=1, replica_groups=mesh['gx'=4,'gy'=8] {'gx','gy'}, dimensions={0} | all-to-all | bytes 262144 | tf_op jit(solution)/shard_map/all_to_all | solution.py:327
  28.3 0.0 copy-done
  28.3 0.0 copy-done.2
  28.3 0.0 copy-done.5
  28.3 2.3 %shard_map.123 = (bf16[256,128]{1,0:T(8,128)(2,1)S(1)}, bf16[128,128]{1,0:T(8,128)(2,1)S(1)}) custom-call(bf16[2,2,128,128]{3,2,1,0:T(8,128)(2,1)S(1)} %bitcast.13, bf16[256,256]{1,0:T(8,128)(2,1)S(1)} %copy-done.2, bf16[8,32,128,128]{3,2,1,0:T(8,128)(2,1)S(1)} %bitcast.12, bf16[256,128]{1,0:T(8,128)(2,1)S(1)} %bitcast.20, ...), custom_call_target="tpu_custom_call" | custom-call | flops 67108864 | bytes 9437184 | tf_op jit(solution)/shard_map/pallas_call | solution.py:362
  30.6 0.7 %pad_maximum_fusion = bf16[32,4,384]{2,1,0:T(4,128)(2,1)} fusion(bf16[32,4,128]{2,1,0:T(4,128)(2,1)S(1)} %bitcast.21, bf16[32,4,256]{2,1,0:T(4,128)(2,1)S(1)} %reshape.63), kind=kLoop, calls=%fused_computation | loop fusion | flops 196608 | bytes 196608 | tf_op jit(solution)/shard_map/concatenate | solution.py:378
  31.3 2.6 %all-to-all-start.2 = ((bf16[32,4,384]{2,1,0:T(4,128)(2,1)}), bf16[32,4,384]{2,1,0:T(4,128)(2,1)S(1)}, u32[]{:S(2)}, u32[]{:S(2)}) async-start(bf16[32,4,384]{2,1,0:T(4,128)(2,1)} %pad_maximum_fusion), calls=%async_computation.2 | async-start | bytes 196608 | tf_op jit(solution)/shard_map/all_to_all | solution.py:327
  33.9 0.0 copy-done.4
  33.9 4.3 %shard_map.124 = (bf16[256,128,128]{2,1,0:T(8,128)(2,1)}, f32[8,128]{1,0:T(8,128)S(1)}) custom-call(bf16[2,2,128,128]{3,2,1,0:T(8,128)(2,1)S(1)} %bitcast.14, bf16[256,256]{1,0:T(8,128)(2,1)S(1)} %copy-done.4), custom_call_target="tpu_custom_call" | custom-call | flops 8388608 | bytes 9437184 | tf_op jit(solution)/shard_map/pallas_call | solution.py:386
  38.2 3.5 %all-to-all-done.2 = bf16[32,4,384]{2,1,0:T(4,128)(2,1)S(1)} async-done(((bf16[32,4,384]{2,1,0:T(4,128)(2,1)}), bf16[32,4,384]{2,1,0:T(4,128)(2,1)S(1)}, u32[]{:S(2)}, u32[]{:S(2)}) %all-to-all-start.2) | async-done | bytes 98336 | tf_op jit(solution)/shard_map/all_to_all | solution.py:327
  41.8 0.0 copy-done.1
  41.8 0.8 %shard_map.125 = bf16[256,128]{1,0:T(8,128)(2,1)S(1)} custom-call(bf16[256,128]{1,0:T(8,128)(2,1)S(1)} %reshape.65.x_ref, bf16[1024,1024]{1,0:T(8,128)(2,1)S(1)} %copy-done.1, f32[8,128]{1,0:T(8,128)S(1)} %get-tuple-element.15.after), custom_call_target="tpu_custom_call" | custom-call | flops 268435456 | bytes 4194304 | tf_op jit(solution)/shard_map/pallas_call | solution.py:403
  42.7 9.9 %all_to_all.22 = bf16[32,4,384]{2,1,0:T(4,128)(2,1)S(1)} all-to-all(bf16[32,4,384]{2,1,0:T(4,128)(2,1)S(1)} %pad_maximum_fusion.1), channel_id=1, replica_groups=mesh['gx'=4,'gy'=8] {'gx','gy'}, dimensions={0} | all-to-all | bytes 196608 | tf_op jit(solution)/shard_map/all_to_all | solution.py:327
  52.7 0.0 copy-done.3
  52.7 0.9 %shard_map.126 = (bf16[256,128]{1,0:T(8,128)(2,1)}, f32[128,128]{1,0:T(8,128)}) custom-call(bf16[256,128]{1,0:T(8,128)(2,1)S(1)} %reshape.67.x_ref, bf16[256,256]{1,0:T(8,128)(2,1)S(1)} %copy-done.3, bf16[256,128]{1,0:T(8,128)(2,1)S(1)} %get-tuple-element.12.pre_ref, bf16[128,128]{1,0:T(8,128)(2,1)S(1)} %copy-done.6, bf16[128,128]{1,0:T(8,128)(2,1)S(1)} %bitcast.15), custom_call_target="tpu_custom_call" | custom-call | flops 33554432 | bytes 1048576 | tf_op jit(solution)/shard_map/pallas_call | solution.py:413
  (15 shorter events, 0.3 us)
Async XLA Ops:
  0.6 16.7 %copy-start.7 = (bf16[2048,512]{1,0:T(8,128)(2,1)S(1)}, bf16[2048,512]{1,0:T(8,128)(2,1)}, u32[]{:S(2)}) copy-start(bf16[2048,512]{1,0:T(8,128)(2,1)} %constant.14.clone.table_ref) | copy-start | bytes 6291460
  17.3 11.0 %copy-start = (bf16[8,4,8,128,128]{4,3,2,1,0:T(8,128)(2,1)S(1)}, bf16[8,4,8,128,128]{4,3,2,1,0:T(8,128)(2,1)}, u32[]{:S(2)}) copy-start(bf16[8,4,8,128,128]{4,3,2,1,0:T(8,128)(2,1)} %param.13) | copy-start | bytes 25165828
  17.3 11.0 %copy-start.2 = (bf16[256,256]{1,0:T(8,128)(2,1)S(1)}, bf16[256,256]{1,0:T(8,128)(2,1)}, u32[]{:S(2)}) copy-start(bf16[256,256]{1,0:T(8,128)(2,1)} %constant.16.clone.z_ref) | copy-start | bytes 393220
  17.3 11.0 %copy-start.5 = (bf16[8,4,8,128]{3,2,1,0:T(8,128)(2,1)S(1)}, bf16[8,4,8,128]{3,2,1,0:T(8,128)(2,1)}, u32[]{:S(2)}) copy-start(bf16[8,4,8,128]{3,2,1,0:T(8,128)(2,1)} %param.10) | copy-start | bytes 196612
  18.1 15.8 %copy-start.4 = (bf16[256,256]{1,0:T(8,128)(2,1)S(1)}, bf16[256,256]{1,0:T(8,128)(2,1)}, u32[]{:S(2)}) copy-start(bf16[256,256]{1,0:T(8,128)(2,1)} %constant.15.clone.z_ref) | copy-start | bytes 393220
  18.1 23.7 %copy-start.1 = (bf16[1024,1024]{1,0:T(8,128)(2,1)S(1)}, bf16[1024,1024]{1,0:T(8,128)(2,1)}, u32[]{:S(2)}) copy-start(bf16[1024,1024]{1,0:T(8,128)(2,1)} %constant.17.clone.table_ref) | copy-start | bytes 6291460
  18.1 34.6 %copy-start.3 = (bf16[256,256]{1,0:T(8,128)(2,1)S(1)}, bf16[256,256]{1,0:T(8,128)(2,1)}, u32[]{:S(2)}) copy-start(bf16[256,256]{1,0:T(8,128)(2,1)} %constant.18.clone.z_ref) | copy-start | bytes 393220
  18.1 34.6 %copy-start.6 = (bf16[128,128]{1,0:T(8,128)(2,1)S(1)}, bf16[128,128]{1,0:T(8,128)(2,1)}, u32[]{:S(2)}) copy-start(bf16[128,128]{1,0:T(8,128)(2,1)} %weight_ref.1) | copy-start | bytes 98308
  31.3 10.3 %all-to-all-start.2 = ((bf16[32,4,384]{2,1,0:T(4,128)(2,1)}), bf16[32,4,384]{2,1,0:T(4,128)(2,1)S(1)}, u32[]{:S(2)}, u32[]{:S(2)}) async-start(bf16[32,4,384]{2,1,0:T(4,128)(2,1)} %pad_maximum_fusion), calls=%async_computation.2 | async-start | bytes 196608 | tf_op jit(solution)/shard_map/all_to_all | solution.py:327

commit v4 on v3

--- a/solution.py
+++ b/solution.py
@@ -92,7 +92,7 @@
     half = cells // 2
     yl, rest = place // half, place % half
     z, rest = rest // (s.x * half_y), rest % (s.x * half_y)
-    x, yh = rest // half_y, rest % half_y
+    yh, x = rest // s.x, rest % s.x
     source = (x * s.y + yh * 2 + yl) * s.z + z
     order = (lax.broadcasted_iota(jnp.int32, (cells, cells), 1) == source).astype(f32).astype(bf16)
     for copy in copies:
@@ -111,13 +111,39 @@
         pack_ref[field, 1] = jnp.where(low, pltpu.roll(even, width, 1), odd).astype(bf16)
 
 
-def plane_kernel(scale, x_ref, table_ref, out_ref):
-    rows, width = x_ref.shape[0], LANES // 2
-    made = jnp.dot(table_ref[...], x_ref[...], preferred_element_type=f32)
+def first_axis(tiles, table_ref, along, across):
+    lines = [tiles[:, j].reshape(along * 8, LANES) for j in range(across)]
+    lines = jnp.concatenate(lines, 1).astype(bf16)
+    made = jnp.dot(
+        table_ref[...], jnp.concatenate([lines, lines], 0), preferred_element_type=f32
+    )
+    return [
+        jnp.concatenate(
+            [made[i * 8 : i * 8 + 8, j * LANES : (j + 1) * LANES] for j in range(across)], 0
+        )
+        for i in range(along)
+    ]
+
+
+def plane_kernel(s, scale, x_ref, first_ref, second_ref, out_ref):
+    width = LANES // 2
+    across = s.gy * s.y // 2
+    tiles = x_ref[...].astype(f32).reshape(s.gx, across, 8, LANES)
+    parts = jnp.concatenate(first_axis(tiles, first_ref, s.gx, across), 1)
+    rows = across * 8
+    table = second_ref[...]
+    made = jnp.dot(
+        jnp.concatenate([table, table], 1),
+        jnp.concatenate(split_twice(parts), 0),
+        preferred_element_type=f32,
+    )
     low = lanes_of((rows, LANES)) < width
-    straight = jnp.where(low, made[:rows], made[rows : 2 * rows])
-    crossed = jnp.where(low, made[2 * rows : 3 * rows], made[3 * rows :])
-    out_ref[...] = ((straight + pltpu.roll(crossed, width, 1)) * scale).astype(bf16)
+    for part in range(s.gx):
+        here = made[:, part * LANES : (part + 1) * LANES]
+        straight = jnp.where(low, here[:rows], here[rows : 2 * rows])
+        crossed = jnp.where(low, here[2 * rows : 3 * rows], here[3 * rows :])
+        value = (straight + pltpu.roll(crossed, width, 1)) * scale
+        out_ref[part * rows : (part + 1) * rows, :] = value.astype(bf16)
 
 
 def field_modes(scale, first, second, z_ref):
@@ -194,19 +220,20 @@
     pack_ref[...] = quarters(rows).astype(bf16)
 
 
-def outer_kernel(scale, x_ref, z_ref, out_hbm, flag_ref, in_ref, grad_ref, made, sems):
+def outer_kernel(scale, x_ref, z_ref, grad_ref, after, out_hbm, in_ref, made, sems):
     in_ref[...] = field_modes(scale, x_ref[0, 0], x_ref[0, 1], z_ref)
-    grad_ref[...] = field_modes(scale, x_ref[1, 0], x_ref[1, 1], z_ref)
-    flag_ref[...] = jnp.zeros(flag_ref.shape, f32)
-    modes = in_ref.shape[0]
-    size, unrolled = 16, 4
+    del after
+    lines, columns = made.shape[:2]
+    across = 2
+    size, unrolled = across * lines, 4
+    groups = columns // across
     row = lax.broadcasted_iota(jnp.int32, (3 * size, LANES), 0) % size
 
     def copy(group):
-        part = pl.ds(group * size, size)
-        return pltpu.make_async_copy(made.at[part], out_hbm.at[part], sems.at[group])
-
-    @pl.loop(0, modes // size // unrolled)
+        part = pl.ds(group * across, across)
+        return pltpu.make_async_copy(made.at[:, part], out_hbm.at[:, part], sems.at[group])
+
+    @pl.loop(0, groups // unrolled)
     def _(turn):
         for at in range(unrolled):
             group = turn * unrolled + at
@@ -221,27 +248,41 @@
                 left, right, (((0,), (0,)), ((), ())), preferred_element_type=f32
             )
             for mode in range(size):
-                made[group * size + mode] = every[:, mode * LANES : (mode + 1) * LANES].astype(bf16)
+                part = every[:, mode * LANES : (mode + 1) * LANES].astype(bf16)
+                made[mode % lines, group * across + mode // lines] = part
             copy(group).start()
 
-    @pl.loop(0, modes // size)
+    @pl.loop(0, groups)
     def _(group):
         copy(group).wait()
 
 
-def back_plane_kernel(scale, x_ref, table_ref, after, out_ref):
-    del after
-    x = x_ref[...].astype(f32)
-    rows = x.shape[0]
-    turned = [x if s == 0 else pltpu.roll(x, s * (LANES // 4), 1) for s in range(4)]
+def back_plane_kernel(s, scale, x_ref, first_ref, second_ref, out_ref):
+    tiles = x_ref[...].astype(f32).reshape(s.gx, s.gy, 8, LANES)
+    parts = jnp.concatenate(first_axis(tiles, first_ref, s.gx, s.gy), 1)
+    rows, across = parts.shape
+    wide = across // LANES
+    turned = [parts]
+    for turn in range(1, 4):
+        moved = [
+            pltpu.roll(parts[:, i * LANES : (i + 1) * LANES], turn * (LANES // 4), 1)
+            for i in range(wide)
+        ]
+        turned.append(jnp.concatenate(moved, 1))
+    high, low = split_twice(jnp.concatenate(turned, 0))
+    table = second_ref[...]
     made = jnp.dot(
-        table_ref[...], jnp.concatenate(turned, 0).astype(bf16), preferred_element_type=f32
+        jnp.concatenate([table, table], 1),
+        jnp.concatenate([high, low], 0),
+        preferred_element_type=f32,
     )
     group_of = lanes_of((rows, LANES)) // (LANES // 4)
-    out = made[:rows]
-    for place in range(1, 4):
-        out = jnp.where(group_of == place, made[place * rows : (place + 1) * rows], out)
-    out_ref[...] = (out * scale).astype(bf16)
+    for part in range(wide):
+        here = made[:, part * LANES : (part + 1) * LANES]
+        value = here[:rows]
+        for place in range(1, 4):
+            value = jnp.where(group_of == place, here[place * rows : (place + 1) * rows], value)
+        out_ref[part * rows : (part + 1) * rows, :] = (value * scale).astype(bf16)
 
 
 def close_kernel(scale, x_ref, z_ref, pre_ref, weight_ref, sum_ref, out_ref, skip_ref):
@@ -256,6 +297,12 @@
 
 def one_hot(rows, columns):
     return (np.asarray(rows)[:, None] == np.asarray(columns)[None, :]).astype(np.float32)
+
+
+def twice(table):
+    high = table.astype(np.float32).astype(bf16)
+    low = (table - high.astype(np.float64)).astype(np.float32).astype(bf16)
+    return np.concatenate([high, low], 1)
 
 
 def make_tables(s):
@@ -264,36 +311,32 @@
     cas_z = plain_cas(s.z, s.z)
     norm = math.sqrt(s.x * s.gx * s.y * s.gy)
     t = {}
-    count = s.devices * s.x * s.y // 2
-    px, py, x, yh = split_index(count, s.gx, s.gy, s.x, s.y // 2)
-    at_x = px * s.x + x
-    blocks = []
-    for b, y in ((0, 0), (1, 1), (1, 0), (0, 1)):
-        at_b = py * s.y + yh * 2 + b
-        at_y = py * s.y + yh * 2 + y
-        blocks.append(cas_x[at_x[:, None], at_x[None, :]] * cas_y[at_b[:, None], at_y[None, :]])
-    t["plane"], factor = rounded_table(np.concatenate(blocks, 0))
-    t["plane_scale"] = factor / norm
-    a, b, c = split_index(s.cells, s.x, s.y, s.z)
-    bl, z, al, bh = split_index(s.cells, 2, s.z, s.x, s.y // 2)
+    t["first"] = twice(cas_x)
+    t["back_first"] = twice(cas_x.T)
+    count = s.gy * s.y // 2 * s.x
+    py, yh, x = split_index(count, s.gy, s.y // 2, s.x)
+    at = py * s.y + yh * 2
+    same = one_hot(x, x)
+    blocks = [cas_y[(at + b)[:, None], (at + y)[None, :]] * same for b, y in ((0, 0), (1, 1), (1, 0), (0, 1))]
+    t["second"], factor = rounded_table(np.concatenate(blocks, 0))
+    t["scale"] = factor / norm
+    b, c, a = split_index(s.cells, s.y, s.z, s.x)
+    bl, z, bh, al = split_index(s.cells, 2, s.z, s.y // 2, s.x)
     same = one_hot(a * s.y + b, al * s.y + bh * 2 + bl)
     t["z"] = same * cas_z[c[:, None], z[None, :]]
     t["z_scale"] = 1.0 / math.sqrt(s.z)
-    b, c, a = split_index(s.cells, s.y, s.z, s.x)
-    t["z_turned"] = t["z"][(a * s.y + b) * s.z + c]
-    count = s.devices * s.x
-    px, py, x = split_index(count, s.gx, s.gy, s.x)
-    at_x = px * s.x + x
+    py, x = split_index(s.gy * s.x, s.gy, s.x)
+    same = one_hot(x, x)
     blocks = []
     for place in range(4):
         line = []
         for turn in range(4):
             at_y = py * s.y + place
             at_b = py * s.y + (place - turn) % 4
-            line.append(cas_x[at_x[None, :], at_x[:, None]] * cas_y[at_b[None, :], at_y[:, None]])
+            line.append(cas_y[at_b[None, :], at_y[:, None]] * same)
         blocks.append(np.concatenate(line, 1))
-    t["back_plane"], factor = rounded_table(np.concatenate(blocks, 0))
-    t["back_plane_scale"] = factor / norm
+    t["back_second"], factor = rounded_table(np.concatenate(blocks, 0))
+    t["back_scale"] = factor / norm
     x, y, z = split_index(s.cells, s.x, s.y, s.z)
     yl, c, xl = split_index(s.cells, s.y, s.z, s.x)
     t["back_z"] = one_hot(x * s.y + y, xl * s.y + yl) * cas_z[c[None, :], z[:, None]]
@@ -349,28 +392,32 @@
     )(*(pltpu.with_memory_space_constraint(flat(a), pltpu.HBM) for a in (inputs, preact, cotangent)))
     columns = exchange(pieces.reshape(devices, -1, LANES))
     planes = call(
-        functools.partial(plane_kernel, t["plane_scale"]),
+        functools.partial(plane_kernel, s, t["scale"]),
         in_vmem(rows, LANES),
         16,
         1 << 36,
-        4 * MIB,
-        in_specs=[vmem, vmem],
+        MIB,
+        in_specs=[vmem] * 3,
         out_specs=vmem,
-    )(columns.reshape(rows, LANES), t["plane"])
+    )(columns.reshape(rows, LANES), t["first"], t["second"])
     owned = exchange(planes.reshape(devices, -1, LANES))
     owned = owned.reshape(2, 2, cells // 2, LANES)
-    back, sums = call(
+    back, sums, grad_modes = call(
         functools.partial(modes_kernel, t["z_scale"]),
-        (in_vmem(cells, channels), in_vmem(channels, channels)),
+        (
+            in_vmem(cells, channels),
+            in_vmem(channels, channels),
+            in_vmem(cells, channels, kind=f32),
+        ),
         24,
         cells * channels * channels * 16,
         9 * MIB,
         in_specs=[vmem] * 5,
-        out_specs=(vmem, vmem),
-        scratch_shapes=[pltpu.VMEM((cells, channels), f32), pltpu.VMEM((cells, channels), f32)],
+        out_specs=(vmem, vmem, vmem),
+        scratch_shapes=[pltpu.VMEM((cells, channels), f32)],
     )(
         owned,
-        t["z_turned"],
+        t["z"],
         spectral_w.reshape(s.x, s.y * s.z, channels, channels),
         flat(inputs),
         grad_pre,
@@ -383,32 +430,32 @@
         got[:, :, 2 * LANES :],
     )
     back_columns, sums = split(exchange(pieces(back, sums)))
-    grad_spectral, flag = call(
+    skip_rows = jnp.sum(sums.astype(f32), 0) * (1.0 / math.sqrt(cells * devices))
+    skip_rows = jnp.broadcast_to(skip_rows.astype(bf16), sums.shape)
+    back_planes = call(
+        functools.partial(back_plane_kernel, s, t["back_scale"]),
+        in_vmem(back_rows, LANES),
+        16,
+        back_rows * back_rows * LANES * 8,
+        MIB,
+        in_specs=[vmem] * 3,
+        out_specs=vmem,
+    )(back_columns, t["back_first"], t["back_second"])
+    split_modes = (s.x, s.y * s.z, channels, channels)
+    grad_spectral = call(
         functools.partial(outer_kernel, t["z_scale"]),
-        (in_hbm(cells, channels, channels), in_vmem(8, LANES, kind=f32)),
+        in_hbm(*split_modes),
         24,
         cells * channels * channels * 2,
         9 * MIB,
-        in_specs=[vmem] * 2,
-        out_specs=(hbm, vmem),
+        in_specs=[vmem] * 3 + [anywhere],
+        out_specs=hbm,
         scratch_shapes=[
             pltpu.VMEM((cells, channels), f32),
-            pltpu.VMEM((cells, channels), f32),
-            pltpu.VMEM((cells, channels, channels), bf16),
-            pltpu.SemaphoreType.DMA((cells // 16,)),
+            pltpu.VMEM(split_modes, bf16),
+            pltpu.SemaphoreType.DMA((s.y * s.z // 2,)),
         ],
-    )(owned, t["z"])
-    skip_rows = jnp.sum(sums.astype(f32), 0) * (1.0 / math.sqrt(cells * devices))
-    skip_rows = jnp.broadcast_to(skip_rows.astype(bf16), sums.shape)
-    back_planes = call(
-        functools.partial(back_plane_kernel, t["back_plane_scale"]),
-        in_vmem(back_rows, LANES),
-        16,
-        back_rows * back_rows * LANES * 32,
-        4 * MIB,
-        in_specs=[vmem, vmem, anywhere],
-        out_specs=vmem,
-    )(back_columns, t["back_plane"], flag)
+    )(owned, t["z"], grad_modes, back_planes)
     spectral, sums = split(exchange(pieces(back_planes, skip_rows)))
     grad_inputs, grad_skip = call(
         functools.partial(close_kernel, t["z_scale"]),

time: 53.9 us -> 52.9 us (0.981)
  Pallas kernels: 10.4 us -> 9.81 us
where the time goes in v4:
time: 52.9 us; the launch traced here: 52.7 us
  blocking collectives  34.9 us (66%)
  Pallas kernels  9.81 us (19%)
  waiting for transfers between devices  3.56 us (7%)
  starting transfers between devices  2.57 us (5%)
  between operations  0.82 us (2%)
  other arithmetic  0.78 us (1%)
    all_to_all x3, blocking collectives, exchange(): return lax.all_to_all(pieces, ('gx', 'gy'), 0, 0)  34.9 us
    pallas_call x1, Pallas kernels, on_device_whole_planes(): call(functools.partial(outer_kernel, t['z_scale']), in_hbm(*split_modes),...  4.21 us
    all_to_all x1, waiting for transfers between devices, exchange(): return lax.all_to_all(pieces, ('gx', 'gy'), 0, 0)  3.56 us
    all_to_all x1, starting transfers between devices, exchange(): return lax.all_to_all(pieces, ('gx', 'gy'), 0, 0)  2.57 us
    pallas_call x1, Pallas kernels, on_device_whole_planes(): call(functools.partial(modes_kernel, t['z_scale']), (in_vmem(cells, chann...  2.27 us
    pallas_call x1, Pallas kernels, on_device_whole_planes(): call(functools.partial(open_kernel, s), (in_vmem(2, 2, cells // 2, LANES)...  1.27 us
  transfers between devices with their start and end apart: 1, of which 1 were waited for; matrix products, arithmetic and copies ran while one was open for 0% of the time, Pallas kernels for 8%

profile of v4, /device:TPU:0, one launch (start us, length us, event | category | flops | bytes accessed | tf_op | source)
XLA Modules:
  0.0 52.7 jit_solution(3024515175282809872)
XLA Ops:
  0.6 0.0 copy-start.6
  0.6 0.0 copy-start.7
  0.7 1.3 %shard_map.130 = (bf16[2,2,128,128]{3,2,1,0:T(8,128)(2,1)S(1)}, bf16[256,128]{1,0:T(8,128)(2,1)S(1)}) custom-call(bf16[256,128]{1,0:T(8,128)(2,1)} %bitcast.19, bf16[256,128]{1,0:T(8,128)(2,1)} %bitcast.23, bf16[256,128]{1,0:T(8,128)(2,1)} %bitcast.24), custom_call_target="tpu_custom_call" | custom-call | flops 1099511627776 | bytes 1048576 | tf_op jit(solution)/shard_map/pallas_call | solution.py:383
  1.9 15.3 %all_to_all.20 = bf16[32,16,128]{2,1,0:T(8,128)(2,1)S(1)} all-to-all(bf16[32,16,128]{2,1,0:T(8,128)(2,1)S(1)} %bitcast.16), channel_id=1, replica_groups=mesh['gx'=4,'gy'=8] {'gx','gy'}, dimensions={0} | all-to-all | bytes 262144 | tf_op jit(solution)/shard_map/all_to_all | solution.py:370
  17.2 0.0 copy-done.6
  17.2 0.0 copy-done.7
  17.2 0.0 copy-start.4
  17.2 0.5 %shard_map.131 = bf16[512,128]{1,0:T(8,128)(2,1)S(1)} custom-call(bf16[512,128]{1,0:T(8,128)(2,1)S(1)} %bitcast.17, bf16[32,64]{1,0:T(8,128)(2,1)S(1)} %copy-done.6, bf16[512,128]{1,0:T(8,128)(2,1)S(1)} %copy-done.7), custom_call_target="tpu_custom_call" | custom-call | flops 68719476736 | bytes 1048576 | tf_op jit(solution)/shard_map/pallas_call | solution.py:394
  17.8 0.0 copy-start.3
  17.8 10.1 %all_to_all.21 = bf16[32,16,128]{2,1,0:T(8,128)(2,1)S(1)} all-to-all(bf16[32,16,128]{2,1,0:T(8,128)(2,1)S(1)} %bitcast.18), channel_id=1, replica_groups=mesh['gx'=4,'gy'=8] {'gx','gy'}, dimensions={0} | all-to-all | bytes 262144 | tf_op jit(solution)/shard_map/all_to_all | solution.py:370
  27.9 0.0 copy-done
  28.0 0.0 copy-done.1
  28.0 0.0 copy-done.4
  28.0 0.0 copy-start.2
  28.0 0.0 copy-start.5
  28.0 2.3 %shard_map.132 = (bf16[256,128]{1,0:T(8,128)(2,1)S(1)}, bf16[128,128]{1,0:T(8,128)(2,1)S(1)}, f32[256,128]{1,0:T(8,128)S(1)}) custom-call(bf16[2,2,128,128]{3,2,1,0:T(8,128)(2,1)S(1)} %bitcast.13, bf16[256,256]{1,0:T(8,128)(2,1)S(1)} %copy-done.1, bf16[8,32,128,128]{3,2,1,0:T(8,128)(2,1)S(1)} %bitcast.12, bf16[256,128]{1,0:T(8,128)(2,1)S(1)} %bitcast.20, ...), custom_call_target="tpu_custom_call" | custom-call | flops 67108864 | bytes 9437184 | tf_op jit(solution)/shard_map/pallas_call | solution.py:405
  30.4 9.5 %all_to_all.22 = bf16[32,4,384]{2,1,0:T(4,128)(2,1)S(1)} all-to-all(bf16[32,4,384]{2,1,0:T(4,128)(2,1)S(1)} %pad_maximum_fusion), channel_id=1, replica_groups=mesh['gx'=4,'gy'=8] {'gx','gy'}, dimensions={0} | all-to-all | bytes 196608 | tf_op jit(solution)/shard_map/all_to_all | solution.py:370
  40.0 0.0 copy-done.3
  40.0 0.6 %shard_map.133.after = bf16[256,128]{1,0:T(8,128)(2,1)S(1)} custom-call(bf16[256,128]{1,0:T(8,128)(2,1)S(1)} %reshape.65.x_ref, bf16[32,64]{1,0:T(8,128)(2,1)S(1)} %copy-done.6, bf16[256,256]{1,0:T(8,128)(2,1)S(1)} %copy-done.3), custom_call_target="tpu_custom_call" | custom-call | flops 67108864 | bytes 1048576 | tf_op jit(solution)/shard_map/pallas_call | solution.py:435
  40.6 0.7 %pad_maximum_fusion.1 = bf16[32,4,384]{2,1,0:T(4,128)(2,1)} fusion(bf16[32,4,128]{2,1,0:T(4,128)(2,1)S(1)} %broadcast_in_dim.3, bf16[32,4,256]{2,1,0:T(4,128)(2,1)S(1)} %reshape.66), kind=kLoop, calls=%fused_computation.1 | loop fusion | flops 196608 | bytes 196608 | tf_op jit(solution)/shard_map/concatenate | solution.py:425
  41.3 2.6 %all-to-all-start.3 = ((bf16[32,4,384]{2,1,0:T(4,128)(2,1)}), bf16[32,4,384]{2,1,0:T(4,128)(2,1)S(1)}, u32[]{:S(2)}, u32[]{:S(2)}) async-start(bf16[32,4,384]{2,1,0:T(4,128)(2,1)} %pad_maximum_fusion.1), calls=%async_computation.3 | async-start | bytes 196608 | tf_op jit(solution)/shard_map/all_to_all | solution.py:370
  43.9 4.2 %shard_map.135 = bf16[8,32,128,128]{3,2,1,0:T(8,128)(2,1)} custom-call(bf16[2,2,128,128]{3,2,1,0:T(8,128)(2,1)S(1)} %bitcast.14, bf16[256,256]{1,0:T(8,128)(2,1)S(1)} %copy-done.1, f32[256,128]{1,0:T(8,128)S(1)} %get-tuple-element.15.grad_ref, bf16[256,128]{1,0:T(8,128)(2,1)S(1)} %shard_map.133.after), custom_call_target="tpu_custom_call" | custom-call | flops 8388608 | bytes 9437184 | tf_op jit(solution)/shard_map/pallas_call | solution.py:445
  48.1 3.6 %all-to-all-done.3 = bf16[32,4,384]{2,1,0:T(4,128)(2,1)S(1)} async-done(((bf16[32,4,384]{2,1,0:T(4,128)(2,1)}), bf16[32,4,384]{2,1,0:T(4,128)(2,1)S(1)}, u32[]{:S(2)}, u32[]{:S(2)}) %all-to-all-start.3) | async-done | bytes 98336 | tf_op jit(solution)/shard_map/all_to_all | solution.py:370
  51.8 0.9 %shard_map.134 = (bf16[256,128]{1,0:T(8,128)(2,1)}, f32[128,128]{1,0:T(8,128)}) custom-call(bf16[256,128]{1,0:T(8,128)(2,1)S(1)} %reshape.67.x_ref, bf16[256,256]{1,0:T(8,128)(2,1)S(1)} %copy-done.2, bf16[256,128]{1,0:T(8,128)(2,1)S(1)} %get-tuple-element.11.pre_ref, bf16[128,128]{1,0:T(8,128)(2,1)S(1)} %copy-done.5, bf16[128,128]{1,0:T(8,128)(2,1)S(1)} %bitcast.15), custom_call_target="tpu_custom_call" | custom-call | flops 33554432 | bytes 1048576 | tf_op jit(solution)/shard_map/pallas_call | solution.py:460
  (15 shorter events, 0.3 us)
Async XLA Ops:
  0.6 16.6 %copy-start.6 = (bf16[32,64]{1,0:T(8,128)(2,1)S(1)}, bf16[32,64]{1,0:T(8,128)(2,1)}, u32[]{:S(2)}) copy-start(bf16[32,64]{1,0:T(8,128)(2,1)} %constant.14.clone.first_ref) | copy-start | bytes 12292
  0.6 16.6 %copy-start.7 = (bf16[512,128]{1,0:T(8,128)(2,1)S(1)}, bf16[512,128]{1,0:T(8,128)(2,1)}, u32[]{:S(2)}) copy-start(bf16[512,128]{1,0:T(8,128)(2,1)} %constant.15.clone.second_ref) | copy-start | bytes 393220
  17.2 10.7 %copy-start = (bf16[8,4,8,128,128]{4,3,2,1,0:T(8,128)(2,1)S(1)}, bf16[8,4,8,128,128]{4,3,2,1,0:T(8,128)(2,1)}, u32[]{:S(2)}) copy-start(bf16[8,4,8,128,128]{4,3,2,1,0:T(8,128)(2,1)} %param.14) | copy-start | bytes 25165828
  17.2 10.7 %copy-start.1 = (bf16[256,256]{1,0:T(8,128)(2,1)S(1)}, bf16[256,256]{1,0:T(8,128)(2,1)}, u32[]{:S(2)}) copy-start(bf16[256,256]{1,0:T(8,128)(2,1)} %constant.16.clone.z_ref) | copy-start | bytes 393220
  17.2 10.7 %copy-start.4 = (bf16[8,4,8,128]{3,2,1,0:T(8,128)(2,1)S(1)}, bf16[8,4,8,128]{3,2,1,0:T(8,128)(2,1)}, u32[]{:S(2)}) copy-start(bf16[8,4,8,128]{3,2,1,0:T(8,128)(2,1)} %param.11) | copy-start | bytes 196612
  17.8 22.2 %copy-start.3 = (bf16[256,256]{1,0:T(8,128)(2,1)S(1)}, bf16[256,256]{1,0:T(8,128)(2,1)}, u32[]{:S(2)}) copy-start(bf16[256,256]{1,0:T(8,128)(2,1)} %constant.17.clone.second_ref) | copy-start | bytes 393220
  28.0 23.8 %copy-start.2 = (bf16[256,256]{1,0:T(8,128)(2,1)S(1)}, bf16[256,256]{1,0:T(8,128)(2,1)}, u32[]{:S(2)}) copy-start(bf16[256,256]{1,0:T(8,128)(2,1)} %constant.18.clone.z_ref) | copy-start | bytes 393220
  28.0 23.8 %copy-start.5 = (bf16[128,128]{1,0:T(8,128)(2,1)S(1)}, bf16[128,128]{1,0:T(8,128)(2,1)}, u32[]{:S(2)}) copy-start(bf16[128,128]{1,0:T(8,128)(2,1)} %weight_ref.1) | copy-start | bytes 98308
  41.3 10.4 %all-to-all-start.3 = ((bf16[32,4,384]{2,1,0:T(4,128)(2,1)}), bf16[32,4,384]{2,1,0:T(4,128)(2,1)S(1)}, u32[]{:S(2)}, u32[]{:S(2)}) async-start(bf16[32,4,384]{2,1,0:T(4,128)(2,1)} %pad_maximum_fusion.1), calls=%async_computation.3 | async-start | bytes 196608 | tf_op jit(solution)/shard_map/all_to_all | solution.py:370

commit v5 on v4

--- a/solution.py
+++ b/solution.py
@@ -182,39 +182,34 @@
     ).astype(bf16)
     modes_ref[...] = field_modes(scale, x_ref[1, 0], x_ref[1, 1], z_ref)
     groups = modes_ref.shape[0] // 8
-    unrolled, on_vector = 16, 4
     row = lax.broadcasted_iota(jnp.int32, (8, LANES), 0)
     lane = lanes_of((LANES, LANES))
-
-    @pl.loop(0, groups // unrolled)
-    def _(turn):
-        kept = jnp.zeros((LANES, LANES), f32)
-        for at in range(unrolled):
-            group = turn * unrolled + at
-            start = pl.multiple_of(group * 8, 8)
-            if at < unrolled - on_vector:
-                modes = modes_ref[pl.ds(start, 8), :]
-                high = modes.astype(bf16).astype(f32)
-                every = lax.dot_general(
-                    jnp.concatenate([high, modes - high], 0).astype(bf16),
-                    w_ref[:, group].reshape(8 * LANES, LANES),
-                    (((1,), (1,)), ((), ())),
-                    preferred_element_type=f32,
-                )
-                every = every[:8] + every[8:]
-                total = jnp.zeros((8, LANES), f32)
-                for mode in range(8):
-                    part = every[:, mode * LANES : (mode + 1) * LANES]
-                    total = jnp.where(row == mode, part, total)
-                back[pl.ds(start, 8), :] = total
-            else:
-                for mode in range(8):
-                    weights = w_ref[mode, group].astype(f32)
-                    total = jnp.sum(weights * modes_ref[pl.ds(start + mode, 1), :], 1, keepdims=True)
-                    place = (at - unrolled + on_vector) * 8 + mode
-                    kept = jnp.where(lane == place, total, kept)
-        start = pl.multiple_of(((turn + 1) * unrolled - on_vector) * 8, 8)
-        back[pl.ds(start, on_vector * 8), :] = kept.T[: on_vector * 8]
+    on_vector = [group for group in range(groups) if group * 10 // groups != (group + 1) * 10 // groups]
+    kept = jnp.zeros((LANES, LANES), f32)
+    for group in range(groups):
+        start = group * 8
+        if group in on_vector:
+            for mode in range(8):
+                weights = w_ref[mode, group].astype(f32)
+                total = jnp.sum(weights * modes_ref[start + mode : start + mode + 1, :], 1, keepdims=True)
+                kept = jnp.where(lane == on_vector.index(group) * 8 + mode, total, kept)
+            continue
+        modes = modes_ref[start : start + 8, :]
+        high = modes.astype(bf16).astype(f32)
+        every = lax.dot_general(
+            jnp.concatenate([high, modes - high], 0).astype(bf16),
+            w_ref[:, group].reshape(8 * LANES, LANES),
+            (((1,), (1,)), ((), ())),
+            preferred_element_type=f32,
+        )
+        every = every[:8] + every[8:]
+        total = jnp.zeros((8, LANES), f32)
+        for mode in range(8):
+            total = jnp.where(row == mode, every[:, mode * LANES : (mode + 1) * LANES], total)
+        back[start : start + 8, :] = total
+    kept = kept.T
+    for at, group in enumerate(on_vector):
+        back[group * 8 : group * 8 + 8, :] = kept[at * 8 : at * 8 + 8]
 
     rows = back[...].astype(bf16).astype(f32)
     pack_ref[...] = quarters(rows).astype(bf16)
@@ -257,7 +252,7 @@
         copy(group).wait()
 
 
-def back_plane_kernel(s, scale, x_ref, first_ref, second_ref, out_ref):
+def back_plane_kernel(s, scale, x_ref, first_ref, second_ref, sum_ref, out_ref):
     tiles = x_ref[...].astype(f32).reshape(s.gx, s.gy, 8, LANES)
     parts = jnp.concatenate(first_axis(tiles, first_ref, s.gx, s.gy), 1)
     rows, across = parts.shape
@@ -282,7 +277,12 @@
         value = here[:rows]
         for place in range(1, 4):
             value = jnp.where(group_of == place, here[place * rows : (place + 1) * rows], value)
-        out_ref[part * rows : (part + 1) * rows, :] = (value * scale).astype(bf16)
+        value = (value * scale).reshape(s.gy, 8, LANES)
+        mine = slice(part * s.gy, (part + 1) * s.gy)
+        out_ref[mine, :, :LANES] = value[:, :4].astype(bf16)
+        out_ref[mine, :, LANES : 2 * LANES] = value[:, 4:].astype(bf16)
+    sums = jnp.broadcast_to(sum_ref[...][None], (s.devices, 4, LANES))
+    out_ref[:, :, 2 * LANES :] = sums.astype(bf16)
 
 
 def close_kernel(scale, x_ref, z_ref, pre_ref, weight_ref, sum_ref, out_ref, skip_ref):
@@ -423,24 +423,23 @@
         grad_pre,
     )
     pieces = lambda rows, sums: jnp.concatenate(
-        [rows.reshape(devices, 4, -1), sums.reshape(devices, 4, channels)], 2
+        [rows[:, :4], rows[:, 4:], sums.reshape(devices, 4, channels)], 2
     )
     split = lambda got: (
-        got[:, :, : 2 * LANES].reshape(cells, LANES),
+        jnp.concatenate([got[:, :, :LANES], got[:, :, LANES : 2 * LANES]], 1).reshape(cells, LANES),
         got[:, :, 2 * LANES :],
     )
-    back_columns, sums = split(exchange(pieces(back, sums)))
+    back_columns, sums = split(exchange(pieces(back.reshape(devices, 8, LANES), sums)))
     skip_rows = jnp.sum(sums.astype(f32), 0) * (1.0 / math.sqrt(cells * devices))
-    skip_rows = jnp.broadcast_to(skip_rows.astype(bf16), sums.shape)
     back_planes = call(
         functools.partial(back_plane_kernel, s, t["back_scale"]),
-        in_vmem(back_rows, LANES),
+        in_hbm(devices, 4, 3 * LANES),
         16,
         back_rows * back_rows * LANES * 8,
         MIB,
-        in_specs=[vmem] * 3,
+        in_specs=[vmem] * 4,
         out_specs=vmem,
-    )(back_columns, t["back_first"], t["back_second"])
+    )(back_columns, t["back_first"], t["back_second"], skip_rows)
     split_modes = (s.x, s.y * s.z, channels, channels)
     grad_spectral = call(
         functools.partial(outer_kernel, t["z_scale"]),
@@ -456,7 +455,7 @@
             pltpu.SemaphoreType.DMA((s.y * s.z // 2,)),
         ],
     )(owned, t["z"], grad_modes, back_planes)
-    spectral, sums = split(exchange(pieces(back_planes, skip_rows)))
+    spectral, sums = split(exchange(back_planes))
     grad_inputs, grad_skip = call(
         functools.partial(close_kernel, t["z_scale"]),
         (in_hbm(cells, channels), in_hbm(channels, channels, kind=f32)),

time: 52.9 us -> 52.4 us (level)
  other arithmetic: 0.78 us -> 0.18 us
    concatenate x2 -> x1, other arithmetic: 0.73 us -> 0.05 us  [on_device_whole_planes(): jnp.concatenate([rows[:, :4], rows[:, 4:], sums.reshape(devices, 4, chann...]
    pallas_call x1, Pallas kernels: 0.57 us -> 1.2 us  [on_device_whole_planes(): call(functools.partial(back_plane_kernel, s, t['back_scale']), in_hbm(dev...]
where the time goes in v5:
time: 52.4 us; the launch traced here: 52.2 us
  blocking collectives  34.9 us (67%)
  Pallas kernels  10.1 us (19%)
  waiting for transfers between devices  3.56 us (7%)
  starting transfers between devices  2.56 us (5%)
  between operations  0.78 us (1%)
    all_to_all x3, blocking collectives, exchange(): return lax.all_to_all(pieces, ('gx', 'gy'), 0, 0)  34.9 us
    pallas_call x1, Pallas kernels, on_device_whole_planes(): call(functools.partial(outer_kernel, t['z_scale']), in_hbm(*split_modes),...  4.21 us
    all_to_all x1, waiting for transfers between devices, exchange(): return lax.all_to_all(pieces, ('gx', 'gy'), 0, 0)  3.56 us
    all_to_all x1, starting transfers between devices, exchange(): return lax.all_to_all(pieces, ('gx', 'gy'), 0, 0)  2.56 us
    pallas_call x1, Pallas kernels, on_device_whole_planes(): call(functools.partial(modes_kernel, t['z_scale']), (in_vmem(cells, chann...  1.91 us
    pallas_call x1, Pallas kernels, on_device_whole_planes(): call(functools.partial(open_kernel, s), (in_vmem(2, 2, cells // 2, LANES)...  1.27 us
    pallas_call x1, Pallas kernels, on_device_whole_planes(): call(functools.partial(back_plane_kernel, s, t['back_scale']), in_hbm(dev...  1.2 us
  transfers between devices with their start and end apart: 1, of which 1 were waited for; matrix products, arithmetic and copies ran while one was open for 0% of the time, Pallas kernels for 8%

profile of v5, /device:TPU:0, one launch (start us, length us, event | category | flops | bytes accessed | tf_op | source)
XLA Modules:
  0.0 52.2 jit_solution(4936884715212072153)
XLA Ops:
  0.6 0.0 copy-start.6
  0.6 0.0 copy-start.7
  0.7 1.3 %shard_map.130 = (bf16[2,2,128,128]{3,2,1,0:T(8,128)(2,1)S(1)}, bf16[256,128]{1,0:T(8,128)(2,1)S(1)}) custom-call(bf16[256,128]{1,0:T(8,128)(2,1)} %bitcast.24, bf16[256,128]{1,0:T(8,128)(2,1)} %bitcast.29, bf16[256,128]{1,0:T(8,128)(2,1)} %bitcast.30), custom_call_target="tpu_custom_call" | custom-call | flops 1099511627776 | bytes 1048576 | tf_op jit(solution)/shard_map/pallas_call | solution.py:383
  1.9 15.3 %all_to_all.20 = bf16[32,16,128]{2,1,0:T(8,128)(2,1)S(1)} all-to-all(bf16[32,16,128]{2,1,0:T(8,128)(2,1)S(1)} %bitcast.20), channel_id=1, replica_groups=mesh['gx'=4,'gy'=8] {'gx','gy'}, dimensions={0} | all-to-all | bytes 262144 | tf_op jit(solution)/shard_map/all_to_all | solution.py:370
  17.2 0.0 copy-done.6
  17.2 0.0 copy-done.7
  17.2 0.0 copy-start.4
  17.2 0.6 %shard_map.131 = bf16[512,128]{1,0:T(8,128)(2,1)S(1)} custom-call(bf16[512,128]{1,0:T(8,128)(2,1)S(1)} %bitcast.21, bf16[32,64]{1,0:T(8,128)(2,1)S(1)} %copy-done.6, bf16[512,128]{1,0:T(8,128)(2,1)S(1)} %copy-done.7), custom_call_target="tpu_custom_call" | custom-call | flops 68719476736 | bytes 1048576 | tf_op jit(solution)/shard_map/pallas_call | solution.py:394
  17.8 0.0 copy-start.2
  17.8 10.1 %all_to_all.21 = bf16[32,16,128]{2,1,0:T(8,128)(2,1)S(1)} all-to-all(bf16[32,16,128]{2,1,0:T(8,128)(2,1)S(1)} %bitcast.22), channel_id=1, replica_groups=mesh['gx'=4,'gy'=8] {'gx','gy'}, dimensions={0} | all-to-all | bytes 262144 | tf_op jit(solution)/shard_map/all_to_all | solution.py:370
  28.0 0.0 copy-done
  28.0 0.0 copy-done.1
  28.0 0.0 copy-start.3
  28.0 0.0 copy-start.5
  28.0 1.9 %shard_map.132 = (bf16[256,128]{1,0:T(8,128)(2,1)S(1)}, bf16[128,128]{1,0:T(8,128)(2,1)S(1)}, f32[256,128]{1,0:T(8,128)S(1)}) custom-call(bf16[2,2,128,128]{3,2,1,0:T(8,128)(2,1)S(1)} %bitcast.18, bf16[256,256]{1,0:T(8,128)(2,1)S(1)} %copy-done.1, bf16[8,32,128,128]{3,2,1,0:T(8,128)(2,1)S(1)} %bitcast.17, bf16[256,128]{1,0:T(8,128)(2,1)S(1)} %bitcast.25, ...), custom_call_target="tpu_custom_call" | custom-call | flops 67108864 | bytes 9437184 | tf_op jit(solution)/shard_map/pallas_call | solution.py:405
  29.9 0.1 pad_maximum_fusion
  30.0 9.5 %all_to_all.22 = bf16[32,4,384]{2,1,0:T(4,128)(2,1)S(1)} all-to-all(bf16[32,4,384]{2,1,0:T(4,128)(2,1)S(1)} %pad_maximum_fusion), channel_id=1, replica_groups=mesh['gx'=4,'gy'=8] {'gx','gy'}, dimensions={0} | all-to-all | bytes 196608 | tf_op jit(solution)/shard_map/all_to_all | solution.py:370
  39.6 1.2 %shard_map.133.after = bf16[32,4,384]{2,1,0:T(4,128)(2,1)} custom-call(bf16[256,128]{1,0:T(8,128)(2,1)S(1)} %maximum_bitcast_fusion.x_ref, bf16[32,64]{1,0:T(8,128)(2,1)S(1)} %copy-done.6, bf16[256,256]{1,0:T(8,128)(2,1)S(1)} %copy-done.2, f32[4,128]{1,0:T(4,128)S(1)} %broadcast_multiply_fusion.sum_ref), custom_call_target="tpu_custom_call" | custom-call | flops 67108864 | bytes 1048576 | tf_op jit(solution)/shard_map/pallas_call | solution.py:434
  40.8 2.6 %all-to-all-start.3 = ((bf16[32,4,384]{2,1,0:T(4,128)(2,1)}), bf16[32,4,384]{2,1,0:T(4,128)(2,1)S(1)}, u32[]{:S(2)}, u32[]{:S(2)}) async-start(bf16[32,4,384]{2,1,0:T(4,128)(2,1)} %shard_map.133.after), calls=%async_computation.3 | async-start | bytes 196608 | tf_op jit(solution)/shard_map/all_to_all | solution.py:370
  43.4 4.2 %shard_map.135 = bf16[8,32,128,128]{3,2,1,0:T(8,128)(2,1)} custom-call(bf16[2,2,128,128]{3,2,1,0:T(8,128)(2,1)S(1)} %bitcast.19, bf16[256,256]{1,0:T(8,128)(2,1)S(1)} %copy-done.1, f32[256,128]{1,0:T(8,128)S(1)} %get-tuple-element.15.grad_ref, bf16[32,4,384]{2,1,0:T(4,128)(2,1)} %shard_map.133.after), custom_call_target="tpu_custom_call" | custom-call | flops 8388608 | bytes 9437184 | tf_op jit(solution)/shard_map/pallas_call | solution.py:444
  47.6 3.6 %all-to-all-done.3 = bf16[32,4,384]{2,1,0:T(4,128)(2,1)S(1)} async-done(((bf16[32,4,384]{2,1,0:T(4,128)(2,1)}), bf16[32,4,384]{2,1,0:T(4,128)(2,1)S(1)}, u32[]{:S(2)}, u32[]{:S(2)}) %all-to-all-start.3) | async-done | bytes 98336 | tf_op jit(solution)/shard_map/all_to_all | solution.py:370
  51.2 0.0 copy-done.3
  51.2 0.0 copy-done.5
  51.3 0.9 %shard_map.134 = (bf16[256,128]{1,0:T(8,128)(2,1)}, f32[128,128]{1,0:T(8,128)}) custom-call(bf16[256,128]{1,0:T(8,128)(2,1)S(1)} %maximum_bitcast_fusion.1.x_ref, bf16[256,256]{1,0:T(8,128)(2,1)S(1)} %copy-done.3, bf16[256,128]{1,0:T(8,128)(2,1)S(1)} %get-tuple-element.11.pre_ref, bf16[128,128]{1,0:T(8,128)(2,1)S(1)} %copy-done.5, bf16[128,128]{1,0:T(8,128)(2,1)S(1)} %bitcast.23), custom_call_target="tpu_custom_call" | custom-call | flops 33554432 | bytes 1048576 | tf_op jit(solution)/shard_map/pallas_call | solution.py:459
  (11 shorter events, 0.2 us)
Async XLA Ops:
  0.6 16.6 %copy-start.6 = (bf16[32,64]{1,0:T(8,128)(2,1)S(1)}, bf16[32,64]{1,0:T(8,128)(2,1)}, u32[]{:S(2)}) copy-start(bf16[32,64]{1,0:T(8,128)(2,1)} %constant.14.clone.first_ref) | copy-start | bytes 12292
  0.6 16.6 %copy-start.7 = (bf16[512,128]{1,0:T(8,128)(2,1)S(1)}, bf16[512,128]{1,0:T(8,128)(2,1)}, u32[]{:S(2)}) copy-start(bf16[512,128]{1,0:T(8,128)(2,1)} %constant.15.clone.second_ref) | copy-start | bytes 393220
  17.2 10.7 %copy-start = (bf16[8,4,8,128,128]{4,3,2,1,0:T(8,128)(2,1)S(1)}, bf16[8,4,8,128,128]{4,3,2,1,0:T(8,128)(2,1)}, u32[]{:S(2)}) copy-start(bf16[8,4,8,128,128]{4,3,2,1,0:T(8,128)(2,1)} %param.14) | copy-start | bytes 25165828
  17.2 10.7 %copy-start.1 = (bf16[256,256]{1,0:T(8,128)(2,1)S(1)}, bf16[256,256]{1,0:T(8,128)(2,1)}, u32[]{:S(2)}) copy-start(bf16[256,256]{1,0:T(8,128)(2,1)} %constant.16.clone.z_ref) | copy-start | bytes 393220
  17.2 10.7 %copy-start.4 = (bf16[8,4,8,128]{3,2,1,0:T(8,128)(2,1)S(1)}, bf16[8,4,8,128]{3,2,1,0:T(8,128)(2,1)}, u32[]{:S(2)}) copy-start(bf16[8,4,8,128]{3,2,1,0:T(8,128)(2,1)} %param.11) | copy-start | bytes 196612
  17.8 21.8 %copy-start.2 = (bf16[256,256]{1,0:T(8,128)(2,1)S(1)}, bf16[256,256]{1,0:T(8,128)(2,1)}, u32[]{:S(2)}) copy-start(bf16[256,256]{1,0:T(8,128)(2,1)} %constant.17.clone.second_ref) | copy-start | bytes 393220
  28.0 23.3 %copy-start.3 = (bf16[256,256]{1,0:T(8,128)(2,1)S(1)}, bf16[256,256]{1,0:T(8,128)(2,1)}, u32[]{:S(2)}) copy-start(bf16[256,256]{1,0:T(8,128)(2,1)} %constant.18.clone.z_ref) | copy-start | bytes 393220
  28.0 23.3 %copy-start.5 = (bf16[128,128]{1,0:T(8,128)(2,1)S(1)}, bf16[128,128]{1,0:T(8,128)(2,1)}, u32[]{:S(2)}) copy-start(bf16[128,128]{1,0:T(8,128)(2,1)} %weight_ref.1) | copy-start | bytes 98308
  40.8 10.3 %all-to-all-start.3 = ((bf16[32,4,384]{2,1,0:T(4,128)(2,1)}), bf16[32,4,384]{2,1,0:T(4,128)(2,1)S(1)}, u32[]{:S(2)}, u32[]{:S(2)}) async-start(bf16[32,4,384]{2,1,0:T(4,128)(2,1)} %shard_map.133.after), calls=%async_computation.3 | async-start | bytes 196608 | tf_op jit(solution)/shard_map/all_to_all | solution.py:370

commit v6 on v5

--- a/solution.py
+++ b/solution.py
@@ -84,25 +84,32 @@
 
 def open_kernel(s, in_hbm, pre_hbm, cot_hbm, pack_ref, grad_ref, in_ref, pre_ref, cot_ref, sems):
     copies = load(
-        (in_hbm, in_ref, sems.at[0]), (pre_hbm, pre_ref, sems.at[1]), (cot_hbm, cot_ref, sems.at[2])
+        (in_hbm, in_ref, sems.at[0]),
+        (pre_hbm, pre_ref, sems.at[1]),
+        (cot_hbm, cot_ref, sems.at[2]),
     )
     cells = s.cells
     place = lax.broadcasted_iota(jnp.int32, (cells, 1), 0)
-    half_y = s.y // 2
-    half = cells // 2
+    half_y, half = s.y // 2, cells // 2
     yl, rest = place // half, place % half
-    z, rest = rest // (s.x * half_y), rest % (s.x * half_y)
+    mode, rest = rest // (s.x * half_y), rest % (s.x * half_y)
     yh, x = rest // s.x, rest % s.x
-    source = (x * s.y + yh * 2 + yl) * s.z + z
-    order = (lax.broadcasted_iota(jnp.int32, (cells, cells), 1) == source).astype(f32).astype(bf16)
+    source = lax.broadcasted_iota(jnp.int32, (1, cells), 1)
+    phase = mode * (source % s.z) % s.z
+    table = jnp.zeros((cells, cells), f32)
+    for value in range(s.z):
+        angle = 2.0 * math.pi * value / s.z
+        table = jnp.where(phase == value, math.cos(angle) + math.sin(angle), table)
+    table = jnp.where(x * s.y + yh * 2 + yl == source // s.z, table, 0.0).astype(bf16)
     for copy in copies:
         copy.wait()
     grad = (cot_ref[...].astype(f32) * gelu_slope_of(pre_ref[...].astype(f32))).astype(bf16)
     grad_ref[...] = grad
     rows = jnp.dot(
-        order, jnp.concatenate([in_ref[...], grad], 1), preferred_element_type=f32
+        table, jnp.concatenate([in_ref[...], grad], 1), preferred_element_type=f32
     )
     width = LANES // 2
+    half = rows.shape[0] // 2
     low = lanes_of((half, LANES)) < width
     for field in range(2):
         even = rows[:half, field * LANES : (field + 1) * LANES]
@@ -146,14 +153,15 @@
         out_ref[part * rows : (part + 1) * rows, :] = value.astype(bf16)
 
 
-def field_modes(scale, first, second, z_ref):
+def field_modes(s, first, second):
     width = LANES // 2
     first, second = first.astype(f32), second.astype(f32)
     low = lanes_of(first.shape) < width
     even = jnp.where(low, first, pltpu.roll(second, width, 1))
     odd = jnp.where(low, pltpu.roll(first, width, 1), second)
-    rows = jnp.concatenate([even, odd], 0).astype(bf16)
-    return jnp.dot(z_ref[...], rows, preferred_element_type=f32) * scale
+    even, odd = (value.reshape(s.z, s.y // 2, s.x, LANES) for value in (even, odd))
+    lines = [value[:, half].reshape(s.z * s.x, LANES) for half in range(s.y // 2) for value in (even, odd)]
+    return jnp.concatenate(lines, 0)
 
 
 def split_twice(value):
@@ -176,11 +184,12 @@
     return jnp.concatenate(pieces, 0)
 
 
-def modes_kernel(scale, x_ref, z_ref, w_ref, field_ref, pre_ref, pack_ref, sum_ref, modes_ref, back):
-    sum_ref[...] = lax.dot_general(
+def modes_kernel(s, x_ref, w_ref, field_ref, pre_ref, pack_ref, modes_ref, back):
+    sums = lax.dot_general(
         field_ref[...], pre_ref[...], (((0,), (0,)), ((), ())), preferred_element_type=f32
-    ).astype(bf16)
-    modes_ref[...] = field_modes(scale, x_ref[1, 0], x_ref[1, 1], z_ref)
+    )
+    pack_ref[:, :, 2 * LANES :] = sums.reshape(s.devices, 4, LANES).astype(bf16)
+    modes_ref[...] = field_modes(s, x_ref[1, 0], x_ref[1, 1])
     groups = modes_ref.shape[0] // 8
     row = lax.broadcasted_iota(jnp.int32, (8, LANES), 0)
     lane = lanes_of((LANES, LANES))
@@ -194,15 +203,12 @@
                 total = jnp.sum(weights * modes_ref[start + mode : start + mode + 1, :], 1, keepdims=True)
                 kept = jnp.where(lane == on_vector.index(group) * 8 + mode, total, kept)
             continue
-        modes = modes_ref[start : start + 8, :]
-        high = modes.astype(bf16).astype(f32)
         every = lax.dot_general(
-            jnp.concatenate([high, modes - high], 0).astype(bf16),
+            modes_ref[start : start + 8, :].astype(bf16),
             w_ref[:, group].reshape(8 * LANES, LANES),
             (((1,), (1,)), ((), ())),
             preferred_element_type=f32,
         )
-        every = every[:8] + every[8:]
         total = jnp.zeros((8, LANES), f32)
         for mode in range(8):
             total = jnp.where(row == mode, every[:, mode * LANES : (mode + 1) * LANES], total)
@@ -212,17 +218,19 @@
         back[group * 8 : group * 8 + 8, :] = kept[at * 8 : at * 8 + 8]
 
     rows = back[...].astype(bf16).astype(f32)
-    pack_ref[...] = quarters(rows).astype(bf16)
-
-
-def outer_kernel(scale, x_ref, z_ref, grad_ref, after, out_hbm, in_ref, made, sems):
-    in_ref[...] = field_modes(scale, x_ref[0, 0], x_ref[0, 1], z_ref)
+    rows = quarters(rows).reshape(s.devices, 8, LANES)
+    pack_ref[:, :, :LANES] = rows[:, :4].astype(bf16)
+    pack_ref[:, :, LANES : 2 * LANES] = rows[:, 4:].astype(bf16)
+
+
+def outer_kernel(s, x_ref, grad_ref, pre_ref, weight_ref, after, out_hbm, part_ref, in_ref, made, sems):
     del after
+    in_ref[...] = field_modes(s, x_ref[0, 0], x_ref[0, 1])
     lines, columns = made.shape[:2]
     across = 2
     size, unrolled = across * lines, 4
     groups = columns // across
-    row = lax.broadcasted_iota(jnp.int32, (3 * size, LANES), 0) % size
+    row = lax.broadcasted_iota(jnp.int32, (size, LANES), 0)
 
     def copy(group):
         part = pl.ds(group * across, across)
@@ -233,10 +241,8 @@
         for at in range(unrolled):
             group = turn * unrolled + at
             start = pl.multiple_of(group * size, size)
-            in_high, in_low = split_twice(in_ref[pl.ds(start, size), :])
-            high, low = split_twice(grad_ref[pl.ds(start, size), :])
-            left = jnp.concatenate([in_high, in_low, in_high], 0)
-            right = jnp.concatenate([high, high, low], 0)
+            left = in_ref[pl.ds(start, size), :].astype(bf16)
+            right = grad_ref[pl.ds(start, size), :].astype(bf16)
             zero = jnp.zeros((), bf16)
             right = jnp.concatenate([jnp.where(row == mode, right, zero) for mode in range(size)], 1)
             every = lax.dot_general(
@@ -247,13 +253,23 @@
                 made[mode % lines, group * across + mode // lines] = part
             copy(group).start()
 
+    part_ref[...] = lax.dot_general(
+        pre_ref[...], weight_ref[...], (((1,), (1,)), ((), ())), preferred_element_type=f32
+    )
+
     @pl.loop(0, groups)
     def _(group):
         copy(group).wait()
 
 
-def back_plane_kernel(s, scale, x_ref, first_ref, second_ref, sum_ref, out_ref):
-    tiles = x_ref[...].astype(f32).reshape(s.gx, s.gy, 8, LANES)
+def opened(got_ref):
+    got = [got_ref[:, :, i * LANES : (i + 1) * LANES].astype(f32) for i in range(3)]
+    return jnp.concatenate(got[:2], 1), got[2]
+
+
+def back_plane_kernel(s, scale, skip_scale, got_ref, first_ref, second_ref, out_ref):
+    tiles, sums = opened(got_ref)
+    tiles = tiles.reshape(s.gx, s.gy, 8, LANES)
     parts = jnp.concatenate(first_axis(tiles, first_ref, s.gx, s.gy), 1)
     rows, across = parts.shape
     wide = across // LANES
@@ -281,18 +297,16 @@
         mine = slice(part * s.gy, (part + 1) * s.gy)
         out_ref[mine, :, :LANES] = value[:, :4].astype(bf16)
         out_ref[mine, :, LANES : 2 * LANES] = value[:, 4:].astype(bf16)
-    sums = jnp.broadcast_to(sum_ref[...][None], (s.devices, 4, LANES))
-    out_ref[:, :, 2 * LANES :] = sums.astype(bf16)
-
-
-def close_kernel(scale, x_ref, z_ref, pre_ref, weight_ref, sum_ref, out_ref, skip_ref):
-    pieces = quarters(x_ref[...].astype(f32)).astype(bf16)
+    sums = jnp.sum(sums, 0, keepdims=True) * skip_scale
+    out_ref[:, :, 2 * LANES :] = jnp.broadcast_to(sums, (s.devices, 4, LANES)).astype(bf16)
+
+
+def close_kernel(scale, got_ref, z_ref, part_ref, out_ref, skip_ref):
+    rows, sums = opened(got_ref)
+    skip_ref[...] = sums
+    pieces = quarters(rows.reshape(-1, LANES)).astype(bf16)
     cells = jnp.dot(z_ref[...], pieces, preferred_element_type=f32)
-    part = lax.dot_general(
-        pre_ref[...], weight_ref[...], (((1,), (1,)), ((), ())), preferred_element_type=f32
-    )
-    out_ref[...] = (part + cells * scale).astype(bf16)
-    skip_ref[...] = sum_ref[...].astype(f32)
+    out_ref[...] = (part_ref[...] + cells * scale).astype(bf16)
 
 
 def one_hot(rows, columns):
@@ -320,10 +334,6 @@
     blocks = [cas_y[(at + b)[:, None], (at + y)[None, :]] * same for b, y in ((0, 0), (1, 1), (1, 0), (0, 1))]
     t["second"], factor = rounded_table(np.concatenate(blocks, 0))
     t["scale"] = factor / norm
-    b, c, a = split_index(s.cells, s.y, s.z, s.x)
-    bl, z, bh, al = split_index(s.cells, 2, s.z, s.y // 2, s.x)
-    same = one_hot(a * s.y + b, al * s.y + bh * 2 + bl)
-    t["z"] = same * cas_z[c[:, None], z[None, :]]
     t["z_scale"] = 1.0 / math.sqrt(s.z)
     py, x = split_index(s.gy * s.x, s.gy, s.x)
     same = one_hot(x, x)
@@ -380,6 +390,7 @@
     hbm = pl.BlockSpec(memory_space=pltpu.HBM)
     anywhere = pl.BlockSpec(memory_space=pl.ANY)
     field = pltpu.VMEM((cells, channels), bf16)
+    given = (flat(inputs), flat(preact), flat(cotangent))
     pieces, grad_pre = call(
         functools.partial(open_kernel, s),
         (in_vmem(2, 2, cells // 2, LANES), in_vmem(cells, channels)),
@@ -389,10 +400,10 @@
         in_specs=[hbm] * 3,
         out_specs=(vmem, vmem),
         scratch_shapes=[field, field, field, pltpu.SemaphoreType.DMA((3,))],
-    )(*(pltpu.with_memory_space_constraint(flat(a), pltpu.HBM) for a in (inputs, preact, cotangent)))
+    )(*(pltpu.with_memory_space_constraint(a, pltpu.HBM) for a in given))
     columns = exchange(pieces.reshape(devices, -1, LANES))
     planes = call(
-        functools.partial(plane_kernel, s, t["scale"]),
+        functools.partial(plane_kernel, s, t["scale"] * t["z_scale"]),
         in_vmem(rows, LANES),
         16,
         1 << 36,
@@ -402,73 +413,66 @@
     )(columns.reshape(rows, LANES), t["first"], t["second"])
     owned = exchange(planes.reshape(devices, -1, LANES))
     owned = owned.reshape(2, 2, cells // 2, LANES)
-    back, sums, grad_modes = call(
-        functools.partial(modes_kernel, t["z_scale"]),
+    back, grad_modes = call(
+        functools.partial(modes_kernel, s),
         (
-            in_vmem(cells, channels),
-            in_vmem(channels, channels),
+            in_vmem(devices, 4, 3 * LANES),
             in_vmem(cells, channels, kind=f32),
         ),
         24,
         cells * channels * channels * 16,
         9 * MIB,
-        in_specs=[vmem] * 5,
-        out_specs=(vmem, vmem, vmem),
+        in_specs=[vmem] * 4,
+        out_specs=(vmem, vmem),
         scratch_shapes=[pltpu.VMEM((cells, channels), f32)],
     )(
         owned,
-        t["z"],
         spectral_w.reshape(s.x, s.y * s.z, channels, channels),
         flat(inputs),
         grad_pre,
     )
-    pieces = lambda rows, sums: jnp.concatenate(
-        [rows[:, :4], rows[:, 4:], sums.reshape(devices, 4, channels)], 2
-    )
-    split = lambda got: (
-        jnp.concatenate([got[:, :, :LANES], got[:, :, LANES : 2 * LANES]], 1).reshape(cells, LANES),
-        got[:, :, 2 * LANES :],
-    )
-    back_columns, sums = split(exchange(pieces(back.reshape(devices, 8, LANES), sums)))
-    skip_rows = jnp.sum(sums.astype(f32), 0) * (1.0 / math.sqrt(cells * devices))
+    got = exchange(back)
     back_planes = call(
-        functools.partial(back_plane_kernel, s, t["back_scale"]),
+        functools.partial(
+            back_plane_kernel, s, t["back_scale"], 1.0 / math.sqrt(cells * devices)
+        ),
         in_hbm(devices, 4, 3 * LANES),
         16,
         back_rows * back_rows * LANES * 8,
         MIB,
-        in_specs=[vmem] * 4,
+        in_specs=[vmem] * 3,
         out_specs=vmem,
-    )(back_columns, t["back_first"], t["back_second"], skip_rows)
+    )(got, t["back_first"], t["back_second"])
     split_modes = (s.x, s.y * s.z, channels, channels)
-    grad_spectral = call(
-        functools.partial(outer_kernel, t["z_scale"]),
-        in_hbm(*split_modes),
+    split_modes = (s.x, s.y * s.z, channels, channels)
+    grad_spectral, skip_part = call(
+        functools.partial(outer_kernel, s),
+        (in_hbm(*split_modes), in_vmem(cells, channels, kind=f32)),
         24,
         cells * channels * channels * 2,
         9 * MIB,
-        in_specs=[vmem] * 3 + [anywhere],
-        out_specs=hbm,
+        in_specs=[vmem] * 4 + [anywhere],
+        out_specs=(hbm, vmem),
         scratch_shapes=[
             pltpu.VMEM((cells, channels), f32),
             pltpu.VMEM(split_modes, bf16),
             pltpu.SemaphoreType.DMA((s.y * s.z // 2,)),
         ],
-    )(owned, t["z"], grad_modes, back_planes)
-    spectral, sums = split(exchange(back_planes))
+    )(owned, grad_modes, grad_pre, skip_w, back_planes)
+    got = exchange(back_planes)
     grad_inputs, grad_skip = call(
         functools.partial(close_kernel, t["z_scale"]),
-        (in_hbm(cells, channels), in_hbm(channels, channels, kind=f32)),
+        (in_hbm(cells, channels), in_hbm(devices, 4, channels, kind=f32)),
         16,
         cells * cells * LANES * 4,
         MIB,
-        in_specs=[vmem] * 5,
+        in_specs=[vmem] * 3,
         out_specs=(vmem, vmem),
-    )(spectral, t["back_z"], grad_pre, skip_w, sums.reshape(channels, channels))
+    )(got, t["back_z"], skip_part)
     return (
         grad_inputs.reshape(inputs.shape),
         grad_spectral.reshape(spectral_w.shape),
-        grad_skip,
+        grad_skip.reshape(channels, channels),
     )
 
 

time: 52.4 us -> 51.9 us (level)
  no operation moved by 1% of the time
where the time goes in v6:
time: 51.9 us; the launch traced here: 51.7 us
  blocking collectives  34.9 us (67%)
  Pallas kernels  9.71 us (19%)
  waiting for transfers between devices  3.75 us (7%)
  starting transfers between devices  2.56 us (5%)
  between operations  0.73 us (1%)
    all_to_all x3, blocking collectives, exchange(): return lax.all_to_all(pieces, ('gx', 'gy'), 0, 0)  34.9 us
    pallas_call x1, Pallas kernels, on_device_whole_planes(): call(functools.partial(outer_kernel, s), (in_hbm(*split_modes), in_vmem(c...  4.01 us
    all_to_all x1, waiting for transfers between devices, exchange(): return lax.all_to_all(pieces, ('gx', 'gy'), 0, 0)  3.75 us
    all_to_all x1, starting transfers between devices, exchange(): return lax.all_to_all(pieces, ('gx', 'gy'), 0, 0)  2.56 us
    pallas_call x1, Pallas kernels, on_device_whole_planes(): call(functools.partial(modes_kernel, s), (in_vmem(devices, 4, 3 * LANES),...  1.75 us
    pallas_call x1, Pallas kernels, on_device_whole_planes(): call(functools.partial(open_kernel, s), (in_vmem(2, 2, cells // 2, LANES)...  1.27 us
    pallas_call x1, Pallas kernels, on_device_whole_planes(): call(functools.partial(back_plane_kernel, s, t['back_scale'], 1.0 / math....  1.22 us
  transfers between devices with their start and end apart: 1, of which 1 were waited for; matrix products, arithmetic and copies ran while one was open for 0% of the time, Pallas kernels for 8%

profile of v6, /device:TPU:0, one launch (start us, length us, event | category | flops | bytes accessed | tf_op | source)
XLA Modules:
  0.0 51.7 jit_solution(7961131427133176688)
XLA Ops:
  0.6 0.0 copy-start.5
  0.6 0.0 copy-start.6
  0.7 1.3 %shard_map.121 = (bf16[2,2,128,128]{3,2,1,0:T(8,128)(2,1)S(1)}, bf16[256,128]{1,0:T(8,128)(2,1)S(1)}) custom-call(bf16[256,128]{1,0:T(8,128)(2,1)} %bitcast.17, bf16[256,128]{1,0:T(8,128)(2,1)} %bitcast.20, bf16[256,128]{1,0:T(8,128)(2,1)} %bitcast.21), custom_call_target="tpu_custom_call" | custom-call | flops 1099511627776 | bytes 1048576 | tf_op jit(solution)/shard_map/pallas_call | solution.py:394
  1.9 15.3 %all_to_all.20 = bf16[32,16,128]{2,1,0:T(8,128)(2,1)S(1)} all-to-all(bf16[32,16,128]{2,1,0:T(8,128)(2,1)S(1)} %bitcast.14), channel_id=1, replica_groups=mesh['gx'=4,'gy'=8] {'gx','gy'}, dimensions={0} | all-to-all | bytes 262144 | tf_op jit(solution)/shard_map/all_to_all | solution.py:380
  17.2 0.0 copy-done.5
  17.2 0.0 copy-done.6
  17.2 0.0 copy-start
  17.2 0.5 %shard_map.122 = bf16[512,128]{1,0:T(8,128)(2,1)S(1)} custom-call(bf16[512,128]{1,0:T(8,128)(2,1)S(1)} %bitcast.15, bf16[32,64]{1,0:T(8,128)(2,1)S(1)} %copy-done.5, bf16[512,128]{1,0:T(8,128)(2,1)S(1)} %copy-done.6), custom_call_target="tpu_custom_call" | custom-call | flops 68719476736 | bytes 1048576 | tf_op jit(solution)/shard_map/pallas_call | solution.py:405
  17.8 0.0 copy-start.2
  17.8 0.0 copy-start.4
  17.8 0.0 copy-start.1
  17.8 10.1 %all_to_all.21 = bf16[32,16,128]{2,1,0:T(8,128)(2,1)S(1)} all-to-all(bf16[32,16,128]{2,1,0:T(8,128)(2,1)S(1)} %bitcast.16), channel_id=1, replica_groups=mesh['gx'=4,'gy'=8] {'gx','gy'}, dimensions={0} | all-to-all | bytes 262144 | tf_op jit(solution)/shard_map/all_to_all | solution.py:380
  28.0 0.0 copy-done
  28.0 0.0 copy-done.3
  28.0 1.7 %shard_map.123 = (bf16[32,4,384]{2,1,0:T(4,128)(2,1)S(1)}, f32[256,128]{1,0:T(8,128)S(1)}) custom-call(bf16[2,2,128,128]{3,2,1,0:T(8,128)(2,1)S(1)} %bitcast.12, bf16[8,32,128,128]{3,2,1,0:T(8,128)(2,1)S(1)} %bitcast.11, bf16[256,128]{1,0:T(8,128)(2,1)S(1)} %bitcast.18, bf16[256,128]{1,0:T(8,128)(2,1)S(1)} %get-tuple-element.12.pre_ref), custom_call_target="tpu_custom_call" | custom-call | flops 67108864 | bytes 9437184 | tf_op jit(solution)/shard_map/pallas_call | solution.py:416
  29.7 9.5 %all_to_all.22.got_ref = bf16[32,4,384]{2,1,0:T(4,128)(2,1)S(1)} all-to-all(bf16[32,4,384]{2,1,0:T(4,128)(2,1)S(1)} %get-tuple-element.13), channel_id=1, replica_groups=mesh['gx'=4,'gy'=8] {'gx','gy'}, dimensions={0} | all-to-all | bytes 196608 | tf_op jit(solution)/shard_map/all_to_all | solution.py:380
  39.2 0.0 copy-done.2
  39.2 1.2 %shard_map.124.after = bf16[32,4,384]{2,1,0:T(4,128)(2,1)} custom-call(bf16[32,4,384]{2,1,0:T(4,128)(2,1)S(1)} %all_to_all.22.got_ref, bf16[32,64]{1,0:T(8,128)(2,1)S(1)} %copy-done.5, bf16[256,256]{1,0:T(8,128)(2,1)S(1)} %copy-done.2), custom_call_target="tpu_custom_call" | custom-call | flops 67108864 | bytes 1048576 | tf_op jit(solution)/shard_map/pallas_call | solution.py:435
  40.4 2.6 %all-to-all-start.3 = ((bf16[32,4,384]{2,1,0:T(4,128)(2,1)}), bf16[32,4,384]{2,1,0:T(4,128)(2,1)S(1)}, u32[]{:S(2)}, u32[]{:S(2)}) async-start(bf16[32,4,384]{2,1,0:T(4,128)(2,1)} %shard_map.124.after), calls=%async_computation.3 | async-start | bytes 196608 | tf_op jit(solution)/shard_map/all_to_all | solution.py:380
  43.0 0.0 copy-done.4
  43.0 4.0 %shard_map.125 = (bf16[8,32,128,128]{3,2,1,0:T(8,128)(2,1)}, f32[256,128]{1,0:T(8,128)S(1)}) custom-call(bf16[2,2,128,128]{3,2,1,0:T(8,128)(2,1)S(1)} %bitcast.13, f32[256,128]{1,0:T(8,128)S(1)} %get-tuple-element.14.grad_ref, bf16[256,128]{1,0:T(8,128)(2,1)S(1)} %get-tuple-element.12.pre_ref, bf16[128,128]{1,0:T(8,128)(2,1)S(1)} %copy-done.4, ...), custom_call_target="tpu_custom_call" | custom-call | flops 8388608 | bytes 9437184 | tf_op jit(solution)/shard_map/pallas_call | solution.py:448
  47.0 3.7 %all-to-all-done.3.got_ref = bf16[32,4,384]{2,1,0:T(4,128)(2,1)S(1)} async-done(((bf16[32,4,384]{2,1,0:T(4,128)(2,1)}), bf16[32,4,384]{2,1,0:T(4,128)(2,1)S(1)}, u32[]{:S(2)}, u32[]{:S(2)}) %all-to-all-start.3) | async-done | bytes 98336 | tf_op jit(solution)/shard_map/all_to_all | solution.py:380
  50.8 0.0 copy-done.1
  50.8 0.9 %shard_map.126 = (bf16[256,128]{1,0:T(8,128)(2,1)}, f32[32,4,128]{2,1,0:T(4,128)}) custom-call(bf16[32,4,384]{2,1,0:T(4,128)(2,1)S(1)} %all-to-all-done.3.got_ref, bf16[256,256]{1,0:T(8,128)(2,1)S(1)} %copy-done.1, f32[256,128]{1,0:T(8,128)S(1)} %get-tuple-element.15.part_ref), custom_call_target="tpu_custom_call" | custom-call | flops 33554432 | bytes 1048576 | tf_op jit(solution)/shard_map/pallas_call | solution.py:463
  (1 shorter events, 0.0 us)
Async XLA Ops:
  0.6 16.6 %copy-start.5 = (bf16[32,64]{1,0:T(8,128)(2,1)S(1)}, bf16[32,64]{1,0:T(8,128)(2,1)}, u32[]{:S(2)}) copy-start(bf16[32,64]{1,0:T(8,128)(2,1)} %constant.8.clone.first_ref) | copy-start | bytes 12292
  0.6 16.6 %copy-start.6 = (bf16[512,128]{1,0:T(8,128)(2,1)S(1)}, bf16[512,128]{1,0:T(8,128)(2,1)}, u32[]{:S(2)}) copy-start(bf16[512,128]{1,0:T(8,128)(2,1)} %constant.9.clone.second_ref) | copy-start | bytes 393220
  17.2 10.7 %copy-start = (bf16[8,4,8,128,128]{4,3,2,1,0:T(8,128)(2,1)S(1)}, bf16[8,4,8,128,128]{4,3,2,1,0:T(8,128)(2,1)}, u32[]{:S(2)}) copy-start(bf16[8,4,8,128,128]{4,3,2,1,0:T(8,128)(2,1)} %param.13) | copy-start | bytes 25165828
  17.2 10.7 %copy-start.3 = (bf16[8,4,8,128]{3,2,1,0:T(8,128)(2,1)S(1)}, bf16[8,4,8,128]{3,2,1,0:T(8,128)(2,1)}, u32[]{:S(2)}) copy-start(bf16[8,4,8,128]{3,2,1,0:T(8,128)(2,1)} %param.10) | copy-start | bytes 196612
  17.8 21.4 %copy-start.2 = (bf16[256,256]{1,0:T(8,128)(2,1)S(1)}, bf16[256,256]{1,0:T(8,128)(2,1)}, u32[]{:S(2)}) copy-start(bf16[256,256]{1,0:T(8,128)(2,1)} %constant.10.clone.second_ref) | copy-start | bytes 393220
  17.8 25.2 %copy-start.4 = (bf16[128,128]{1,0:T(8,128)(2,1)S(1)}, bf16[128,128]{1,0:T(8,128)(2,1)}, u32[]{:S(2)}) copy-start(bf16[128,128]{1,0:T(8,128)(2,1)} %weight_ref.1) | copy-start | bytes 98308
  17.8 33.0 %copy-start.1 = (bf16[256,256]{1,0:T(8,128)(2,1)S(1)}, bf16[256,256]{1,0:T(8,128)(2,1)}, u32[]{:S(2)}) copy-start(bf16[256,256]{1,0:T(8,128)(2,1)} %constant.11.clone.z_ref) | copy-start | bytes 393220
  40.4 10.3 %all-to-all-start.3 = ((bf16[32,4,384]{2,1,0:T(4,128)(2,1)}), bf16[32,4,384]{2,1,0:T(4,128)(2,1)S(1)}, u32[]{:S(2)}, u32[]{:S(2)}) async-start(bf16[32,4,384]{2,1,0:T(4,128)(2,1)} %shard_map.124.after), calls=%async_computation.3 | async-start | bytes 196608 | tf_op jit(solution)/shard_map/all_to_all | solution.py:380

commit v7 on v6

--- a/solution.py
+++ b/solution.py
@@ -132,25 +132,36 @@
     ]
 
 
+def halves(first, second):
+    width = LANES // 2
+    low = lanes_of(first.shape) < width
+    return (
+        jnp.where(low, first, pltpu.roll(second, width, 1)),
+        jnp.where(low, pltpu.roll(first, width, 1), second),
+    )
+
+
+def second_axis(table_ref, value):
+    table = table_ref[...]
+    return jnp.dot(
+        jnp.concatenate([table, table], 1),
+        jnp.concatenate(split_twice(value), 0),
+        preferred_element_type=f32,
+    )
+
+
 def plane_kernel(s, scale, x_ref, first_ref, second_ref, out_ref):
-    width = LANES // 2
     across = s.gy * s.y // 2
     tiles = x_ref[...].astype(f32).reshape(s.gx, across, 8, LANES)
-    parts = jnp.concatenate(first_axis(tiles, first_ref, s.gx, across), 1)
+    parts = first_axis(tiles, first_ref, s.gx, across)
+    pairs = [jnp.concatenate(halves(*parts[i : i + 2]), 0) for i in range(0, s.gx, 2)]
+    made = second_axis(second_ref, jnp.concatenate(pairs, 1)) * scale
     rows = across * 8
-    table = second_ref[...]
-    made = jnp.dot(
-        jnp.concatenate([table, table], 1),
-        jnp.concatenate(split_twice(parts), 0),
-        preferred_element_type=f32,
-    )
-    low = lanes_of((rows, LANES)) < width
-    for part in range(s.gx):
-        here = made[:, part * LANES : (part + 1) * LANES]
-        straight = jnp.where(low, here[:rows], here[rows : 2 * rows])
-        crossed = jnp.where(low, here[2 * rows : 3 * rows], here[3 * rows :])
-        value = (straight + pltpu.roll(crossed, width, 1)) * scale
-        out_ref[part * rows : (part + 1) * rows, :] = value.astype(bf16)
+    for pair in range(s.gx // 2):
+        here = made[:, pair * LANES : (pair + 1) * LANES]
+        for i, value in enumerate(halves(here[:rows], here[rows:])):
+            start = (pair * 2 + i) * rows
+            out_ref[start : start + rows, :] = value.astype(bf16)
 
 
 def field_modes(s, first, second):
@@ -270,33 +281,11 @@
 def back_plane_kernel(s, scale, skip_scale, got_ref, first_ref, second_ref, out_ref):
     tiles, sums = opened(got_ref)
     tiles = tiles.reshape(s.gx, s.gy, 8, LANES)
-    parts = jnp.concatenate(first_axis(tiles, first_ref, s.gx, s.gy), 1)
-    rows, across = parts.shape
-    wide = across // LANES
-    turned = [parts]
-    for turn in range(1, 4):
-        moved = [
-            pltpu.roll(parts[:, i * LANES : (i + 1) * LANES], turn * (LANES // 4), 1)
-            for i in range(wide)
-        ]
-        turned.append(jnp.concatenate(moved, 1))
-    high, low = split_twice(jnp.concatenate(turned, 0))
-    table = second_ref[...]
-    made = jnp.dot(
-        jnp.concatenate([table, table], 1),
-        jnp.concatenate([high, low], 0),
-        preferred_element_type=f32,
-    )
-    group_of = lanes_of((rows, LANES)) // (LANES // 4)
-    for part in range(wide):
-        here = made[:, part * LANES : (part + 1) * LANES]
-        value = here[:rows]
-        for place in range(1, 4):
-            value = jnp.where(group_of == place, here[place * rows : (place + 1) * rows], value)
-        value = (value * scale).reshape(s.gy, 8, LANES)
-        mine = slice(part * s.gy, (part + 1) * s.gy)
-        out_ref[mine, :, :LANES] = value[:, :4].astype(bf16)
-        out_ref[mine, :, LANES : 2 * LANES] = value[:, 4:].astype(bf16)
+    parts = jnp.concatenate(first_axis(tiles, first_ref, s.gx, s.gy), 0)
+    made = quarters(second_axis(second_ref, quarters(parts)) * scale)
+    made = made.reshape(s.devices, 8, LANES)
+    out_ref[:, :, :LANES] = made[:, :4].astype(bf16)
+    out_ref[:, :, LANES : 2 * LANES] = made[:, 4:].astype(bf16)
     sums = jnp.sum(sums, 0, keepdims=True) * skip_scale
     out_ref[:, :, 2 * LANES :] = jnp.broadcast_to(sums, (s.devices, 4, LANES)).astype(bf16)
 
@@ -327,25 +316,14 @@
     t = {}
     t["first"] = twice(cas_x)
     t["back_first"] = twice(cas_x.T)
-    count = s.gy * s.y // 2 * s.x
-    py, yh, x = split_index(count, s.gy, s.y // 2, s.x)
-    at = py * s.y + yh * 2
-    same = one_hot(x, x)
-    blocks = [cas_y[(at + b)[:, None], (at + y)[None, :]] * same for b, y in ((0, 0), (1, 1), (1, 0), (0, 1))]
-    t["second"], factor = rounded_table(np.concatenate(blocks, 0))
+    yl, py, yh, x = split_index(2 * s.gy * s.y // 2 * s.x, 2, s.gy, s.y // 2, s.x)
+    at = py * s.y + yh * 2 + yl
+    t["second"], factor = rounded_table(cas_y[at[:, None], at[None, :]] * one_hot(x, x))
     t["scale"] = factor / norm
     t["z_scale"] = 1.0 / math.sqrt(s.z)
-    py, x = split_index(s.gy * s.x, s.gy, s.x)
-    same = one_hot(x, x)
-    blocks = []
-    for place in range(4):
-        line = []
-        for turn in range(4):
-            at_y = py * s.y + place
-            at_b = py * s.y + (place - turn) % 4
-            line.append(cas_y[at_b[None, :], at_y[:, None]] * same)
-        blocks.append(np.concatenate(line, 1))
-    t["back_second"], factor = rounded_table(np.concatenate(blocks, 0))
+    yl, py, x = split_index(4 * s.gy * s.x, 4, s.gy, s.x)
+    at = py * s.y + yl
+    t["back_second"], factor = rounded_table(cas_y[at[None, :], at[:, None]] * one_hot(x, x))
     t["back_scale"] = factor / norm
     x, y, z = split_index(s.cells, s.x, s.y, s.z)
     yl, c, xl = split_index(s.cells, s.y, s.z, s.x)
@@ -406,7 +384,7 @@
         functools.partial(plane_kernel, s, t["scale"] * t["z_scale"]),
         in_vmem(rows, LANES),
         16,
-        1 << 36,
+        1 << 31,
         MIB,
         in_specs=[vmem] * 3,
         out_specs=vmem,

time: 51.9 us -> 51.7 us (level)
  no operation moved by 1% of the time
where the time goes in v7:
time: 51.7 us; the launch traced here: 51.4 us
  blocking collectives  34.6 us (67%)
  Pallas kernels  9.72 us (19%)
  waiting for transfers between devices  3.74 us (7%)
  starting transfers between devices  2.56 us (5%)
  between operations  0.73 us (1%)
    all_to_all x3, blocking collectives, exchange(): return lax.all_to_all(pieces, ('gx', 'gy'), 0, 0)  34.6 us
    pallas_call x1, Pallas kernels, on_device_whole_planes(): call(functools.partial(outer_kernel, s), (in_hbm(*split_modes), in_vmem(c...  4.02 us
    all_to_all x1, waiting for transfers between devices, exchange(): return lax.all_to_all(pieces, ('gx', 'gy'), 0, 0)  3.74 us
    all_to_all x1, starting transfers between devices, exchange(): return lax.all_to_all(pieces, ('gx', 'gy'), 0, 0)  2.56 us
    pallas_call x1, Pallas kernels, on_device_whole_planes(): call(functools.partial(modes_kernel, s), (in_vmem(devices, 4, 3 * LANES),...  1.75 us
    pallas_call x1, Pallas kernels, on_device_whole_planes(): call(functools.partial(open_kernel, s), (in_vmem(2, 2, cells // 2, LANES)...  1.27 us
    pallas_call x1, Pallas kernels, on_device_whole_planes(): call(functools.partial(back_plane_kernel, s, t['back_scale'], 1.0 / math....  1.23 us
  transfers between devices with their start and end apart: 1, of which 1 were waited for; matrix products, arithmetic and copies ran while one was open for 0% of the time, Pallas kernels for 8%

profile of v7, /device:TPU:0, one launch (start us, length us, event | category | flops | bytes accessed | tf_op | source)
XLA Modules:
  0.0 51.4 jit_solution(7639499903644543609)
XLA Ops:
  0.6 0.0 copy-start.5
  0.6 0.0 copy-start.6
  0.7 1.3 %shard_map.121 = (bf16[2,2,128,128]{3,2,1,0:T(8,128)(2,1)S(1)}, bf16[256,128]{1,0:T(8,128)(2,1)S(1)}) custom-call(bf16[256,128]{1,0:T(8,128)(2,1)} %bitcast.17, bf16[256,128]{1,0:T(8,128)(2,1)} %bitcast.20, bf16[256,128]{1,0:T(8,128)(2,1)} %bitcast.21), custom_call_target="tpu_custom_call" | custom-call | flops 1099511627776 | bytes 1048576 | tf_op jit(solution)/shard_map/pallas_call | solution.py:372
  1.9 0.0 copy-start
  1.9 0.0 copy-start.3
  2.0 15.3 %all_to_all.20 = bf16[32,16,128]{2,1,0:T(8,128)(2,1)S(1)} all-to-all(bf16[32,16,128]{2,1,0:T(8,128)(2,1)S(1)} %bitcast.14), channel_id=1, replica_groups=mesh['gx'=4,'gy'=8] {'gx','gy'}, dimensions={0} | all-to-all | bytes 262144 | tf_op jit(solution)/shard_map/all_to_all | solution.py:358
  17.2 0.0 copy-done.5
  17.2 0.0 copy-done.6
  17.2 0.0 copy-start.4
  17.2 0.0 copy-start.1
  17.3 0.5 %shard_map.122 = bf16[512,128]{1,0:T(8,128)(2,1)S(1)} custom-call(bf16[512,128]{1,0:T(8,128)(2,1)S(1)} %bitcast.15, bf16[32,64]{1,0:T(8,128)(2,1)S(1)} %copy-done.5, bf16[256,256]{1,0:T(8,128)(2,1)S(1)} %copy-done.6), custom_call_target="tpu_custom_call" | custom-call | flops 2147483648 | bytes 1048576 | tf_op jit(solution)/shard_map/pallas_call | solution.py:383
  17.8 9.9 %all_to_all.21 = bf16[32,16,128]{2,1,0:T(8,128)(2,1)S(1)} all-to-all(bf16[32,16,128]{2,1,0:T(8,128)(2,1)S(1)} %bitcast.16), channel_id=1, replica_groups=mesh['gx'=4,'gy'=8] {'gx','gy'}, dimensions={0} | all-to-all | bytes 262144 | tf_op jit(solution)/shard_map/all_to_all | solution.py:358
  27.7 0.0 copy-done
  27.7 0.0 copy-done.3
  27.7 1.7 %shard_map.123 = (bf16[32,4,384]{2,1,0:T(4,128)(2,1)S(1)}, f32[256,128]{1,0:T(8,128)S(1)}) custom-call(bf16[2,2,128,128]{3,2,1,0:T(8,128)(2,1)S(1)} %bitcast.12, bf16[8,32,128,128]{3,2,1,0:T(8,128)(2,1)S(1)} %bitcast.11, bf16[256,128]{1,0:T(8,128)(2,1)S(1)} %bitcast.18, bf16[256,128]{1,0:T(8,128)(2,1)S(1)} %get-tuple-element.12.pre_ref), custom_call_target="tpu_custom_call" | custom-call | flops 67108864 | bytes 9437184 | tf_op jit(solution)/shard_map/pallas_call | solution.py:394
  29.5 9.5 %all_to_all.22.got_ref = bf16[32,4,384]{2,1,0:T(4,128)(2,1)S(1)} all-to-all(bf16[32,4,384]{2,1,0:T(4,128)(2,1)S(1)} %get-tuple-element.13), channel_id=1, replica_groups=mesh['gx'=4,'gy'=8] {'gx','gy'}, dimensions={0} | all-to-all | bytes 196608 | tf_op jit(solution)/shard_map/all_to_all | solution.py:358
  38.9 0.0 copy-done.2
  38.9 1.2 %shard_map.124.after = bf16[32,4,384]{2,1,0:T(4,128)(2,1)} custom-call(bf16[32,4,384]{2,1,0:T(4,128)(2,1)S(1)} %all_to_all.22.got_ref, bf16[32,64]{1,0:T(8,128)(2,1)S(1)} %copy-done.5, bf16[256,256]{1,0:T(8,128)(2,1)S(1)} %copy-done.2), custom_call_target="tpu_custom_call" | custom-call | flops 67108864 | bytes 1048576 | tf_op jit(solution)/shard_map/pallas_call | solution.py:413
  40.2 2.6 %all-to-all-start.3 = ((bf16[32,4,384]{2,1,0:T(4,128)(2,1)}), bf16[32,4,384]{2,1,0:T(4,128)(2,1)S(1)}, u32[]{:S(2)}, u32[]{:S(2)}) async-start(bf16[32,4,384]{2,1,0:T(4,128)(2,1)} %shard_map.124.after), calls=%async_computation.3 | async-start | bytes 196608 | tf_op jit(solution)/shard_map/all_to_all | solution.py:358
  42.7 0.0 copy-done.4
  42.7 4.0 %shard_map.125 = (bf16[8,32,128,128]{3,2,1,0:T(8,128)(2,1)}, f32[256,128]{1,0:T(8,128)S(1)}) custom-call(bf16[2,2,128,128]{3,2,1,0:T(8,128)(2,1)S(1)} %bitcast.13, f32[256,128]{1,0:T(8,128)S(1)} %get-tuple-element.14.grad_ref, bf16[256,128]{1,0:T(8,128)(2,1)S(1)} %get-tuple-element.12.pre_ref, bf16[128,128]{1,0:T(8,128)(2,1)S(1)} %copy-done.4, ...), custom_call_target="tpu_custom_call" | custom-call | flops 8388608 | bytes 9437184 | tf_op jit(solution)/shard_map/pallas_call | solution.py:426
  46.8 3.7 %all-to-all-done.3.got_ref = bf16[32,4,384]{2,1,0:T(4,128)(2,1)S(1)} async-done(((bf16[32,4,384]{2,1,0:T(4,128)(2,1)}), bf16[32,4,384]{2,1,0:T(4,128)(2,1)S(1)}, u32[]{:S(2)}, u32[]{:S(2)}) %all-to-all-start.3) | async-done | bytes 98336 | tf_op jit(solution)/shard_map/all_to_all | solution.py:358
  50.5 0.0 copy-done.1
  50.5 0.9 %shard_map.126 = (bf16[256,128]{1,0:T(8,128)(2,1)}, f32[32,4,128]{2,1,0:T(4,128)}) custom-call(bf16[32,4,384]{2,1,0:T(4,128)(2,1)S(1)} %all-to-all-done.3.got_ref, bf16[256,256]{1,0:T(8,128)(2,1)S(1)} %copy-done.1, f32[256,128]{1,0:T(8,128)S(1)} %get-tuple-element.15.part_ref), custom_call_target="tpu_custom_call" | custom-call | flops 33554432 | bytes 1048576 | tf_op jit(solution)/shard_map/pallas_call | solution.py:441
  (1 shorter events, 0.0 us)
Async XLA Ops:
  0.6 16.6 %copy-start.5 = (bf16[32,64]{1,0:T(8,128)(2,1)S(1)}, bf16[32,64]{1,0:T(8,128)(2,1)}, u32[]{:S(2)}) copy-start(bf16[32,64]{1,0:T(8,128)(2,1)} %constant.8.clone.first_ref) | copy-start | bytes 12292
  0.6 16.6 %copy-start.6 = (bf16[256,256]{1,0:T(8,128)(2,1)S(1)}, bf16[256,256]{1,0:T(8,128)(2,1)}, u32[]{:S(2)}) copy-start(bf16[256,256]{1,0:T(8,128)(2,1)} %constant.9.clone.second_ref) | copy-start | bytes 393220
  1.9 25.8 %copy-start = (bf16[8,4,8,128,128]{4,3,2,1,0:T(8,128)(2,1)S(1)}, bf16[8,4,8,128,128]{4,3,2,1,0:T(8,128)(2,1)}, u32[]{:S(2)}) copy-start(bf16[8,4,8,128,128]{4,3,2,1,0:T(8,128)(2,1)} %param.13) | copy-start | bytes 25165828
  1.9 25.8 %copy-start.3 = (bf16[8,4,8,128]{3,2,1,0:T(8,128)(2,1)S(1)}, bf16[8,4,8,128]{3,2,1,0:T(8,128)(2,1)}, u32[]{:S(2)}) copy-start(bf16[8,4,8,128]{3,2,1,0:T(8,128)(2,1)} %param.10) | copy-start | bytes 196612
  17.2 21.7 %copy-start.2 = (bf16[256,256]{1,0:T(8,128)(2,1)S(1)}, bf16[256,256]{1,0:T(8,128)(2,1)}, u32[]{:S(2)}) copy-start(bf16[256,256]{1,0:T(8,128)(2,1)} %constant.10.clone.second_ref) | copy-start | bytes 393220
  17.2 25.5 %copy-start.4 = (bf16[128,128]{1,0:T(8,128)(2,1)S(1)}, bf16[128,128]{1,0:T(8,128)(2,1)}, u32[]{:S(2)}) copy-start(bf16[128,128]{1,0:T(8,128)(2,1)} %weight_ref.1) | copy-start | bytes 98308
  17.2 33.3 %copy-start.1 = (bf16[256,256]{1,0:T(8,128)(2,1)S(1)}, bf16[256,256]{1,0:T(8,128)(2,1)}, u32[]{:S(2)}) copy-start(bf16[256,256]{1,0:T(8,128)(2,1)} %constant.11.clone.z_ref) | copy-start | bytes 393220
  40.2 10.3 %all-to-all-start.3 = ((bf16[32,4,384]{2,1,0:T(4,128)(2,1)}), bf16[32,4,384]{2,1,0:T(4,128)(2,1)S(1)}, u32[]{:S(2)}, u32[]{:S(2)}) async-start(bf16[32,4,384]{2,1,0:T(4,128)(2,1)} %shard_map.124.after), calls=%async_computation.3 | async-start | bytes 196608 | tf_op jit(solution)/shard_map/all_to_all | solution.py:358

commit v8 on v7

--- a/solution.py
+++ b/solution.py
@@ -203,16 +203,14 @@
     modes_ref[...] = field_modes(s, x_ref[1, 0], x_ref[1, 1])
     groups = modes_ref.shape[0] // 8
     row = lax.broadcasted_iota(jnp.int32, (8, LANES), 0)
-    lane = lanes_of((LANES, LANES))
     on_vector = [group for group in range(groups) if group * 10 // groups != (group + 1) * 10 // groups]
-    kept = jnp.zeros((LANES, LANES), f32)
     for group in range(groups):
         start = group * 8
         if group in on_vector:
             for mode in range(8):
                 weights = w_ref[mode, group].astype(f32)
-                total = jnp.sum(weights * modes_ref[start + mode : start + mode + 1, :], 1, keepdims=True)
-                kept = jnp.where(lane == on_vector.index(group) * 8 + mode, total, kept)
+                product = weights * modes_ref[start + mode : start + mode + 1, :]
+                back[start + mode : start + mode + 1, :] = jnp.sum(product.T, 0, keepdims=True)
             continue
         every = lax.dot_general(
             modes_ref[start : start + 8, :].astype(bf16),
@@ -224,10 +222,6 @@
         for mode in range(8):
             total = jnp.where(row == mode, every[:, mode * LANES : (mode + 1) * LANES], total)
         back[start : start + 8, :] = total
-    kept = kept.T
-    for at, group in enumerate(on_vector):
-        back[group * 8 : group * 8 + 8, :] = kept[at * 8 : at * 8 + 8]
-
     rows = back[...].astype(bf16).astype(f32)
     rows = quarters(rows).reshape(s.devices, 8, LANES)
     pack_ref[:, :, :LANES] = rows[:, :4].astype(bf16)

time: 51.7 us -> 51.7 us (level)
  no operation moved by 1% of the time
where the time goes in v8:
time: 51.7 us; the launch traced here: 51.4 us
  blocking collectives  34.6 us (67%)
  Pallas kernels  9.72 us (19%)
  waiting for transfers between devices  3.74 us (7%)
  starting transfers between devices  2.56 us (5%)
  between operations  0.72 us (1%)
    all_to_all x3, blocking collectives, exchange(): return lax.all_to_all(pieces, ('gx', 'gy'), 0, 0)  34.6 us
    pallas_call x1, Pallas kernels, on_device_whole_planes(): call(functools.partial(outer_kernel, s), (in_hbm(*split_modes), in_vmem(c...  4.02 us
    all_to_all x1, waiting for transfers between devices, exchange(): return lax.all_to_all(pieces, ('gx', 'gy'), 0, 0)  3.74 us
    all_to_all x1, starting transfers between devices, exchange(): return lax.all_to_all(pieces, ('gx', 'gy'), 0, 0)  2.56 us
    pallas_call x1, Pallas kernels, on_device_whole_planes(): call(functools.partial(modes_kernel, s), (in_vmem(devices, 4, 3 * LANES),...  1.75 us
    pallas_call x1, Pallas kernels, on_device_whole_planes(): call(functools.partial(open_kernel, s), (in_vmem(2, 2, cells // 2, LANES)...  1.27 us
    pallas_call x1, Pallas kernels, on_device_whole_planes(): call(functools.partial(back_plane_kernel, s, t['back_scale'], 1.0 / math....  1.23 us
  transfers between devices with their start and end apart: 1, of which 1 were waited for; matrix products, arithmetic and copies ran while one was open for 0% of the time, Pallas kernels for 8%

profile of v8, /device:TPU:0, one launch (start us, length us, event | category | flops | bytes accessed | tf_op | source)
XLA Modules:
  0.0 51.4 jit_solution(3562517992189480503)
XLA Ops:
  0.6 0.0 copy-start.5
  0.6 0.0 copy-start.6
  0.7 1.3 %shard_map.121 = (bf16[2,2,128,128]{3,2,1,0:T(8,128)(2,1)S(1)}, bf16[256,128]{1,0:T(8,128)(2,1)S(1)}) custom-call(bf16[256,128]{1,0:T(8,128)(2,1)} %bitcast.17, bf16[256,128]{1,0:T(8,128)(2,1)} %bitcast.20, bf16[256,128]{1,0:T(8,128)(2,1)} %bitcast.21), custom_call_target="tpu_custom_call" | custom-call | flops 1099511627776 | bytes 1048576 | tf_op jit(solution)/shard_map/pallas_call | solution.py:366
  1.9 0.0 copy-start
  1.9 0.0 copy-start.3
  2.0 15.3 %all_to_all.20 = bf16[32,16,128]{2,1,0:T(8,128)(2,1)S(1)} all-to-all(bf16[32,16,128]{2,1,0:T(8,128)(2,1)S(1)} %bitcast.14), channel_id=1, replica_groups=mesh['gx'=4,'gy'=8] {'gx','gy'}, dimensions={0} | all-to-all | bytes 262144 | tf_op jit(solution)/shard_map/all_to_all | solution.py:352
  17.2 0.0 copy-done.5
  17.2 0.0 copy-done.6
  17.2 0.0 copy-start.4
  17.2 0.0 copy-start.1
  17.3 0.5 %shard_map.122 = bf16[512,128]{1,0:T(8,128)(2,1)S(1)} custom-call(bf16[512,128]{1,0:T(8,128)(2,1)S(1)} %bitcast.15, bf16[32,64]{1,0:T(8,128)(2,1)S(1)} %copy-done.5, bf16[256,256]{1,0:T(8,128)(2,1)S(1)} %copy-done.6), custom_call_target="tpu_custom_call" | custom-call | flops 2147483648 | bytes 1048576 | tf_op jit(solution)/shard_map/pallas_call | solution.py:377
  17.8 9.9 %all_to_all.21 = bf16[32,16,128]{2,1,0:T(8,128)(2,1)S(1)} all-to-all(bf16[32,16,128]{2,1,0:T(8,128)(2,1)S(1)} %bitcast.16), channel_id=1, replica_groups=mesh['gx'=4,'gy'=8] {'gx','gy'}, dimensions={0} | all-to-all | bytes 262144 | tf_op jit(solution)/shard_map/all_to_all | solution.py:352
  27.7 0.0 copy-done
  27.7 0.0 copy-done.3
  27.7 1.7 %shard_map.123 = (bf16[32,4,384]{2,1,0:T(4,128)(2,1)S(1)}, f32[256,128]{1,0:T(8,128)S(1)}) custom-call(bf16[2,2,128,128]{3,2,1,0:T(8,128)(2,1)S(1)} %bitcast.12, bf16[8,32,128,128]{3,2,1,0:T(8,128)(2,1)S(1)} %bitcast.11, bf16[256,128]{1,0:T(8,128)(2,1)S(1)} %bitcast.18, bf16[256,128]{1,0:T(8,128)(2,1)S(1)} %get-tuple-element.12.pre_ref), custom_call_target="tpu_custom_call" | custom-call | flops 67108864 | bytes 9437184 | tf_op jit(solution)/shard_map/pallas_call | solution.py:388
  29.4 9.5 %all_to_all.22.got_ref = bf16[32,4,384]{2,1,0:T(4,128)(2,1)S(1)} all-to-all(bf16[32,4,384]{2,1,0:T(4,128)(2,1)S(1)} %get-tuple-element.13), channel_id=1, replica_groups=mesh['gx'=4,'gy'=8] {'gx','gy'}, dimensions={0} | all-to-all | bytes 196608 | tf_op jit(solution)/shard_map/all_to_all | solution.py:352
  38.9 0.0 copy-done.2
  38.9 1.2 %shard_map.124.after = bf16[32,4,384]{2,1,0:T(4,128)(2,1)} custom-call(bf16[32,4,384]{2,1,0:T(4,128)(2,1)S(1)} %all_to_all.22.got_ref, bf16[32,64]{1,0:T(8,128)(2,1)S(1)} %copy-done.5, bf16[256,256]{1,0:T(8,128)(2,1)S(1)} %copy-done.2), custom_call_target="tpu_custom_call" | custom-call | flops 67108864 | bytes 1048576 | tf_op jit(solution)/shard_map/pallas_call | solution.py:407
  40.1 2.6 %all-to-all-start.3 = ((bf16[32,4,384]{2,1,0:T(4,128)(2,1)}), bf16[32,4,384]{2,1,0:T(4,128)(2,1)S(1)}, u32[]{:S(2)}, u32[]{:S(2)}) async-start(bf16[32,4,384]{2,1,0:T(4,128)(2,1)} %shard_map.124.after), calls=%async_computation.3 | async-start | bytes 196608 | tf_op jit(solution)/shard_map/all_to_all | solution.py:352
  42.7 0.0 copy-done.4
  42.7 4.0 %shard_map.125 = (bf16[8,32,128,128]{3,2,1,0:T(8,128)(2,1)}, f32[256,128]{1,0:T(8,128)S(1)}) custom-call(bf16[2,2,128,128]{3,2,1,0:T(8,128)(2,1)S(1)} %bitcast.13, f32[256,128]{1,0:T(8,128)S(1)} %get-tuple-element.14.grad_ref, bf16[256,128]{1,0:T(8,128)(2,1)S(1)} %get-tuple-element.12.pre_ref, bf16[128,128]{1,0:T(8,128)(2,1)S(1)} %copy-done.4, ...), custom_call_target="tpu_custom_call" | custom-call | flops 8388608 | bytes 9437184 | tf_op jit(solution)/shard_map/pallas_call | solution.py:420
  46.7 3.7 %all-to-all-done.3.got_ref = bf16[32,4,384]{2,1,0:T(4,128)(2,1)S(1)} async-done(((bf16[32,4,384]{2,1,0:T(4,128)(2,1)}), bf16[32,4,384]{2,1,0:T(4,128)(2,1)S(1)}, u32[]{:S(2)}, u32[]{:S(2)}) %all-to-all-start.3) | async-done | bytes 98336 | tf_op jit(solution)/shard_map/all_to_all | solution.py:352
  50.5 0.0 copy-done.1
  50.5 0.9 %shard_map.126 = (bf16[256,128]{1,0:T(8,128)(2,1)}, f32[32,4,128]{2,1,0:T(4,128)}) custom-call(bf16[32,4,384]{2,1,0:T(4,128)(2,1)S(1)} %all-to-all-done.3.got_ref, bf16[256,256]{1,0:T(8,128)(2,1)S(1)} %copy-done.1, f32[256,128]{1,0:T(8,128)S(1)} %get-tuple-element.15.part_ref), custom_call_target="tpu_custom_call" | custom-call | flops 33554432 | bytes 1048576 | tf_op jit(solution)/shard_map/pallas_call | solution.py:435
  (1 shorter events, 0.0 us)
Async XLA Ops:
  0.6 16.6 %copy-start.5 = (bf16[32,64]{1,0:T(8,128)(2,1)S(1)}, bf16[32,64]{1,0:T(8,128)(2,1)}, u32[]{:S(2)}) copy-start(bf16[32,64]{1,0:T(8,128)(2,1)} %constant.8.clone.first_ref) | copy-start | bytes 12292
  0.6 16.6 %copy-start.6 = (bf16[256,256]{1,0:T(8,128)(2,1)S(1)}, bf16[256,256]{1,0:T(8,128)(2,1)}, u32[]{:S(2)}) copy-start(bf16[256,256]{1,0:T(8,128)(2,1)} %constant.9.clone.second_ref) | copy-start | bytes 393220
  1.9 25.8 %copy-start = (bf16[8,4,8,128,128]{4,3,2,1,0:T(8,128)(2,1)S(1)}, bf16[8,4,8,128,128]{4,3,2,1,0:T(8,128)(2,1)}, u32[]{:S(2)}) copy-start(bf16[8,4,8,128,128]{4,3,2,1,0:T(8,128)(2,1)} %param.13) | copy-start | bytes 25165828
  1.9 25.8 %copy-start.3 = (bf16[8,4,8,128]{3,2,1,0:T(8,128)(2,1)S(1)}, bf16[8,4,8,128]{3,2,1,0:T(8,128)(2,1)}, u32[]{:S(2)}) copy-start(bf16[8,4,8,128]{3,2,1,0:T(8,128)(2,1)} %param.10) | copy-start | bytes 196612
  17.2 21.7 %copy-start.2 = (bf16[256,256]{1,0:T(8,128)(2,1)S(1)}, bf16[256,256]{1,0:T(8,128)(2,1)}, u32[]{:S(2)}) copy-start(bf16[256,256]{1,0:T(8,128)(2,1)} %constant.10.clone.second_ref) | copy-start | bytes 393220
  17.2 25.5 %copy-start.4 = (bf16[128,128]{1,0:T(8,128)(2,1)S(1)}, bf16[128,128]{1,0:T(8,128)(2,1)}, u32[]{:S(2)}) copy-start(bf16[128,128]{1,0:T(8,128)(2,1)} %weight_ref.1) | copy-start | bytes 98308
  17.2 33.2 %copy-start.1 = (bf16[256,256]{1,0:T(8,128)(2,1)S(1)}, bf16[256,256]{1,0:T(8,128)(2,1)}, u32[]{:S(2)}) copy-start(bf16[256,256]{1,0:T(8,128)(2,1)} %constant.11.clone.z_ref) | copy-start | bytes 393220
  40.1 10.3 %all-to-all-start.3 = ((bf16[32,4,384]{2,1,0:T(4,128)(2,1)}), bf16[32,4,384]{2,1,0:T(4,128)(2,1)S(1)}, u32[]{:S(2)}, u32[]{:S(2)}) async-start(bf16[32,4,384]{2,1,0:T(4,128)(2,1)} %shard_map.124.after), calls=%async_computation.3 | async-start | bytes 196608 | tf_op jit(solution)/shard_map/all_to_all | solution.py:352
